TPU v7x, 128 devices: a whole 4x4x4 slice. The times are simulated.
128 devices in a mesh: gx: 8 (over z, x_lo), gy: 4 (over x_hi, core), gz: 4 (over y).
Axes of the slice: x: 4 (x_hi: 2, x_lo: 2; x = x_hi * 2 + x_lo), y: 4, z: 4, core: 2. Of those that a mesh axis runs over, the one named last changes fastest.
Arguments:
- volume: bfloat16 [64, 128, 512], P('gx', 'gy', 'gz'), may hold values from -60 to 60
- conv_one: bfloat16 [3, 3, 3, 1, 16], replicated, may hold values from -1.25 to 1.25
- gain_one: float32 [16], replicated, may hold values from 0.1 to 1.9
- shift_one: float32 [16], replicated, may hold values from -3 to 3
- second_level_kernel: bfloat16 [3, 3, 3, 16, 32], replicated, may hold values from -0.3125 to 0.3125
- second_level_gain: float32 [32], replicated, may hold values from 0.1 to 1.9
- second_level_bias: float32 [32], replicated, may hold values from -3 to 3
- third_level_kernel: bfloat16 [3, 3, 3, 32, 64], replicated, may hold values from -0.21875 to 0.21875
- third_level_gain: float32 [64], replicated, may hold values from 0.1 to 1.9
- third_level_bias: float32 [64], replicated, may hold values from -3 to 3
- bottleneck_kernel: bfloat16 [3, 3, 3, 64, 128], replicated, may hold values from -0.15625 to 0.15625
- bottleneck_norm_gain: float32 [128], replicated, may hold values from 0.1 to 1.9
- bottleneck_norm_bias: float32 [128], replicated, may hold values from -3 to 3
Outputs:
- first_level_features: bfloat16 [64, 128, 8192], P('gx', 'gy', 'gz')
- second_level_features: bfloat16 [32, 64, 8192], P('gx', 'gy', 'gz')
- third_level_features: bfloat16 [16, 32, 8192], P('gx', 'gy', 'gz')
- bottleneck: bfloat16 [8, 16, 8192], replicated
All inputs are finite; a program needn't handle non-finite values.
Results may differ from a plain program's by a relative error of at most 0.012.
The roundings to bfloat16 on the way count: a program that leaves them out, or rounds other values in their place, can miss the bound.
Values may be sent and summed in bfloat16 or wider, within the bound.
No kernel may reach another device: no remote copies, remote signals or barrier semaphores. Data moves between devices by JAX's collectives and lax.ppermute only.
A program may use at most 128 MiB of HBM per device.

v0:
```python
import jax
import jax.numpy as jnp
from jax import lax
from jax.sharding import PartitionSpec as P

EPSILON = 1e-05


def padded_2(block, sides, width):
    for axis, dim in sides:
        count = lax.axis_size(axis)
        forward = [(i, i + 1) for i in range(count - 1)]
        backward = [(target, source) for source, target in forward]
        low = lax.ppermute(
            lax.slice_in_dim(block, block.shape[dim] - width, None, axis=dim), axis, forward
        )
        high = lax.ppermute(lax.slice_in_dim(block, 0, width, axis=dim), axis, backward)
        block = jnp.concatenate([low, block, high], axis=dim)
    return block


def shifted(value, axis, steps):
    count = lax.axis_size(axis)
    first, last = (max(0, -steps), min(count, count - steps))
    return lax.ppermute(value, axis, [(source, source + steps) for source in range(first, last)])


def conv_valid(padded, weight):
    chans_in = weight.shape[3]
    chans_out = weight.shape[4]
    px, py, merged = padded.shape
    pz = merged // chans_in
    shaped = padded.reshape(1, px, py, pz, chans_in)
    result = lax.conv_general_dilated(
        shaped,
        weight,
        (1, 1, 1),
        "VALID",
        dimension_numbers=("NDHWC", "DHWIO", "NDHWC"),
        preferred_element_type=jnp.float32,
    )
    return result.reshape(px - 2, py - 2, (pz - 2) * chans_out)


def settle(response, totals, cells_total, scale_gain, shift_vec):
    channel_list = scale_gain.shape[0]
    mean_vec = totals[0] / cells_total
    variance = totals[1] / cells_total - mean_vec * mean_vec
    factor = scale_gain * lax.rsqrt(variance + EPSILON)
    flat = response.reshape(-1, channel_list)
    normed = (flat - mean_vec[None, :]) * factor[None, :] + shift_vec[None, :]
    return jax.nn.relu(normed).astype(jnp.bfloat16).reshape(response.shape)


def halve_resolution(input_volume, channel_list):
    sx, sy, merged = input_volume.shape
    sz = merged // channel_list
    pooled = jnp.max(
        input_volume.reshape(sx // 2, 2, sy // 2, 2, sz // 2, 2, channel_list), axis=(1, 3, 5)
    )
    return pooled.reshape(sx // 2, sy // 2, sz // 2 * channel_list)


def moments_of(response, channel_list):
    flat = response.reshape(-1, channel_list)
    return (jnp.sum(flat, axis=0), jnp.sum(flat * flat, axis=0))


def distribute_level(input_volume, weight, scale_gain, shift_vec):
    chans_in = weight.shape[3]
    chans_out = weight.shape[4]
    padded = padded_2(input_volume, (("gx", 0), ("gy", 1)), 1)
    lower = shifted(padded[:, :, -chans_in:], "gz", 1)
    upper = shifted(padded[:, :, :chans_in], "gz", -1)
    padded = jnp.concatenate([lower, padded, upper], axis=2)
    response = conv_valid(padded, weight)
    totals = lax.psum(moments_of(response, chans_out), ("gx", "gy", "gz"))
    devices_all = lax.axis_size("gx") * lax.axis_size("gy") * lax.axis_size("gz")
    cells_total = float(
        response.shape[0] * response.shape[1] * (response.shape[2] // chans_out) * devices_all
    )
    return settle(response, totals, cells_total, scale_gain, shift_vec)


def assemble(stacked, channel_list):
    size_x, size_y, size_z = (lax.axis_size("gx"), lax.axis_size("gy"), lax.axis_size("gz"))
    bx, by, merged = stacked.shape[1:]
    bz = merged // channel_list
    blocks = stacked.reshape(size_x, size_y, size_z, bx, by, bz, channel_list)
    blocks = jnp.transpose(blocks, (0, 3, 1, 4, 2, 5, 6))
    return blocks.reshape(size_x * bx, size_y * by, size_z * bz * channel_list)


def shards(
    volume,
    conv_one,
    gain_one,
    shift_one,
    second_level_kernel,
    second_level_gain,
    second_level_bias,
    third_level_kernel,
    third_level_gain,
    third_level_bias,
    bottleneck_kernel,
    bottleneck_norm_gain,
    bottleneck_norm_bias,
):
    channel_count_first = conv_one.shape[4]
    channel_count_second = second_level_kernel.shape[4]
    channel_count_third = third_level_kernel.shape[4]
    chan_four = bottleneck_kernel.shape[4]
    first_level_features = distribute_level(volume, conv_one, gain_one, shift_one)
    second_level_features = distribute_level(
        halve_resolution(first_level_features, channel_count_first),
        second_level_kernel,
        second_level_gain,
        second_level_bias,
    )
    second_level_pooled = halve_resolution(second_level_features, channel_count_second)
    third_level_features = distribute_level(
        second_level_pooled, third_level_kernel, third_level_gain, third_level_bias
    )
    third_level_pooled = halve_resolution(third_level_features, channel_count_third)
    stacked = lax.all_gather(third_level_pooled[None], ("gx", "gy", "gz"), axis=0, tiled=True)
    coarse = assemble(stacked, channel_count_third)
    padded = jnp.pad(coarse, ((1, 1), (1, 1), (channel_count_third, channel_count_third)))
    response = conv_valid(padded, bottleneck_kernel)
    cells_total = float(response.shape[0] * response.shape[1] * (response.shape[2] // chan_four))
    bottleneck = settle(
        response,
        moments_of(response, chan_four),
        cells_total,
        bottleneck_norm_gain,
        bottleneck_norm_bias,
    )
    return (first_level_features, second_level_features, third_level_features, bottleneck)


def solution(mesh):
    return jax.shard_map(
        shards,
        mesh=mesh,
        in_specs=(P("gx", "gy", "gz"), P(), P(), P(), P(), P(), P(), P(), P(), P(), P(), P(), P()),
        out_specs=(P("gx", "gy", "gz"), P("gx", "gy", "gz"), P("gx", "gy", "gz"), P()),
        check_vma=False,
    )
```

profile of v0, /device:TPU:1, one launch (start us, length us, event | category | flops | bytes accessed | tf_op | source)
XLA Modules:
  0.0 903.0 jit_solution(9025755109775774198)
XLA Ops:
  8.0 3.9 collective-permute-start
  11.9 1.3 collective-permute-start.1
  13.3 0.9 constant_dynamic-update-slice_fusion.1
  14.1 2.4 collective-permute-done.1
  16.5 3.9 collective-permute-start.3
  20.4 4.4 collective-permute-start.2
  25.7 1.3 collective-permute-start.5
  27.0 4.0 collective-permute-start.4
  31.1 1.5 collective-permute-done.4
  33.6 5.7 copy.215
  39.3 30.9 %select_reduce_fusion.1 = (f32[16]{0:T(128)S(1)}, f32[16]{0:T(128)S(1)}, f32[8,32,8,17,16]{4,2,3,1,0:T(8,128)}) fusion(pred[8,17]{0,1:T(8,128)(4,1)S(1)} %copy-done.12, bf16[10,34,8,19,1]{2,4,3,1,0:T(2,128)(2,1)} %copy.215, bf16[3,3,3,1,16]{4,2,3,1,0:T(4,128)(2,1)S(1)} %copy-done.11), kind=kOutput, calls=%fused_computation.1 | convolution fusion | flops 33423328 | bytes 2332712 | tf_op jit(solution)/shard_map/conv_general_dilated | solution.py:34
  70.2 15.0 %copy.217 = f32[8,32,8,17,16]{1,4,3,2,0:T(8,128)} copy(f32[8,32,8,17,16]{4,2,3,1,0:T(8,128)} %get-tuple-element.76) | data formatting | bytes 4456448 | tf_op jit(solution)/shard_map/conv_general_dilated | solution.py:34
  85.2 7.1 slice.102
  92.3 16.0 %copy.218 = f32[8,32,1,128,16]{4,3,1,0,2:T(8,128)} copy(f32[8,32,1,128,16]{1,4,3,0,2:T(8,128)} %slice.102) | data formatting | bytes 4194304 | tf_op jit(solution)/shard_map/conv_general_dilated | solution.py:34
  108.3 22.3 %copy.219 = f32[4,2,16,2,64,2,16]{4,6,5,3,2,1,0:T(8,128)} copy(f32[4,2,16,2,64,2,16]{6,5,4,3,2,1,0:T(2,128)} %bitcast.84) | data formatting | bytes 4194304 | tf_op jit(solution)/shard_map/reshape;reshape | solution.py:50
  130.6 81.8 %all-reduce.3 = (f32[16]{0:T(128)S(1)}, f32[16]{0:T(128)S(1)}) all-reduce(f32[16]{0:T(128)S(1)} %get-tuple-element.37, f32[16]{0:T(128)S(1)} %get-tuple-element.36), channel_id=1, replica_groups=mesh['gx'=8,'gy'=4,'gz'=4] {'gx','gy','gz'}, use_global_device_ids=true, to_apply=%region_3.0 | all-reduce | flops 32 | bytes 256 | tf_op jit(solution)/shard_map/psum | solution.py:77
  212.4 3.1 fusion.16
  216.0 1.9 collective-permute-start.6
  218.5 1.8 reshape.124
  220.7 1.3 collective-permute-start.7
  222.1 3.9 collective-permute-done.7
  226.0 3.9 collective-permute-start.9
  230.0 3.7 collective-permute-start.8
  233.6 0.9 collective-permute-done.8
  234.8 2.4 collective-permute-start.10
  237.2 1.3 collective-permute-start.11
  238.5 3.4 collective-permute-done.11
  242.2 1.6 copy.253
  243.8 1.8 pad.7.clone
  245.6 3.8 copy.225
  249.5 1.1 slice.109
  250.6 5.2 select_reduce_fusion.5
  256.5 65.8 %all-reduce.2 = (f32[32]{0:T(128)S(1)}, f32[32]{0:T(128)S(1)}) all-reduce(f32[32]{0:T(128)S(1)} %get-tuple-element.41, f32[32]{0:T(128)S(1)} %get-tuple-element.40), channel_id=1, replica_groups=mesh['gx'=8,'gy'=4,'gz'=4] {'gx','gy','gz'}, use_global_device_ids=true, to_apply=%region_8.9 | all-reduce | flops 64 | bytes 512 | tf_op jit(solution)/shard_map/psum | solution.py:77
  322.3 2.4 fusion.25
  324.9 2.5 collective-permute-start.12
  327.8 1.3 collective-permute-start.13
  329.1 3.3 collective-permute-done.13
  332.5 4.0 collective-permute-start.15
  336.5 4.2 collective-permute-start.14
  340.7 0.8 collective-permute-done.14
  341.7 1.9 collective-permute-start.16
  343.7 1.3 collective-permute-start.17
  345.0 3.2 collective-permute-done.17
  349.1 1.3 select_reduce_fusion.7
  350.4 66.2 %all-reduce.1 = (f32[64]{0:T(128)S(1)}, f32[64]{0:T(128)S(1)}) all-reduce(f32[64]{0:T(128)S(1)} %get-tuple-element.43, f32[64]{0:T(128)S(1)} %get-tuple-element.42), channel_id=1, replica_groups=mesh['gx'=8,'gy'=4,'gz'=4] {'gx','gy','gz'}, use_global_device_ids=true, to_apply=%region_13.14 | all-reduce | flops 128 | bytes 1024 | tf_op jit(solution)/shard_map/psum | solution.py:77
  418.0 5.7 maximum_convert_fusion
  423.7 4.6 copy.246
  428.3 2.0 copy.227
  430.2 2.5 reshape_reshape.25
  432.9 0.8 maximum_convert_fusion.4
  434.8 273.3 %all-gather.2.cloned.1.call-done = bf16[128,1,4,1024]{3,2,1,0:T(4,128)(2,1)} async-done(((bf16[1,1,4,1024]{3,2,1,0:T(4,128)(2,1)}), bf16[128,1,4,1024]{3,2,1,0:T(4,128)(2,1)}) %all-gather.2.cloned.1.call-update) | async-done | bytes 1048592 | tf_op jit(solution)/shard_map/all_gather | solution.py:125
  708.1 2.5 copy.239
  710.6 2.9 reshape.128
  713.6 1.9 copy.240
  715.5 3.3 reshape.129
  718.8 0.9 pad.4
  719.7 4.1 reshape.191
  723.8 2.5 copy.252
  726.3 1.0 pad.11.clone
  728.0 154.2 %select_reduce_fusion.3 = (f32[128]{0:T(128)S(1)}, f32[128]{0:T(128)S(1)}, f32[8,16,8,9,128]{4,2,3,1,0:T(8,128)S(1)}) fusion(pred[8,9]{0,1:T(8,128)(4,1)S(1)} %copy-done.13, bf16[3,3,3,64,128]{4,3,2,1,0:T(8,128)(2,1)S(1)} %copy-done, bf16[10,18,1,7,2,64]{5,3,4,1,0,2:T(8,128)(2,1)S(1)} %slice.120, bf16[10,18,1,8,9,64]{5,3,4,1,0,2:T(8,128)(2,1)S(1)} %copy.243), kind=kOutput, calls=%fused_computation.9 | convolution fusion | flops 4090023936 | bytes 7143496 | tf_op jit(solution)/shard_map/conv_general_dilated | solution.py:34
  882.2 0.8 copy.244
  883.3 3.2 copy.245
  886.5 5.0 reshape_reshape.28
  891.5 4.2 maximum_convert_fusion.1
  (126 shorter events, 10.5 us)
Async XLA Ops:
  7.2 720.8 %copy-start = (bf16[3,3,3,64,128]{4,3,2,1,0:T(8,128)(2,1)S(1)}, bf16[3,3,3,64,128]{4,3,2,1,0:T(8,128)(2,1)}, u32[]{:S(2)}) copy-start(bf16[3,3,3,64,128]{4,3,2,1,0:T(8,128)(2,1)} %param.23) | copy-start | bytes 1327108
  7.2 32.2 %copy-start.12 = (pred[8,17]{0,1:T(8,128)(4,1)S(1)}, pred[8,17]{0,1:T(8,128)(4,1)}, u32[]{:S(2)}) copy-start(pred[8,17]{0,1:T(8,128)(4,1)} %constant.62) | copy-start | bytes 412
  7.2 32.1 %copy-start.11 = (bf16[3,3,3,1,16]{4,2,3,1,0:T(4,128)(2,1)S(1)}, bf16[3,3,3,1,16]{4,2,3,1,0:T(4,128)(2,1)}, u32[]{:S(2)}) copy-start(bf16[3,3,3,1,16]{4,2,3,1,0:T(4,128)(2,1)} %param.14) | copy-start | bytes 2596
  7.2 700.9 %all-gather.2.cloned.1.call-start = ((), (), s32[]{:S(2)}) async-start(), calls=%async_computation | async-start | bytes 1056768 | tf_op jit(solution)/shard_map/all_gather | solution.py:125
  8.0 5.2 collective-permute-start
  11.9 4.6 collective-permute-start.1
  16.5 8.3 collective-permute-start.3
  20.4 5.2 collective-permute-start.2
  25.7 5.4 collective-permute-start.5
  27.0 5.7 collective-permute-start.4
  108.3 104.1 %copy-start.5 = (f32[16]{0:T(128)S(1)}, f32[16]{0:T(128)}, u32[]{:S(2)}) copy-start(f32[16]{0:T(128)} %param.15) | copy-start | bytes 196
  108.3 104.1 %copy-start.3 = (f32[16]{0:T(128)S(1)}, f32[16]{0:T(128)}, u32[]{:S(2)}) copy-start(f32[16]{0:T(128)} %param.16) | copy-start | bytes 196
  216.0 6.0 collective-permute-start.6
  220.7 5.2 collective-permute-start.7
  226.0 7.6 collective-permute-start.9
  230.0 4.6 collective-permute-start.8
  234.8 3.7 collective-permute-start.10
  237.2 4.7 collective-permute-start.11
  243.8 6.8 copy-start.10
  243.8 6.8 copy-start.13
  255.8 66.4 %copy-start.6 = (f32[32]{0:T(128)S(1)}, f32[32]{0:T(128)}, u32[]{:S(2)}) copy-start(f32[32]{0:T(128)} %param.18) | copy-start | bytes 388
  255.9 66.4 %copy-start.1 = (f32[32]{0:T(128)S(1)}, f32[32]{0:T(128)}, u32[]{:S(2)}) copy-start(f32[32]{0:T(128)} %param.19) | copy-start | bytes 388
  256.4 92.6 %copy-start.9 = (bf16[3,3,3,32,64]{4,3,2,1,0:T(8,128)(2,1)S(1)}, bf16[3,3,3,32,64]{4,3,2,1,0:T(8,128)(2,1)}, u32[]{:S(2)}) copy-start(bf16[3,3,3,32,64]{4,3,2,1,0:T(8,128)(2,1)} %param.20) | copy-start | bytes 331780
  256.5 92.6 %copy-start.14 = (pred[8,5]{0,1:T(8,128)(4,1)S(1)}, pred[8,5]{0,1:T(8,128)(4,1)}, u32[]{:S(2)}) copy-start(pred[8,5]{0,1:T(8,128)(4,1)} %constant.68) | copy-start | bytes 124
  324.9 4.2 collective-permute-start.12
  327.8 4.7 collective-permute-start.13
  332.5 84.1 %copy-start.7 = (f32[64]{0:T(128)S(1)}, f32[64]{0:T(128)}, u32[]{:S(2)}) copy-start(f32[64]{0:T(128)} %param.21) | copy-start | bytes 772
  332.5 84.1 %copy-start.2 = (f32[64]{0:T(128)S(1)}, f32[64]{0:T(128)}, u32[]{:S(2)}) copy-start(f32[64]{0:T(128)} %param.22) | copy-start | bytes 772
  332.5 8.2 collective-permute-start.15
  336.5 5.0 collective-permute-start.14
  341.7 3.3 collective-permute-start.16
  343.7 4.5 collective-permute-start.17
  348.6 69.2 %copy-start.4 = (f32[128]{0:T(128)S(1)}, f32[128]{0:T(128)}, u32[]{:S(2)}) copy-start(f32[128]{0:T(128)} %param.25) | copy-start | bytes 1540
  886.5 5.0 copy-start.8
Sparse Core Ops, SparseCore 0:
  417.7 290.3 all-gather.1
where the time goes:
time: 913 us; the launch traced here: 903 us
  waiting for transfers between devices  294 us (32%)
  blocking collectives  214 us (23%)
  matrix products  192 us (21%)
  local copies, waits for them, and re-layouts  122 us (13%)
  starting transfers between devices  48.6 us (5%)
  other arithmetic  17.8 us (2%)
  between operations  15.2 us (2%)
    all_gather x1, waiting for transfers between devices, shards(): lax.all_gather(third_level_pooled[None], ('gx', 'gy', 'gz'), axis=0, tile...  273 us
    psum x3, blocking collectives, distribute_level(): totals = lax.psum(moments_of(response, chans_out), ('gx', 'gy', 'gz'))  214 us
    conv_general_dilated x4, matrix products, conv_valid(): lax.conv_general_dilated(shaped, weight, (1, 1, 1), 'VALID', dimension_nu...  192 us
    conv_general_dilated x21, local copies, waits for them, and re-layouts, conv_valid(): lax.conv_general_dilated(shaped, weight, (1, 1, 1), 'VALID', dimension_nu...  56.7 us
    another operation x4, local copies, waits for them, and re-layouts, settle(): flat = response.reshape(-1, channel_list)  29.9 us
    ppermute x6, starting transfers between devices, padded_2(): lax.ppermute(lax.slice_in_dim(block, block.shape[dim] - width, None, axis...  20.7 us
  transfers between devices with their start and end apart: 19, of which 11 were waited for; matrix products, arithmetic and copies ran while one was open for 2% of the time, Pallas kernels for 0%

commit v1 on v0

v1 whole, which is shorter than its diff:
```python
import jax
import jax.numpy as jnp
from jax import lax
from jax.experimental import pallas as pl
from jax.experimental.pallas import tpu as pltpu
from jax.sharding import PartitionSpec as P

EPSILON = 1e-05
F32 = jnp.float32
BF16 = jnp.bfloat16
AXES = ("gx", "gy", "gz")
DEVICES = 128
VOXELS_1 = 64.0 * 128.0 * 512.0
PARAMS = pltpu.CompilerParams(vmem_limit_bytes=56 * 1024 * 1024)


def full(shape, dtype):
    return jax.ShapeDtypeStruct(shape, dtype)


def iota(shape, dim):
    return lax.broadcasted_iota(jnp.int32, shape, dim)


def band_kernel(k1_ref, k2_ref, k3_ref, k4_ref, w1_ref, w2_ref, w3_ref, w4_ref, t2_ref, t3_ref):
    spread = (iota((16, 768), 1) % 16 == iota((16, 768), 0)).astype(BF16)
    taps = jnp.dot(k1_ref[...], spread, preferred_element_type=F32)
    lag = iota((64, 768), 0) - iota((64, 768), 1) // 16
    for dx in range(3):
        for dy in range(3):
            block = jnp.zeros((64, 768), F32)
            for dz in range(3):
                t = (dx * 3 + dy) * 3 + dz
                block = jnp.where(lag == dz, taps[t : t + 1, :], block)
            w1_ref[dx * 256 + dy * 64 : dx * 256 + dy * 64 + 64, :] = block.astype(BF16)
        w1_ref[dx * 256 + 192 : dx * 256 + 256, :] = jnp.zeros((64, 768), BF16)

    def banded(k_ref, w_ref, t_ref, cin, cout, first):
        outs = 256 // cout
        if outs > 1:
            tile = (iota((cout, 256), 1) % cout == iota((cout, 256), 0)).astype(BF16)
            t_ref[...] = jnp.dot(k_ref[...], tile, preferred_element_type=F32)
        zo = iota((cin, 256), 1) // cout

        def plane(p, carry):
            for zi in range(-first, 256 // cin - first):
                block = jnp.zeros((cin, 256), F32)
                if 0 <= zi < outs + 2:
                    for dz in range(3):
                        start = pl.multiple_of((p * 3 + dz) * cin, cin)
                        block = jnp.where(zo == zi - dz, t_ref[pl.ds(start, cin), :], block)
                start = pl.multiple_of(p * 256 + (zi + first) * cin, cin)
                w_ref[pl.ds(start, cin), :] = block.astype(BF16)
            return carry

        lax.fori_loop(0, 9, plane, 0)

    banded(k2_ref, w2_ref, t2_ref, 16, 32, 1)
    banded(k3_ref, w3_ref, t3_ref.at[0:864], 32, 64, 0)
    banded(k4_ref, w4_ref, t3_ref, 64, 128, 0)


def bands(k1, k2, k3, k4):
    return pl.pallas_call(
        band_kernel,
        out_shape=(
            full((768, 768), BF16),
            full((2304, 256), BF16),
            full((2304, 256), BF16),
            full((2304, 256), BF16),
        ),
        scratch_shapes=[pltpu.VMEM((432, 256), F32), pltpu.VMEM((1728, 256), F32)],
        compiler_params=PARAMS,
    )(k1, k2, k3, k4)


def fold(row, width):
    total = row[:, 0:128]
    for j in range(1, row.shape[1] // 128):
        total = total + row[:, j * 128 : (j + 1) * 128]
    step = 64
    while step >= width:
        total = total + pltpu.roll(total, step, 1)
        step //= 2
    return total


def pack_stats(s1, s2, width):
    return jnp.where(iota((1, 128), 1) < 64, fold(s1, width), fold(s2, width))


def unpack_stats(total, cells):
    low = iota((1, 128), 1) < 64
    other = pltpu.roll(total, 64, 1)
    mean = jnp.where(low, total, other) / cells
    variance = jnp.where(low, other, total) / cells - mean * mean
    return mean, variance


def paired_rows(ref, j, count):
    return jnp.concatenate(
        [
            jnp.maximum(ref[k, pl.ds(0, count, stride=2), :], ref[k, pl.ds(1, count, stride=2), :])
            for k in (j, j + 1)
        ],
        axis=1,
    )


def first_kernel(lo_ref, mid_ref, hi_ref, w1_ref, lhs_ref, stats_ref):
    lane = iota((48, 128), 1)

    def windows(piece_ref, base, first, count):
        def step(i, carry):
            v = piece_ref[first + i].astype(F32)
            for q in range(3):
                start = 119 + 48 * q
                a, b = start // 128, (start + 49) // 128 + 1
                src = v[:, a * 128 : b * 128]
                width = (b - a) * 128
                wa = pltpu.roll(src, width - (start - a * 128), 1)[:, 0:128]
                wb = pltpu.roll(wa, 64, 1)
                left = jnp.where(lane < 64, pltpu.roll(wa, 1, 0), wb)
                right = pltpu.roll(wa, 47, 0)
                lhs_ref[q, base + i, :, 0:128] = left.astype(BF16)
                lhs_ref[q, base + i, :, 128:256] = right.astype(BF16)
            return carry

        lax.fori_loop(0, count, step, 0)

    windows(lo_ref, 0, 1, 7)
    windows(mid_ref, 7, 0, 8)
    windows(hi_ref, 15, 0, 7)
    s1 = jnp.zeros((1, 768), F32)
    s2 = jnp.zeros((1, 768), F32)
    for q in range(3):
        lhs = jnp.concatenate([lhs_ref[q, 6 + dx : 14 + dx, :, :] for dx in range(3)], axis=2)
        lhs = lhs.reshape(8 * 48, 768)
        r = jnp.dot(lhs, w1_ref[...], preferred_element_type=F32)
        own = r.reshape(8, 48, 768)[:, 8:40, :].reshape(256, 768)
        row1 = jnp.sum(own, axis=0, keepdims=True)
        row2 = jnp.sum(own * own, axis=0, keepdims=True)
        at = iota((1, 768), 1)
        if q == 0:
            row1, row2 = (jnp.where(at >= 128, r_, 0.0) for r_ in (row1, row2))
        if q == 2:
            row1, row2 = (jnp.where(at < 640, r_, 0.0) for r_ in (row1, row2))
        s1, s2 = s1 + row1, s2 + row2
    stats_ref[...] = jnp.broadcast_to(pack_stats(s1, s2, 16).reshape(1, 1, 128), (DEVICES, 1, 128))


def first_part(lo, mid, hi, w1):
    return pl.pallas_call(
        first_kernel,
        out_shape=(full((3, 22, 48, 256), BF16), full((DEVICES, 1, 128), F32)),
        compiler_params=PARAMS,
    )(lo, mid, hi, w1)


def second_kernel(
    at_ref, lhs_ref, stats_ref, gain_ref, shift_ref, w1_ref, w2_ref, f1_ref, r2_ref, out_stats_ref, half, p1, pd
):
    mean, variance = unpack_stats(jnp.sum(stats_ref[...], axis=0), VOXELS_1)
    factor = gain_ref[...] * lax.rsqrt(variance + EPSILON)
    shift = shift_ref[...]
    mean, factor, shift = (jnp.concatenate([v] * 6, axis=1) for v in (mean, factor, shift))
    row, col = iota((256, 256), 0), iota((256, 256), 1)
    pick = (row == (col % 128) // 16 * 32 + col % 16 + col // 128 * 16).astype(BF16)
    bx, by, bz = at_ref[0], at_ref[1], at_ref[2]
    p1[:, :, 1152:1280] = jnp.zeros((10, 24, 128), F32)
    for q in range(3):
        lhs = jnp.concatenate([lhs_ref[q, dx : 20 + dx, :, :] for dx in range(3)], axis=2)
        r = jnp.dot(lhs.reshape(960, 768), w1_ref[...], preferred_element_type=F32)
        f = jnp.maximum((r - mean) * factor + shift, 0.0)
        f = f.reshape(20, 48, 768)
        a, b = (128 if q == 0 else 0), (640 if q == 2 else 768)
        f1_ref[:, :, q * 768 - 128 + a : q * 768 - 128 + b] = f[6:14, 8:40, a:b].astype(BF16)
        pairs = jnp.max(f.reshape(10, 2, 48, 768), axis=1).reshape(480, 768)
        for j in range(6):
            half[j] = pairs[:, j * 128 : (j + 1) * 128]
        for j in range(3):
            g = paired_rows(half, 2 * j, 240)
            both = jnp.dot(g.astype(BF16), pick, preferred_element_type=F32)
            pooled = jnp.maximum(both[:, 0:128], both[:, 128:256])
            at = q * 384 + j * 128
            p1[:, :, at : at + 128] = pooled.reshape(10, 24, 128)
    gy = iota((24, 1280), 0) - 4 + by * 16
    gz = iota((24, 1280), 1) // 16 - 4 + bz * 64
    inside = (gy >= 0) & (gy < 64) & (gz >= 0) & (gz < 256)

    def mask(i, carry):
        gx = i - 3 + bx * 4
        v = jnp.where(inside & (gx >= 0) & (gx < 32), p1[i], 0.0)
        pd[0, i] = pltpu.roll(v, 1, 0).astype(BF16)
        pd[1, i] = v.astype(BF16)
        pd[2, i] = pltpu.roll(v, 23, 0).astype(BF16)
        return carry

    lax.fori_loop(0, 10, mask, 0)
    s1 = jnp.zeros((1, 256), F32)
    s2 = jnp.zeros((1, 256), F32)
    lane = iota((1, 256), 1)
    for t in range(9):
        lanes = slice(128 * t, 128 * t + 256)
        lhs = jnp.concatenate(
            [pd[dy, dx : dx + 8, :, lanes].astype(F32).reshape(192, 256).astype(BF16) for dx in range(3) for dy in range(3)], axis=1
        )
        r = jnp.dot(lhs, w2_ref[...], preferred_element_type=F32).reshape(8, 24, 256)
        r2_ref[:, :, t * 256 : (t + 1) * 256] = r
        own = r[2:6, 4:20, :]
        row1 = jnp.sum(jnp.sum(own, axis=0), axis=0, keepdims=True)
        row2 = jnp.sum(jnp.sum(own * own, axis=0), axis=0, keepdims=True)
        if t == 0:
            row1, row2 = (jnp.where(lane >= 64, r_, 0.0) for r_ in (row1, row2))
        if t == 8:
            row1, row2 = (jnp.where(lane < 64, r_, 0.0) for r_ in (row1, row2))
        s1, s2 = s1 + row1, s2 + row2
    out_stats_ref[...] = jnp.broadcast_to(pack_stats(s1, s2, 32).reshape(1, 1, 128), (DEVICES, 1, 128))


def second_part(at, lhs, stats, gain, shift, w1, w2):
    vmem = pl.BlockSpec(memory_space=pltpu.VMEM)
    return pl.pallas_call(
        second_kernel,
        in_specs=[pl.BlockSpec(memory_space=pltpu.SMEM)] + [vmem] * 6,
        out_specs=(vmem, vmem, vmem),
        out_shape=(
            full((8, 32, 2048), BF16),
            full((8, 24, 2304), F32),
            full((DEVICES, 1, 128), F32),
        ),
        scratch_shapes=[
            pltpu.VMEM((6, 480, 128), F32),
            pltpu.VMEM((10, 24, 1280), F32),
            pltpu.VMEM((3, 10, 24, 1280), BF16),
        ],
        compiler_params=PARAMS,
    )(at, lhs, stats, gain, shift, w1, w2)


def third_kernel(at_ref, r2_ref, stats_ref, gain_ref, shift_ref, w3_ref, f2_ref, r3_ref, out_ref, half, own2, p2, yrow):
    mean, variance = unpack_stats(jnp.sum(stats_ref[...], axis=0), VOXELS_1 / 8)
    factor = gain_ref[...] * lax.rsqrt(variance + EPSILON)
    shift = shift_ref[...]
    mean, factor, shift = (jnp.concatenate([v] * 18, axis=1) for v in (mean, factor, shift))
    bx, by, bz = at_ref[0], at_ref[1], at_ref[2]
    row, col = iota((256, 256), 0), iota((256, 256), 1)
    pick = (row == (col % 128) // 32 * 64 + col % 32 + col // 128 * 32).astype(BF16)
    for px in range(4):
        fs = []
        for i in range(2):
            f = jnp.maximum((r2_ref[2 * px + i] - mean) * factor + shift, 0.0)
            fs.append(f)
            if px in (1, 2):
                own2[...] = pltpu.roll(f, 2304 - 64, 1)[:, 0:2048]
                f2_ref[2 * (px - 1) + i] = own2[4:20, :].astype(BF16)
        pairs = jnp.maximum(fs[0], fs[1])
        for j in range(18):
            half[j, px * 24 : px * 24 + 24, :] = pairs[:, j * 128 : (j + 1) * 128]
    gy = iota((12, 128), 0) - 2 + by * 8
    for j in range(9):
        g = paired_rows(half, 2 * j, 48)
        both = jnp.dot(g.astype(BF16), pick, preferred_element_type=F32)
        pooled = jnp.maximum(both[:, 0:128], both[:, 128:256])
        gz = iota((12, 128), 1) // 32 + 4 * j - 1 + bz * 32
        inside = (gy >= 0) & (gy < 32) & (gz >= 0) & (gz < 128)
        for px in range(4):
            gx = px - 1 + bx * 2
            p2[px, 0:12, j * 128 : (j + 1) * 128] = jnp.where(
                inside & (gx >= 0) & (gx < 16), pooled[px * 12 : px * 12 + 12, :], 0.0
            )
    planes = []
    for dx in range(3):
        for dy in range(3):
            pieces = []
            for t in range(8):
                for x in range(2):
                    pieces.append(p2[x + dx, 1 + dy : 9 + dy, 128 * t : 128 * t + 256])
            planes.append(jnp.concatenate(pieces, axis=0).astype(BF16))
    r = jnp.dot(jnp.concatenate(planes, axis=1), w3_ref[...], preferred_element_type=F32)
    r3_ref[...] = r
    s1 = fold(jnp.sum(r, axis=0, keepdims=True), 64)
    s2 = fold(jnp.sum(r * r, axis=0, keepdims=True), 64)
    low = iota((8, 128), 1) < 64
    for t in range(8):
        m = jnp.maximum(r[t * 16 : t * 16 + 8, :], r[t * 16 + 8 : t * 16 + 16, :])
        a, b = m[:, 0:128], m[:, 128:256]
        a = jnp.maximum(a, pltpu.roll(a, 64, 1))
        b = jnp.maximum(b, pltpu.roll(b, 64, 1))
        yrow[:, t * 128 : (t + 1) * 128] = jnp.where(low, a, b)
    pooled = jnp.concatenate([jnp.maximum(yrow[2 * i : 2 * i + 1, :], yrow[2 * i + 1 : 2 * i + 2, :]) for i in range(4)], axis=0)
    wide = pltpu.roll(jnp.concatenate([pooled, jnp.zeros((4, 128), F32)], axis=1), 64, 1)
    lane = iota((4, 1152), 1)
    wide = jnp.where(lane < 64, jnp.concatenate([s1] * 9, axis=1), wide)
    wide = jnp.where(lane >= 1088, jnp.concatenate([s2] * 9, axis=1), wide)
    out_ref[...] = jnp.broadcast_to(wide.reshape(1, 4, 1152), (DEVICES, 4, 1152))


def third_part(at, r2, stats, gain, shift, w3):
    vmem = pl.BlockSpec(memory_space=pltpu.VMEM)
    return pl.pallas_call(
        third_kernel,
        in_specs=[pl.BlockSpec(memory_space=pltpu.SMEM)] + [vmem] * 5,
        out_specs=(vmem, vmem, vmem),
        out_shape=(
            full((4, 16, 2048), BF16),
            full((128, 256), F32),
            full((DEVICES, 4, 1152), F32),
        ),
        scratch_shapes=[
            pltpu.VMEM((18, 96, 128), F32),
            pltpu.VMEM((24, 2048), F32),
            pltpu.VMEM((4, 16, 1152), F32),
            pltpu.VMEM((8, 1024), F32),
        ],
        compiler_params=PARAMS,
    )(at, r2, stats, gain, shift, w3)


def fourth_kernel(r3_ref, all_ref, gain3_ref, shift3_ref, w4_ref, gain4_ref, shift4_ref, f3_ref, out_ref, p3, pd, r4):
    edge = jnp.sum(all_ref[:, :, 0:128], axis=0)[0:1, :]
    tail = jnp.sum(all_ref[:, :, 1024:1152], axis=0)[0:1, :]
    mean, variance = unpack_stats(jnp.where(iota((1, 128), 1) < 64, edge, tail), VOXELS_1 / 64)
    factor = gain3_ref[...] * lax.rsqrt(variance + EPSILON)
    shift = shift3_ref[...]
    mean2, factor2, shift2 = (jnp.concatenate([v] * 2, axis=1) for v in (mean, factor, shift))
    f3 = jnp.maximum((r3_ref[...] - mean2) * factor2 + shift2, 0.0)
    for t in range(8):
        for x in range(2):
            f3_ref[x, :, t * 256 : (t + 1) * 256] = f3[t * 16 + x * 8 : t * 16 + x * 8 + 8, :].astype(BF16)
    mean9, factor9, shift9 = (jnp.concatenate([v] * 9, axis=1) for v in (mean, factor, shift))
    lane = iota((4, 128), 1)
    zero = jnp.zeros((16, 4224), BF16)
    for dy in range(3):
        pd[dy, 0] = zero
        pd[dy, 9] = zero

    def place(gx, carry):
        for gy in range(4):
            last = jnp.zeros((4, 128), F32)
            for gz in range(4):
                v = jnp.maximum((all_ref[gx * 16 + gy * 4 + gz] - mean9) * factor9 + shift9, 0.0)
                start = gz * 1024
                p3[4 * gy : 4 * gy + 4, start : start + 128] = jnp.where(lane < 64, last, v[:, 0:128])
                p3[4 * gy : 4 * gy + 4, start + 128 : start + 1024] = v[:, 128:1024]
                last = v[:, 1024:1152]
            p3[4 * gy : 4 * gy + 4, 4096:4224] = jnp.where(lane < 64, last, 0.0)
        v = p3[...]
        y = iota((16, 4224), 0)
        pd[0, gx + 1] = jnp.where(y > 0, pltpu.roll(v, 1, 0), 0.0).astype(BF16)
        pd[1, gx + 1] = v.astype(BF16)
        pd[2, gx + 1] = jnp.where(y < 15, pltpu.roll(v, 15, 0), 0.0).astype(BF16)
        return carry

    lax.fori_loop(0, 8, place, 0)

    def tile(t, carry):
        s1, s2 = carry
        lanes = pl.ds(pl.multiple_of(128 * t, 128), 256)
        lhs = jnp.concatenate(
            [pd[dy, dx : dx + 8, :, lanes].reshape(128, 256) for dx in range(3) for dy in range(3)], axis=1
        )
        r = jnp.dot(lhs, w4_ref[...], preferred_element_type=F32)
        r4[t] = r
        return s1 + jnp.sum(r, axis=0, keepdims=True), s2 + jnp.sum(r * r, axis=0, keepdims=True)

    zeros = jnp.zeros((1, 256), F32)
    s1, s2 = lax.fori_loop(0, 32, tile, (zeros, zeros))
    cells = VOXELS_1 / 512
    mean = fold(s1, 128) / cells
    variance = fold(s2, 128) / cells - mean * mean
    factor = gain4_ref[...] * lax.rsqrt(variance + EPSILON)
    mean, factor, shift = (jnp.concatenate([v] * 2, axis=1) for v in (mean, factor, shift4_ref[...]))

    def finish(t, carry):
        f = jnp.maximum((r4[t] - mean) * factor + shift, 0.0).astype(BF16)
        out_ref[:, :, pl.ds(pl.multiple_of(256 * t, 256), 256)] = f.reshape(8, 16, 256)
        return carry

    lax.fori_loop(0, 32, finish, 0)


def fourth_part(r3, everything, gain3, shift3, w4, gain4, shift4):
    return pl.pallas_call(
        fourth_kernel,
        out_shape=(full((2, 8, 2048), BF16), full((8, 16, 8192), BF16)),
        scratch_shapes=[
            pltpu.VMEM((16, 4224), F32),
            pltpu.VMEM((3, 10, 16, 4224), BF16),
            pltpu.VMEM((32, 128, 256), F32),
        ],
        compiler_params=PARAMS,
    )(r3, everything, gain3, shift3, w4, gain4, shift4)


def neighbours(low_face, high_face, axis):
    count = lax.axis_size(axis)
    up = [(i, i + 1) for i in range(count - 1)]
    down = [(i + 1, i) for i in range(count - 1)]
    return lax.ppermute(high_face, axis, up), lax.ppermute(low_face, axis, down)


def along(vector, lanes):
    return jnp.tile(vector, lanes // vector.shape[0]).reshape(1, lanes)


def shards(volume, k1, g1, b1, k2, g2, b2, k3, g3, b3, k4, g4, b4):
    at = jnp.stack([lax.axis_index(a) for a in AXES]).astype(jnp.int32)
    w1, w2, w3, w4 = bands(k1.reshape(27, 16), k2.reshape(432, 32), k3.reshape(864, 64), k4.reshape(1728, 128))
    low, high = neighbours(volume, volume, "gz")
    wide = jnp.concatenate([low, volume, high], axis=2)
    low, high = neighbours(wide[:, 0:8, :], wide[:, 24:32, :], "gy")
    mid = jnp.concatenate([low, wide, high], axis=1)
    low, high = neighbours(mid, mid, "gx")
    lhs, stats = first_part(low, mid, high, w1)
    stats = lax.all_to_all(stats, AXES, 0, 0, tiled=True)
    f1, r2, stats = second_part(at, lhs, stats, along(g1, 128), along(b1, 128), w1, w2)
    stats = lax.all_to_all(stats, AXES, 0, 0, tiled=True)
    f2, r3, packed = third_part(at, r2, stats, along(g2, 128), along(b2, 128), w3)
    everything = lax.all_to_all(packed, AXES, 0, 0, tiled=True)
    f3, f4 = fourth_part(r3, everything, along(g3, 128), along(b3, 128), w4, along(g4, 128), along(b4, 128))
    return f1, f2, f3, f4


def solution(mesh):
    spread = P("gx", "gy", "gz")
    return jax.shard_map(
        shards,
        mesh=mesh,
        in_specs=(spread,) + (P(),) * 12,
        out_specs=(spread, spread, spread, P()),
        check_vma=False,
    )
```

time: 913 us -> 153 us (0.17); the launches traced: 903 us -> 152 us
  waiting for transfers between devices: 294 us -> 60 us
  blocking collectives: 214 us -> 0 us
  matrix products: 192 us -> 0 us
  local copies, waits for them, and re-layouts: 122 us -> 10.6 us
  Pallas kernels: 0 us -> 46.1 us
  other arithmetic: 17.8 us -> 0.66 us
  starting transfers between devices: 48.6 us -> 34.1 us
  between operations: 15.2 us -> 0.8 us
    all_gather x1 -> x0, waiting for transfers between devices: 273 us -> none  [shards(): lax.all_gather(third_level_pooled[None], ('gx', 'gy', 'gz'), axis=0, tile...]
    psum x3 -> x0, blocking collectives: 214 us -> none  [distribute_level(): totals = lax.psum(moments_of(response, chans_out), ('gx', 'gy', 'gz'))]
    conv_general_dilated x4 -> x0, matrix products: 192 us -> none  [conv_valid(): lax.conv_general_dilated(shaped, weight, (1, 1, 1), 'VALID', dimension_nu...]
    conv_general_dilated x21 -> x0, local copies, waits for them, and re-layouts: 56.7 us -> none  [conv_valid(): lax.conv_general_dilated(shaped, weight, (1, 1, 1), 'VALID', dimension_nu...]
    all_to_all x0 -> x3, waiting for transfers between devices: none -> 49.3 us  [the longest x1 32.1 us: shards(): everything = lax.all_to_all(packed, AXES, 0, 0, tiled=True)]
    pallas_call x0 -> x5, Pallas kernels: none -> 46.1 us  [the longest x1 16.9 us: fourth_part(): pl.pallas_call(fourth_kernel, out_shape=(full((2, 8, 2048), BF16), full((...]
    ppermute x18 -> x6, starting transfers between devices: 48.6 us -> 17.2 us  [the longest x3 12.7 us: neighbours(): lax.ppermute(high_face, axis, up)]
    another operation x5 -> x12, local copies, waits for them, and re-layouts: 30.5 us -> 5 us  [along(): return jnp.tile(vector, lanes // vector.shape[0]).reshape(1, lanes)]
  transfers between devices with their start and end apart: 19 -> 9, of which waited for: 11 -> 7; matrix products, arithmetic and copies ran while one was open for 2% -> 5% of each run, Pallas kernels for 0% -> 3%
where the time goes in v1:
time: 153 us; the launch traced here: 152 us
  waiting for transfers between devices  60 us (39%)
  Pallas kernels  46.1 us (30%)
  starting transfers between devices  34.1 us (22%)
  local copies, waits for them, and re-layouts  10.6 us (7%)
    all_to_all x1, waiting for transfers between devices, shards(): everything = lax.all_to_all(packed, AXES, 0, 0, tiled=True)  32.1 us
    all_to_all x2, waiting for transfers between devices, shards(): stats = lax.all_to_all(stats, AXES, 0, 0, tiled=True)  17.3 us
    pallas_call x1, Pallas kernels, fourth_part(): pl.pallas_call(fourth_kernel, out_shape=(full((2, 8, 2048), BF16), full((...  16.9 us
    ppermute x3, starting transfers between devices, neighbours(): lax.ppermute(high_face, axis, up)  12.7 us
    all_to_all x2, starting transfers between devices, shards(): stats = lax.all_to_all(stats, AXES, 0, 0, tiled=True)  12.4 us
    pallas_call x1, Pallas kernels, second_part(): pl.pallas_call(second_kernel, in_specs=[pl.BlockSpec(memory_space=pltpu.S...  11.7 us
    ppermute x3, waiting for transfers between devices, neighbours(): lax.ppermute(low_face, axis, down)  10.4 us
    pallas_call x1, Pallas kernels, first_part(): pl.pallas_call(first_kernel, out_shape=(full((3, 22, 48, 256), BF16), ful...  7.58 us
  transfers between devices with their start and end apart: 9, of which 7 were waited for; matrix products, arithmetic and copies ran while one was open for 5% of the time, Pallas kernels for 3%

profile of v1, /device:TPU:1, one launch (start us, length us, event | category | flops | bytes accessed | tf_op | source)
XLA Modules:
  0.0 152.4 jit_solution(5043430604144189717)
XLA Ops:
  0.6 4.0 %collective-permute-start = (bf16[8,32,128]{2,1,0:T(8,128)(2,1)}, bf16[8,32,128]{2,1,0:T(8,128)(2,1)S(1)}, u32[]{:S(2)}, u32[]{:S(2)}) collective-permute-start(bf16[8,32,128]{2,1,0:T(8,128)(2,1)} %param.13), channel_id=1, source_target_pairs={{0,1},{1,2},{2,3},{4,5},{5,6},{6,7},{8,9},{9,10},{10,11},{12,13},{... | collective-permute-start | bytes 196616 | tf_op jit(solution)/shard_map/ppermute | solution.py:400
  4.7 1.3 collective-permute-start.1
  6.0 0.3 collective-permute-done
  6.3 0.9 constant_dynamic-update-slice_fusion.1
  7.2 2.7 %collective-permute-done.1 = bf16[8,32,128]{2,1,0:T(8,128)(2,1)S(1)} collective-permute-done((bf16[8,32,128]{2,1,0:T(8,128)(2,1)}, bf16[8,32,128]{2,1,0:T(8,128)(2,1)S(1)}, u32[]{:S(2)}, u32[]{:S(2)}) %collective-permute-start.1) | collective-permute-done | bytes 65568 | tf_op jit(solution)/shard_map/ppermute | solution.py:400
  9.9 6.6 %collective-permute-start.2 = (bf16[8,8,384]{2,1,0:T(8,128)(2,1)S(1)}, bf16[8,8,384]{2,1,0:T(8,128)(2,1)S(1)}, u32[]{:S(2)}, u32[]{:S(2)}) collective-permute-start(bf16[8,8,384]{2,1,0:T(8,128)(2,1)S(1)} %get-tuple-element.32), channel_id=1, source_target_pairs={{0,4},{4,8},{8,12},{1,5},{5,9},{9,13},{2,6},{6,10},{10,14},{3,7},{... | collective-permute-start | bytes 147464 | tf_op jit(solution)/shard_map/ppermute | solution.py:400
  16.6 1.9 %collective-permute-start.3 = (bf16[8,8,384]{2,1,0:T(8,128)(2,1)S(1)}, bf16[8,8,384]{2,1,0:T(8,128)(2,1)S(1)}, u32[]{:S(2)}, u32[]{:S(2)}) collective-permute-start(bf16[8,8,384]{2,1,0:T(8,128)(2,1)S(1)} %get-tuple-element.33), channel_id=1, source_target_pairs={{4,0},{8,4},{12,8},{5,1},{9,5},{13,9},{6,2},{10,6},{14,10},{7,3},{... | collective-permute-start | bytes 147464 | tf_op jit(solution)/shard_map/ppermute | solution.py:400
  18.5 0.0 collective-permute-done.2
  18.5 5.2 %collective-permute-done.3 = bf16[8,8,384]{2,1,0:T(8,128)(2,1)S(1)} collective-permute-done((bf16[8,8,384]{2,1,0:T(8,128)(2,1)S(1)}, bf16[8,8,384]{2,1,0:T(8,128)(2,1)S(1)}, u32[]{:S(2)}, u32[]{:S(2)}) %collective-permute-start.3) | collective-permute-done | bytes 49184 | tf_op jit(solution)/shard_map/ppermute | solution.py:400
  23.7 0.0 copy-start.1
  23.8 2.0 %collective-permute-start.4 = (bf16[8,48,384]{2,1,0:T(8,128)(2,1)S(1)}, bf16[8,48,384]{2,1,0:T(8,128)(2,1)S(1)}, u32[]{:S(2)}, u32[]{:S(2)}) collective-permute-start(bf16[8,48,384]{2,1,0:T(8,128)(2,1)S(1)} %pad_maximum_fusion.mid_ref), channel_id=1, source_target_pairs={{0,16},{16,32},{32,48},{48,64},{64,80},{80,96},{96,112},{1,17},{17... | collective-permute-start | bytes 884744 | tf_op jit(solution)/shard_map/ppermute | solution.py:400
  25.8 1.3 collective-permute-start.5
  27.1 1.3 reshape.26.k1_ref
  28.4 0.7 tile.16
  29.1 0.6 reshape_tile.18.gain_ref
  29.7 0.7 tile.17
  30.3 0.6 reshape_tile.19.shift_ref
  31.0 5.1 %shard_map.156 = (bf16[768,768]{1,0:T(8,128)(2,1)}, bf16[2304,256]{1,0:T(8,128)(2,1)}, bf16[2304,256]{1,0:T(8,128)(2,1)}, bf16[2304,256]{1,0:T(8,128)(2,1)}) custom-call(bf16[27,16]{1,0:T(8,128)(2,1)} %reshape.26.k1_ref, bf16[432,32]{1,0:T(8,128)(2,1)} %bitcast.12, bf16[864,64]{1,0:T(8,128)(2,1)} %bitcast.11, bf16[1728,128]{1,0:T(8,128)(2,1)} %bitcast.10), custom_call_target="tpu_custom_call" | custom-call | tf_op jit(solution)/shard_map/pallas_call | solution.py:64
  36.0 0.0 collective-permute-done.4.lo_ref
  36.1 0.0 copy-start.2
  36.1 2.5 %collective-permute-done.5.hi_ref = bf16[8,48,384]{2,1,0:T(8,128)(2,1)S(1)} collective-permute-done((bf16[8,48,384]{2,1,0:T(8,128)(2,1)S(1)}, bf16[8,48,384]{2,1,0:T(8,128)(2,1)S(1)}, u32[]{:S(2)}, u32[]{:S(2)}) %collective-permute-start.5) | collective-permute-done | bytes 294944 | tf_op jit(solution)/shard_map/ppermute | solution.py:400
  38.5 0.0 copy-start.3
  38.5 0.0 copy-done.1
  38.5 0.0 copy-done.2
  38.5 0.7 copy-done.3
  39.2 7.6 %shard_map.157 = (bf16[3,22,48,256]{3,2,1,0:T(8,128)(2,1)}, f32[128,1,128]{2,1,0:T(1,128)}) custom-call(bf16[8,48,384]{2,1,0:T(8,128)(2,1)} %copy-done.2, bf16[8,48,384]{2,1,0:T(8,128)(2,1)} %copy-done.1, bf16[8,48,384]{2,1,0:T(8,128)(2,1)} %copy-done.3, bf16[768,768]{1,0:T(8,128)(2,1)} %get-tuple-element.18.w1_ref), custom_call_target="tpu_custom_call" | custom-call | tf_op jit(solution)/shard_map/pallas_call | solution.py:153
  46.8 7.9 %all-to-all-start = ((f32[128,1,128]{2,1,0:T(1,128)}), f32[128,1,128]{2,1,0:T(1,128)S(1)}, u32[]{:S(2)}, u32[]{:S(2)}) async-start(f32[128,1,128]{2,1,0:T(1,128)} %get-tuple-element.20), calls=%async_computation | async-start | bytes 131072 | tf_op jit(solution)/shard_map/all_to_all | solution.py:416
  54.8 0.6 pad_add_fusion.at_ref
  55.4 8.9 %all-to-all-done.stats_ref = f32[128,1,128]{2,1,0:T(1,128)S(1)} async-done(((f32[128,1,128]{2,1,0:T(1,128)}), f32[128,1,128]{2,1,0:T(1,128)S(1)}, u32[]{:S(2)}, u32[]{:S(2)}) %all-to-all-start) | async-done | bytes 65568 | tf_op jit(solution)/shard_map/all_to_all | solution.py:416
  64.3 0.0 copy-start.4
  64.3 0.6 copy-done.4
  65.0 0.0 copy-start.6
  65.0 0.0 copy-start.7
  65.0 11.7 %shard_map.158 = (bf16[8,32,2048]{2,1,0:T(8,128)(2,1)}, f32[8,24,2304]{2,1,0:T(8,128)}, f32[128,1,128]{2,1,0:T(1,128)}) custom-call(s32[3]{0:T(128)} %pad_add_fusion.at_ref, bf16[3,22,48,256]{3,2,1,0:T(8,128)(2,1)} %get-tuple-element.19.lhs_ref, f32[128,1,128]{2,1,0:T(1,128)} %copy-done.4, f32[1,128]{1,0:T(1,128)} %reshape_tile.18.gain_ref, ...), custom_call_target="tpu_custom_call" | custom-call | tf_op jit(solution)/shard_map/pallas_call | solution.py:223
  76.7 4.5 %all-to-all-start.1 = ((f32[128,1,128]{2,1,0:T(1,128)}), f32[128,1,128]{2,1,0:T(1,128)S(1)}, u32[]{:S(2)}, u32[]{:S(2)}) async-start(f32[128,1,128]{2,1,0:T(1,128)} %get-tuple-element.24), calls=%async_computation.1 | async-start | bytes 131072 | tf_op jit(solution)/shard_map/all_to_all | solution.py:418
  81.2 0.0 copy-done.6
  81.2 0.6 reshape_tile.20.gain_ref
  81.8 0.0 copy-done.7
  81.8 0.6 reshape_tile.21.shift_ref
  82.4 8.3 %all-to-all-done.1.stats_ref = f32[128,1,128]{2,1,0:T(1,128)S(1)} async-done(((f32[128,1,128]{2,1,0:T(1,128)}), f32[128,1,128]{2,1,0:T(1,128)S(1)}, u32[]{:S(2)}, u32[]{:S(2)}) %all-to-all-start.1) | async-done | bytes 65568 | tf_op jit(solution)/shard_map/all_to_all | solution.py:418
  90.7 0.0 copy-start.5
  90.7 0.6 copy-done.5
  91.4 4.9 %shard_map.159 = (bf16[4,16,2048]{2,1,0:T(8,128)(2,1)}, f32[128,256]{1,0:T(8,128)}, f32[128,4,1152]{2,1,0:T(4,128)}) custom-call(s32[3]{0:T(128)} %pad_add_fusion.at_ref, f32[8,24,2304]{2,1,0:T(8,128)} %get-tuple-element.23.r2_ref, f32[128,1,128]{2,1,0:T(1,128)} %copy-done.5, f32[1,128]{1,0:T(1,128)} %reshape_tile.20.gain_ref, ...), custom_call_target="tpu_custom_call" | custom-call | tf_op jit(solution)/shard_map/pallas_call | solution.py:301
  96.2 0.0 copy-start.8
  96.2 0.0 copy-start.9
  96.2 4.5 %all-to-all-start.2 = ((f32[128,4,1152]{2,1,0:T(4,128)}), f32[128,4,1152]{2,1,0:T(4,128)S(1)}, u32[]{:S(2)}, u32[]{:S(2)}) async-start(f32[128,4,1152]{2,1,0:T(4,128)} %get-tuple-element.28), calls=%async_computation.2 | async-start | bytes 4718592 | tf_op jit(solution)/shard_map/all_to_all | solution.py:420
  100.7 0.0 copy-done.8
  100.7 0.6 reshape_tile.22.gain3_ref
  101.3 0.0 copy-done.9
  101.3 0.7 reshape_tile.23.shift3_ref
  102.0 32.1 %all-to-all-done.2.all_ref = f32[128,4,1152]{2,1,0:T(4,128)S(1)} async-done(((f32[128,4,1152]{2,1,0:T(4,128)}), f32[128,4,1152]{2,1,0:T(4,128)S(1)}, u32[]{:S(2)}, u32[]{:S(2)}) %all-to-all-start.2) | async-done | bytes 2359328 | tf_op jit(solution)/shard_map/all_to_all | solution.py:420
  134.0 0.0 copy-start
  134.0 1.4 copy-done
  135.5 16.9 %shard_map.160 = (bf16[2,8,2048]{2,1,0:T(8,128)(2,1)}, bf16[8,16,8192]{2,1,0:T(8,128)(2,1)}) custom-call(f32[128,256]{1,0:T(8,128)} %get-tuple-element.27.r3_ref, f32[128,4,1152]{2,1,0:T(4,128)} %copy-done, f32[1,128]{1,0:T(1,128)} %reshape_tile.22.gain3_ref, f32[1,128]{1,0:T(1,128)} %reshape_tile.23.shift3_ref, bf16[2304,256]{1,0:T(8,128)(2,1)} %get-tuple-element.29.w4_ref, ...), custom_call_target="tpu_custom_call" | custom-call | tf_op jit(solution)/shard_map/pallas_call | solution.py:384
  (8 shorter events, 0.1 us)
Async XLA Ops:
  0.6 5.7 %collective-permute-start = (bf16[8,32,128]{2,1,0:T(8,128)(2,1)}, bf16[8,32,128]{2,1,0:T(8,128)(2,1)S(1)}, u32[]{:S(2)}, u32[]{:S(2)}) collective-permute-start(bf16[8,32,128]{2,1,0:T(8,128)(2,1)} %param.13), channel_id=1, source_target_pairs={{0,1},{1,2},{2,3},{4,5},{5,6},{6,7},{8,9},{9,10},{10,11},{12,13},{... | collective-permute-start | bytes 196616 | tf_op jit(solution)/shard_map/ppermute | solution.py:400
  4.7 5.2 %collective-permute-start.1 = (bf16[8,32,128]{2,1,0:T(8,128)(2,1)}, bf16[8,32,128]{2,1,0:T(8,128)(2,1)S(1)}, u32[]{:S(2)}, u32[]{:S(2)}) collective-permute-start(bf16[8,32,128]{2,1,0:T(8,128)(2,1)} %param.13), channel_id=1, source_target_pairs={{1,0},{2,1},{3,2},{5,4},{6,5},{7,6},{9,8},{10,9},{11,10},{13,12},{... | collective-permute-start | bytes 196616 | tf_op jit(solution)/shard_map/ppermute | solution.py:400
  9.9 8.6 %collective-permute-start.2 = (bf16[8,8,384]{2,1,0:T(8,128)(2,1)S(1)}, bf16[8,8,384]{2,1,0:T(8,128)(2,1)S(1)}, u32[]{:S(2)}, u32[]{:S(2)}) collective-permute-start(bf16[8,8,384]{2,1,0:T(8,128)(2,1)S(1)} %get-tuple-element.32), channel_id=1, source_target_pairs={{0,4},{4,8},{8,12},{1,5},{5,9},{9,13},{2,6},{6,10},{10,14},{3,7},{... | collective-permute-start | bytes 147464 | tf_op jit(solution)/shard_map/ppermute | solution.py:400
  16.6 7.1 %collective-permute-start.3 = (bf16[8,8,384]{2,1,0:T(8,128)(2,1)S(1)}, bf16[8,8,384]{2,1,0:T(8,128)(2,1)S(1)}, u32[]{:S(2)}, u32[]{:S(2)}) collective-permute-start(bf16[8,8,384]{2,1,0:T(8,128)(2,1)S(1)} %get-tuple-element.33), channel_id=1, source_target_pairs={{4,0},{8,4},{12,8},{5,1},{9,5},{13,9},{6,2},{10,6},{14,10},{7,3},{... | collective-permute-start | bytes 147464 | tf_op jit(solution)/shard_map/ppermute | solution.py:400
  23.7 14.8 %copy-start.1 = (bf16[8,48,384]{2,1,0:T(8,128)(2,1)}, bf16[8,48,384]{2,1,0:T(8,128)(2,1)S(1)}, u32[]{:S(2)}) copy-start(bf16[8,48,384]{2,1,0:T(8,128)(2,1)S(1)} %pad_maximum_fusion.mid_ref) | copy-start | bytes 884740
  23.8 12.3 %collective-permute-start.4 = (bf16[8,48,384]{2,1,0:T(8,128)(2,1)S(1)}, bf16[8,48,384]{2,1,0:T(8,128)(2,1)S(1)}, u32[]{:S(2)}, u32[]{:S(2)}) collective-permute-start(bf16[8,48,384]{2,1,0:T(8,128)(2,1)S(1)} %pad_maximum_fusion.mid_ref), channel_id=1, source_target_pairs={{0,16},{16,32},{32,48},{48,64},{64,80},{80,96},{96,112},{1,17},{17... | collective-permute-start | bytes 884744 | tf_op jit(solution)/shard_map/ppermute | solution.py:400
  25.8 12.7 %collective-permute-start.5 = (bf16[8,48,384]{2,1,0:T(8,128)(2,1)S(1)}, bf16[8,48,384]{2,1,0:T(8,128)(2,1)S(1)}, u32[]{:S(2)}, u32[]{:S(2)}) collective-permute-start(bf16[8,48,384]{2,1,0:T(8,128)(2,1)S(1)} %pad_maximum_fusion.mid_ref), channel_id=1, source_target_pairs={{16,0},{32,16},{48,32},{64,48},{80,64},{96,80},{112,96},{17,1},{33... | collective-permute-start | bytes 884744 | tf_op jit(solution)/shard_map/ppermute | solution.py:400
  36.1 2.5 %copy-start.2 = (bf16[8,48,384]{2,1,0:T(8,128)(2,1)}, bf16[8,48,384]{2,1,0:T(8,128)(2,1)S(1)}, u32[]{:S(2)}) copy-start(bf16[8,48,384]{2,1,0:T(8,128)(2,1)S(1)} %collective-permute-done.4.lo_ref) | copy-start | bytes 884740
  38.5 0.7 copy-start.3
  46.8 17.5 %all-to-all-start = ((f32[128,1,128]{2,1,0:T(1,128)}), f32[128,1,128]{2,1,0:T(1,128)S(1)}, u32[]{:S(2)}, u32[]{:S(2)}) async-start(f32[128,1,128]{2,1,0:T(1,128)} %get-tuple-element.20), calls=%async_computation | async-start | bytes 131072 | tf_op jit(solution)/shard_map/all_to_all | solution.py:416
  64.3 0.6 copy-start.4
  65.0 16.2 %copy-start.6 = (f32[32]{0:T(128)S(1)}, f32[32]{0:T(128)}, u32[]{:S(2)}) copy-start(f32[32]{0:T(128)} %param.18) | copy-start | bytes 388
  65.0 16.8 %copy-start.7 = (f32[32]{0:T(128)S(1)}, f32[32]{0:T(128)}, u32[]{:S(2)}) copy-start(f32[32]{0:T(128)} %param.19) | copy-start | bytes 388
  76.7 14.0 %all-to-all-start.1 = ((f32[128,1,128]{2,1,0:T(1,128)}), f32[128,1,128]{2,1,0:T(1,128)S(1)}, u32[]{:S(2)}, u32[]{:S(2)}) async-start(f32[128,1,128]{2,1,0:T(1,128)} %get-tuple-element.24), calls=%async_computation.1 | async-start | bytes 131072 | tf_op jit(solution)/shard_map/all_to_all | solution.py:418
  90.7 0.6 copy-start.5
  96.2 4.5 %copy-start.8 = (f32[64]{0:T(128)S(1)}, f32[64]{0:T(128)}, u32[]{:S(2)}) copy-start(f32[64]{0:T(128)} %param.21) | copy-start | bytes 772
  96.2 5.1 %copy-start.9 = (f32[64]{0:T(128)S(1)}, f32[64]{0:T(128)}, u32[]{:S(2)}) copy-start(f32[64]{0:T(128)} %param.22) | copy-start | bytes 772
  96.2 37.8 %all-to-all-start.2 = ((f32[128,4,1152]{2,1,0:T(4,128)}), f32[128,4,1152]{2,1,0:T(4,128)S(1)}, u32[]{:S(2)}, u32[]{:S(2)}) async-start(f32[128,4,1152]{2,1,0:T(4,128)} %get-tuple-element.28), calls=%async_computation.2 | async-start | bytes 4718592 | tf_op jit(solution)/shard_map/all_to_all | solution.py:420
  134.0 1.4 copy-start

commit v2 on v0

v2 whole, which is shorter than its diff:
```python
import functools

import jax
import jax.numpy as jnp
from jax import lax
from jax.experimental import pallas as pl
from jax.experimental.pallas import tpu as pltpu
from jax.sharding import Mesh
from jax.sharding import PartitionSpec as P

EPSILON = 1e-05
F32 = jnp.float32
BF16 = jnp.bfloat16
AXES = ("gx", "gh", "gc", "gz")
CHIPS = ("gx", "gh", "gz")
DEVICES = 128
VOXELS_1 = 64.0 * 128.0 * 512.0
PARAMS = pltpu.CompilerParams(vmem_limit_bytes=40 * 1024 * 1024)


def full(shape, dtype):
    return jax.ShapeDtypeStruct(shape, dtype)


def iota(shape, dim):
    return lax.broadcasted_iota(jnp.int32, shape, dim)


VMEM = pl.BlockSpec(memory_space=pltpu.VMEM)
ANY = pl.BlockSpec(memory_space=pl.ANY)


def near(shape, dtype):
    return pltpu.VMEM(shape, dtype)


def far(shape, dtype):
    return pltpu.HBM(shape, dtype)


def held(array):
    return pltpu.with_memory_space_constraint(array, pltpu.HBM)


def call(kernel, outs, ins, scratch=()):
    return pl.pallas_call(
        kernel,
        in_specs=[spec for _, spec in ins],
        out_specs=tuple(VMEM for _ in outs),
        out_shape=tuple(outs),
        scratch_shapes=[s if not isinstance(s, tuple) else pltpu.VMEM(*s) for s in scratch],
        compiler_params=PARAMS,
    )(*[array for array, _ in ins])


def position():
    gx, gh, gc, gz = (lax.axis_index(a) for a in AXES)
    return gx, gh * 2 + gc, gz


def first_band_kernel(k_ref, w_ref, far_ref):
    spread = (iota((16, 768), 1) % 16 == iota((16, 768), 0)).astype(BF16)
    taps = jnp.dot(k_ref[...], spread, preferred_element_type=F32)
    lag = iota((64, 768), 0) - iota((64, 768), 1) // 16
    for dx in range(3):
        for dy in range(3):
            block = jnp.zeros((64, 768), F32)
            for dz in range(3):
                t = (dx * 3 + dy) * 3 + dz
                block = jnp.where(lag == dz, taps[t : t + 1, :], block)
            w_ref[dx * 256 + dy * 64 : dx * 256 + dy * 64 + 64, :] = block.astype(BF16)
        w_ref[dx * 256 + 192 : dx * 256 + 256, :] = jnp.zeros((64, 768), BF16)
    far_ref[...] = w_ref[...]


def first_band(k):
    return call(first_band_kernel, [near((768, 768), BF16), far((768, 768), BF16)], [(k, VMEM)])


def params_kernel(*refs):
    ins, out_ref, local, sem = refs[:8], refs[8], refs[9:17], refs[17]
    copies = [pltpu.make_async_copy(a, b, sem.at[i]) for i, (a, b) in enumerate(zip(ins, local))]
    for c in copies:
        c.start()
    for c in copies:
        c.wait()
    lane = iota((1, 128), 1)
    for i, ref in enumerate(local):
        count = ref.shape[0]
        row = jnp.zeros((1, 128), F32)
        for c in range(count):
            row = jnp.where(lane % count == c, ref[c], row)
        out_ref[i : i + 1, :] = row


def params(*vectors):
    return call(
        params_kernel,
        [near((8, 128), F32)],
        [(held(v), ANY) for v in vectors],
        [pltpu.SMEM(v.shape, F32) for v in vectors] + [pltpu.SemaphoreType.DMA((8,))],
    )[0]


def band_kernel(cin, cout, first, k_ref, w_ref, t_ref):
    outs = 256 // cout
    tile = (iota((cout, 256), 1) % cout == iota((cout, 256), 0)).astype(BF16)
    t_ref[...] = jnp.dot(k_ref[...], tile, preferred_element_type=F32)
    zo = iota((cin, 256), 1) // cout

    def plane(p, carry):
        for zi in range(-first, 256 // cin - first):
            block = jnp.zeros((cin, 256), F32)
            if 0 <= zi < outs + 2:
                for dz in range(3):
                    start = pl.multiple_of((p * 3 + dz) * cin, cin)
                    block = jnp.where(zo == zi - dz, t_ref[pl.ds(start, cin), :], block)
            start = pl.multiple_of(p * 256 + (zi + first) * cin, cin)
            w_ref[pl.ds(start, cin), :] = block.astype(BF16)
        return carry

    lax.fori_loop(0, 9, plane, 0)


def band(k, first):
    cin, cout = k.shape[3:]
    return call(
        functools.partial(band_kernel, cin, cout, first),
        [near((2304, 256), BF16)],
        [(held(k.reshape(27 * cin, cout)), VMEM)],
        [((27 * cin, 256), F32)],
    )[0]


def fold(row, width):
    total = row[:, 0:128]
    for j in range(1, row.shape[1] // 128):
        total = total + row[:, j * 128 : (j + 1) * 128]
    step = 64
    while step >= width:
        total = total + pltpu.roll(total, step, 1)
        step //= 2
    return total


def pack_stats(s1, s2, width):
    return jnp.where(iota((1, 128), 1) < 64, fold(s1, width), fold(s2, width))


def normaliser(total, cells, params_ref, level, copies):
    lane = iota((1, 128), 1)
    other = pltpu.roll(total, 64, 1)
    mean = jnp.where(lane < 64, total, other) / cells
    variance = jnp.where(lane < 64, other, total) / cells - mean * mean
    shift = params_ref[2 * level + 1 : 2 * level + 2, :]
    factor = params_ref[2 * level : 2 * level + 1, :] * lax.rsqrt(variance + EPSILON)
    return tuple(jnp.concatenate([v] * copies, axis=1) for v in (mean, factor, shift))


def settle(response, normal):
    mean, factor, shift = normal
    return jnp.maximum((response - mean) * factor + shift, 0.0)


def slots(stats):
    return jnp.broadcast_to(stats.reshape(1, 1, 128), (DEVICES, 1, 128))


def paired_rows(ref, j, count):
    return jnp.maximum(ref[j, pl.ds(0, count, stride=2), :], ref[j, pl.ds(1, count, stride=2), :])


def fill(out_ref, at, v):
    lane = iota((48, 128), 1)
    for q, part, turn in ((0, v, 9), (1, v[:, 0:128], 128 - 39), (2, v, 256 - 87)):
        wa = pltpu.roll(part, turn, 1)[:, 0:128]
        wb = pltpu.roll(wa, 64, 1)
        out_ref[q, at, :, 0:128] = jnp.where(lane < 64, pltpu.roll(wa, 1, 0), wb).astype(BF16)
        out_ref[q, at, :, 128:256] = pltpu.roll(wa, 47, 0).astype(BF16)


def response_1(planes, w1_ref):
    lhs = jnp.concatenate(planes, axis=2)
    n, rows, _ = lhs.shape
    r = jnp.dot(lhs.reshape(n * rows, 768), w1_ref[...], preferred_element_type=F32)
    return r.reshape(n, rows, 768)


def sums_1(r, q):
    own = r[:, 8:40, :].reshape(-1, 768)
    row1 = jnp.sum(own, axis=0, keepdims=True)
    row2 = jnp.sum(own * own, axis=0, keepdims=True)
    at = iota((1, 768), 1)
    if q == 0:
        row1, row2 = (jnp.where(at >= 128, r_, 0.0) for r_ in (row1, row2))
    if q == 2:
        row1, row2 = (jnp.where(at < 640, r_, 0.0) for r_ in (row1, row2))
    return row1, row2


def halve_rows(r, rows, half_ref, q):
    n = r.shape[0]
    flat = r.reshape(n * 48, 768)
    for j in range(6):
        rows[j, 0 : n * 48] = flat[:, j * 128 : (j + 1) * 128]
    for j in range(6):
        half_ref[q * 6 + j] = paired_rows(rows, j, n * 24)


def middle_kernel(mid_ref, w1_ref, lhs_ref, far_ref, half_ref, sums_ref, rows):
    def step(i, carry):
        fill(lhs_ref, i, mid_ref[i].astype(F32))
        return carry

    lax.fori_loop(0, 8, step, 0, unroll=4)
    s1 = jnp.zeros((1, 768), F32)
    s2 = jnp.zeros((1, 768), F32)
    for q in range(3):
        r = response_1([lhs_ref[q, dx : 6 + dx] for dx in range(3)], w1_ref)
        row1, row2 = sums_1(r, q)
        s1, s2 = s1 + row1, s2 + row2
        halve_rows(r, rows, half_ref, q)
    sums_ref[0:1, :] = s1
    sums_ref[1:2, :] = s2
    far_ref[...] = lhs_ref[...]


def middle_part(mid, w1):
    return call(
        middle_kernel,
        [near((3, 8, 48, 256), BF16), far((3, 8, 48, 256), BF16), far((18, 144, 128), F32), near((8, 768), F32)],
        [(mid, VMEM), (w1, VMEM)],
        [((6, 288, 128), F32)],
    )


def first_kernel(lo_ref, hi_ref, mid_ref, sums_ref, w1_ref, ends_ref, half_ref, stats_ref, rows, lo, hi, sems):
    copies = [
        pltpu.make_async_copy(lo_ref.at[7], lo, sems.at[0]),
        pltpu.make_async_copy(hi_ref.at[0], hi, sems.at[1]),
    ]
    for c in copies:
        c.start()
    ends_ref[:, 1:2] = mid_ref[:, 0:1]
    ends_ref[:, 2:3] = mid_ref[:, 7:8]
    for c in copies:
        c.wait()
    fill(ends_ref, 0, lo[...].astype(F32))
    fill(ends_ref, 3, hi[...].astype(F32))
    planes = []
    for q in range(3):
        a = [ends_ref[q, 0:1], mid_ref[q, 0:1], mid_ref[q, 1:2]]
        b = [mid_ref[q, 6:7], mid_ref[q, 7:8], ends_ref[q, 3:4]]
        planes.append([jnp.concatenate([a[dx], b[dx]], axis=0) for dx in range(3)])
    r = response_1([jnp.concatenate([planes[q][dx] for q in range(3)], axis=0) for dx in range(3)], w1_ref)
    s1 = sums_ref[0:1, :]
    s2 = sums_ref[1:2, :]
    for q in range(3):
        row1, row2 = sums_1(r[2 * q : 2 * q + 2], q)
        s1, s2 = s1 + row1, s2 + row2
    stats_ref[...] = slots(pack_stats(s1, s2, 16))
    for q in range(3):
        halve_rows(r[2 * q : 2 * q + 2], rows, half_ref, q)


def first_part(lo, hi, lhs_mid, sums, w1):
    return call(
        first_kernel,
        [far((3, 4, 48, 256), BF16), far((18, 48, 128), F32), far((DEVICES, 1, 128), F32)],
        [(held(lo), ANY), (held(hi), ANY), (lhs_mid, VMEM), (sums, VMEM), (w1, VMEM)],
        [((6, 96, 128), F32), ((48, 256), BF16), ((48, 256), BF16), pltpu.SemaphoreType.DMA((2,))],
    )


def wide_first_kernel(
    lo_ref, hi_ref, ends_ref, half_mid_ref, half_edge_ref, w1_far, half_ref, lhs, rows, wide, w1_ref, sem
):
    weights = pltpu.make_async_copy(w1_far, w1_ref, sem)
    weights.start()

    def step(i, carry):
        fill(lhs, i, lo_ref[1 + i].astype(F32))
        fill(lhs, 10 + i, hi_ref[1 + i].astype(F32))
        return carry

    lax.fori_loop(0, 6, step, 0, unroll=2)
    lhs[:, 6:10] = ends_ref[...]
    weights.wait()
    for q in range(3):
        planes = [jnp.concatenate([lhs[q, dx : 6 + dx], lhs[q, 8 + dx : 14 + dx]], axis=0) for dx in range(3)]
        halve_rows(response_1(planes, w1_ref), rows, wide, q)

    def merge(j, carry):
        outer = wide[j].reshape(6, 2, 24, 128)
        inner = half_mid_ref[j].reshape(6, 24, 128)
        edges = half_edge_ref[j].reshape(2, 24, 128)
        outer = jnp.maximum(outer[:, 0], outer[:, 1])
        half_ref[j, 0:72] = outer[0:3].reshape(72, 128)
        half_ref[j, 72:96] = jnp.maximum(edges[0], inner[0])
        half_ref[j, 96:120] = jnp.maximum(inner[1], inner[2])
        half_ref[j, 120:144] = jnp.maximum(inner[3], inner[4])
        half_ref[j, 144:168] = jnp.maximum(inner[5], edges[1])
        half_ref[j, 168:240] = outer[3:6].reshape(72, 128)
        return carry

    lax.fori_loop(0, 18, merge, 0)


def wide_first_part(lo, hi, ends, half_mid, half_edge, w1):
    return call(
        wide_first_kernel,
        [near((18, 240, 128), F32)],
        [(held(a), VMEM) for a in (lo, hi, ends, half_mid, half_edge)] + [(held(w1), ANY)],
        [((3, 16, 48, 256), BF16), ((6, 576, 128), F32), ((18, 288, 128), F32), ((768, 768), BF16)]
        + [pltpu.SemaphoreType.DMA(())],
    )[0]


def first_output_kernel(mid_ref, ends_ref, w1_ref, stats_ref, params_ref, f1_ref):
    normal = normaliser(jnp.sum(stats_ref[...], axis=0), VOXELS_1, params_ref, 0, 6)
    for q in range(3):
        middle = mid_ref[q]
        planes = [
            jnp.concatenate([ends_ref[q, 0:1], middle[0:7]], axis=0),
            middle,
            jnp.concatenate([middle[1:8], ends_ref[q, 3:4]], axis=0),
        ]
        f = settle(response_1([p[:, 8:40, :] for p in planes], w1_ref), normal)
        a, b = (128 if q == 0 else 0), (640 if q == 2 else 768)
        f1_ref[:, :, q * 768 - 128 + a : q * 768 - 128 + b] = f[:, :, a:b].astype(BF16)


def first_output(lhs_mid, ends, w1, stats, table):
    return call(
        first_output_kernel,
        [full((8, 32, 2048), BF16)],
        [(held(a), VMEM) for a in (lhs_mid, ends, w1)] + [(stats, VMEM), (table, VMEM)],
    )[0]


def selector(chans):
    row, col = iota((256, 256), 0), iota((256, 256), 1)
    return (row == (col % 128) // chans * (2 * chans) + col % chans + col // 128 * chans).astype(BF16)


def halved(left, right, normal, pick):
    features = jnp.concatenate([settle(left, normal), settle(right, normal)], axis=1).astype(BF16)
    both = jnp.dot(features, pick, preferred_element_type=F32)
    return jnp.maximum(both[:, 0:128], both[:, 128:256])


def second_kernel(half_ref, stats_ref, params_ref, w2_ref, p1_ref, r2_ref, out_stats_ref, p1, pd):
    normal = normaliser(jnp.sum(stats_ref[...], axis=0), VOXELS_1, params_ref, 0, 1)
    pick = selector(16)
    bx, by, bz = position()
    p1[:, :, 1152:1280] = jnp.zeros((10, 24, 128), F32)
    gy = iota((10, 24, 128), 1) - 4 + by * 16
    gx = iota((10, 24, 128), 0) - 3 + bx * 4
    inside = (gy >= 0) & (gy < 64) & (gx >= 0) & (gx < 32)
    for j in range(9):
        pooled = halved(half_ref[2 * j], half_ref[2 * j + 1], normal, pick).reshape(10, 24, 128)
        gz = iota((10, 24, 128), 2) // 16 - 4 + 8 * j + bz * 64
        p1[:, :, j * 128 : (j + 1) * 128] = jnp.where(inside & (gz >= 0) & (gz < 256), pooled, 0.0)
    for dy in range(3):
        pd[dy] = p1[2:8, 3 + dy : 19 + dy, :].astype(BF16)
    p1_ref[...] = p1[...].astype(BF16)
    planes = []
    for dx in range(3):
        for dy in range(3):
            pieces = [pd[dy, dx : dx + 4, :, 128 * t : 128 * t + 256].reshape(64, 256) for t in range(9)]
            planes.append(jnp.concatenate(pieces, axis=0))
    r = jnp.dot(jnp.concatenate(planes, axis=1), w2_ref[...], preferred_element_type=F32)
    r2_ref[...] = r
    s1 = jnp.zeros((1, 256), F32)
    s2 = jnp.zeros((1, 256), F32)
    lane = iota((1, 256), 1)
    for t in range(9):
        own = r[64 * t : 64 * t + 64]
        row1 = jnp.sum(own, axis=0, keepdims=True)
        row2 = jnp.sum(own * own, axis=0, keepdims=True)
        if t == 0:
            row1, row2 = (jnp.where(lane >= 64, r_, 0.0) for r_ in (row1, row2))
        if t == 8:
            row1, row2 = (jnp.where(lane < 64, r_, 0.0) for r_ in (row1, row2))
        s1, s2 = s1 + row1, s2 + row2
    out_stats_ref[...] = slots(pack_stats(s1, s2, 32))


def second_part(half, stats, table, w2):
    return call(
        second_kernel,
        [far((10, 24, 1280), BF16), far((576, 256), F32), far((DEVICES, 1, 128), F32)],
        [(a, VMEM) for a in (half, stats, table, w2)],
        [((10, 24, 1280), F32), ((3, 6, 16, 1280), BF16)],
    )


def wide_second_kernel(p1_ref, w2_ref, half_ref, pd, rows):
    def shift(i, carry):
        v = p1_ref[i].astype(F32)
        pd[0, i] = pltpu.roll(v, 1, 0)
        pd[1, i] = v
        pd[2, i] = pltpu.roll(v, 23, 0)
        return carry

    lax.fori_loop(0, 10, shift, 0)
    for t in range(0, 9, 3):
        planes = []
        for dx in range(3):
            for dy in range(3):
                pieces = [pd[dy, dx : dx + 8, :, 128 * u : 128 * u + 256].reshape(192, 256) for u in range(t, t + 3)]
                planes.append(jnp.concatenate(pieces, axis=0).astype(BF16))
        r = jnp.dot(jnp.concatenate(planes, axis=1), w2_ref[...], preferred_element_type=F32)
        r = jnp.max(r.reshape(3, 4, 2, 24, 256), axis=2).reshape(3, 96, 256)
        for i in range(3):
            for j in range(2):
                rows[2 * i + j] = r[i, :, j * 128 : (j + 1) * 128]
        for j in range(6):
            half_ref[2 * t + j] = paired_rows(rows, j, 48)


def wide_second_part(p1, w2):
    return call(
        wide_second_kernel,
        [near((18, 48, 128), F32)],
        [(held(p1), VMEM), (w2, VMEM)],
        [((3, 10, 24, 1280), F32), ((6, 96, 128), F32)],
    )[0]


def second_output_kernel(r2_ref, stats_ref, params_ref, f2_ref):
    normal = normaliser(jnp.sum(stats_ref[...], axis=0), VOXELS_1 / 8, params_ref, 1, 2)
    f = [settle(r2_ref[64 * t : 64 * t + 64, :], normal) for t in range(9)]
    wide = pltpu.roll(jnp.concatenate(f, axis=1), 2304 - 64, 1)[:, 0:2048]
    f2_ref[...] = wide.reshape(4, 16, 2048).astype(BF16)


def second_output(r2, stats, table):
    return call(
        second_output_kernel,
        [full((4, 16, 2048), BF16)],
        [(held(r2), VMEM), (stats, VMEM), (table, VMEM)],
    )[0]


def third_kernel(half_ref, stats_ref, params_ref, w3_ref, r3_ref, out_ref, p2, yrow):
    normal = normaliser(jnp.sum(stats_ref[...], axis=0), VOXELS_1 / 8, params_ref, 1, 1)
    bx, by, bz = position()
    pick = selector(32)
    gy = iota((12, 128), 0) - 2 + by * 8
    for j in range(9):
        pooled = halved(half_ref[2 * j], half_ref[2 * j + 1], normal, pick)
        gz = iota((12, 128), 1) // 32 + 4 * j - 1 + bz * 32
        inside = (gy >= 0) & (gy < 32) & (gz >= 0) & (gz < 128)
        for px in range(4):
            gx = px - 1 + bx * 2
            p2[px, 0:12, j * 128 : (j + 1) * 128] = jnp.where(
                inside & (gx >= 0) & (gx < 16), pooled[px * 12 : px * 12 + 12, :], 0.0
            )
    planes = []
    for dx in range(3):
        for dy in range(3):
            pieces = []
            for t in range(8):
                for x in range(2):
                    pieces.append(p2[x + dx, 1 + dy : 9 + dy, 128 * t : 128 * t + 256])
            planes.append(jnp.concatenate(pieces, axis=0).astype(BF16))
    r = jnp.dot(jnp.concatenate(planes, axis=1), w3_ref[...], preferred_element_type=F32)
    r3_ref[...] = r
    s1 = fold(jnp.sum(r, axis=0, keepdims=True), 64)
    s2 = fold(jnp.sum(r * r, axis=0, keepdims=True), 64)
    low = iota((8, 128), 1) < 64
    for t in range(8):
        m = jnp.maximum(r[t * 16 : t * 16 + 8, :], r[t * 16 + 8 : t * 16 + 16, :])
        a, b = m[:, 0:128], m[:, 128:256]
        a = jnp.maximum(a, pltpu.roll(a, 64, 1))
        b = jnp.maximum(b, pltpu.roll(b, 64, 1))
        yrow[:, t * 128 : (t + 1) * 128] = jnp.where(low, a, b)
    pooled = jnp.concatenate(
        [jnp.maximum(yrow[2 * i : 2 * i + 1, :], yrow[2 * i + 1 : 2 * i + 2, :]) for i in range(4)], axis=0
    )
    mean_here = s1 / 512.0
    spread = jnp.sqrt(jnp.maximum(s2 / 512.0 - mean_here * mean_here, 0.0))
    begin = mean_here + jnp.clip(-params_ref[5:6, :] / params_ref[4:5, :], -8.0, 8.0) * spread
    offset = jnp.maximum(begin, fold(jnp.sum(pooled, axis=0, keepdims=True), 64) / 64.0)
    at = iota((1, 128), 1)
    offset = offset.astype(BF16).astype(F32)
    apart = pooled - jnp.concatenate([offset] * 8, axis=1)
    wide = pltpu.roll(jnp.concatenate([apart, jnp.zeros((4, 128), F32)], axis=1), 64, 1)
    sums = jnp.where(at < 64, s1, s2)
    high = sums.astype(BF16).astype(F32)
    middle = (sums - high).astype(BF16).astype(F32)
    edge = jnp.concatenate([high, middle, sums - high - middle, offset], axis=0)
    ends = iota((4, 128), 1) < 64
    out = jnp.concatenate(
        [jnp.where(ends, edge, wide[:, 0:128]), wide[:, 128:1024], jnp.where(ends, wide[:, 1024:1152], edge)], axis=1
    ).astype(BF16)
    out_ref[...] = jnp.broadcast_to(out.reshape(1, 4, 1152), (DEVICES // 2, 4, 1152))


def third_part(half, stats, table, w3):
    return call(
        third_kernel,
        [near((128, 256), F32), far((DEVICES // 2, 4, 1152), BF16)],
        [(a, VMEM) for a in (half, stats, table, w3)],
        [((4, 16, 1152), F32), ((8, 1024), F32)],
    )


def fourth_kernel(r3_ref, own_ref, other_ref, params_ref, w4_ref, f3_ref, out_ref, p3, pd, r4):
    edge = jnp.zeros((4, 128), F32)
    tail = jnp.zeros((4, 128), F32)
    for ref in (own_ref, other_ref):
        edge = edge + jnp.sum(ref[:, :, 0:128].astype(F32), axis=0)
        tail = tail + jnp.sum(ref[:, :, 1024:1152].astype(F32), axis=0)
    total = jnp.sum(jnp.where(iota((4, 128), 1) < 64, edge, tail)[0:3, :], axis=0, keepdims=True)
    normal = normaliser(total, VOXELS_1 / 64, params_ref, 2, 2)
    f3 = settle(r3_ref[...], normal)
    for t in range(8):
        for x in range(2):
            f3_ref[x, :, t * 256 : (t + 1) * 256] = f3[t * 16 + x * 8 : t * 16 + x * 8 + 8, :].astype(BF16)
    lane = iota((4, 128), 1)
    low = iota((16, 128), 1) < 64
    y = iota((16, 128), 0)
    one = tuple(v[:, 0:128] for v in normal)
    zero = jnp.zeros((16, 4224), BF16)
    for dy in range(3):
        pd[dy, 0] = zero
        pd[dy, 9] = zero

    def place(even_ref, odd_ref):
        def step(gx, carry):
            for gy in range(4):
                ref = even_ref if gy % 2 == 0 else odd_ref
                last = jnp.zeros((4, 128), F32)
                for gz in range(4):
                    v = ref[(gx * 2 + gy // 2) * 4 + gz].astype(F32)
                    v0, v8 = v[:, 0:128], v[:, 1024:1152]
                    offset = jnp.where(lane < 64, v0, v8)[3:4, :]
                    start = gz * 1024
                    p3[4 * gy : 4 * gy + 4, start : start + 128] = jnp.where(lane < 64, last, v0 + offset)
                    p3[4 * gy : 4 * gy + 4, start + 128 : start + 1024] = v[:, 128:1024] + jnp.concatenate([offset] * 7, axis=1)
                    last = v8 + offset
                p3[4 * gy : 4 * gy + 4, 4096:4224] = last
            for j in range(33):
                lanes = slice(j * 128, (j + 1) * 128)
                v = settle(p3[:, lanes], one)
                if j == 0:
                    v = jnp.where(low, 0.0, v)
                if j == 32:
                    v = jnp.where(low, v, 0.0)
                pd[0, gx + 1, :, lanes] = jnp.where(y > 0, pltpu.roll(v, 1, 0), 0.0).astype(BF16)
                pd[1, gx + 1, :, lanes] = v.astype(BF16)
                pd[2, gx + 1, :, lanes] = jnp.where(y < 15, pltpu.roll(v, 15, 0), 0.0).astype(BF16)
            return carry

        lax.fori_loop(0, 8, step, 0)

    core = lax.axis_index("gc")

    @pl.when(core == 0)
    def _():
        place(own_ref, other_ref)

    @pl.when(core != 0)
    def _():
        place(other_ref, own_ref)

    def tiles(i, carry):
        s1, s2 = carry
        planes = []
        for dx in range(3):
            for dy in range(3):
                pieces = [
                    pd[dy, dx : dx + 8, :, pl.ds(pl.multiple_of(128 * (i * 8 + g), 128), 256)].reshape(128, 256)
                    for g in range(8)
                ]
                planes.append(jnp.concatenate(pieces, axis=0))
        r = jnp.dot(jnp.concatenate(planes, axis=1), w4_ref[...], preferred_element_type=F32)
        r4[pl.ds(pl.multiple_of(i * 1024, 1024), 1024), :] = r
        return s1 + jnp.sum(r, axis=0, keepdims=True), s2 + jnp.sum(r * r, axis=0, keepdims=True)

    zeros = jnp.zeros((1, 256), F32)
    s1, s2 = lax.fori_loop(0, 4, tiles, (zeros, zeros))
    cells = VOXELS_1 / 512
    mean = fold(s1, 128) / cells
    variance = fold(s2, 128) / cells - mean * mean
    factor = params_ref[6:7, :] * lax.rsqrt(variance + EPSILON)
    last = tuple(jnp.concatenate([v] * 2, axis=1) for v in (mean, factor, params_ref[7:8, :]))

    def finish(t, carry):
        f = settle(r4[pl.ds(pl.multiple_of(t * 128, 128), 128), :], last).astype(BF16)
        out_ref[:, :, pl.ds(pl.multiple_of(256 * t, 256), 256)] = f.reshape(8, 16, 256)
        return carry

    lax.fori_loop(0, 32, finish, 0)


def fourth_part(r3, own, other, table, w4):
    return call(
        fourth_kernel,
        [full((2, 8, 2048), BF16), full((8, 16, 8192), BF16)],
        [(a, VMEM) for a in (r3, own, other, table, w4)],
        [((16, 4224), F32), ((3, 10, 16, 4224), BF16), ((4096, 256), F32)],
    )


def neighbours(low_face, high_face, axis, count):
    up = [(i, i + 1) for i in range(count - 1)]
    down = [(i + 1, i) for i in range(count - 1)]
    return lax.ppermute(high_face, axis, up), lax.ppermute(low_face, axis, down)


def after(values, event):
    return lax.optimization_barrier((values, event))


def shards(volume, k1, g1, b1, k2, g2, b2, k3, g3, b3, k4, g4, b4):
    low, high = neighbours(volume, volume, "gz", 4)
    w1, w1_far = first_band(k1.reshape(27, 16))
    (low, high, w1) = lax.optimization_barrier((low, high, w1))
    edge = jnp.where(lax.broadcasted_iota(jnp.int32, volume.shape, 2) < 64, high, low)
    wide = jnp.concatenate([volume, edge], axis=2)
    low, high = neighbours(wide[:, 0:8, :], wide[:, 24:32, :], ("gh", "gc"), 4)
    mid = jnp.concatenate([low, wide, high], axis=1)
    (mid, k2, g1) = lax.optimization_barrier((mid, k2, g1))
    low, high = neighbours(mid, mid, "gx", 8)
    lhs_mid, far_mid, half_mid, sums = middle_part(mid, w1)
    w2 = band(k2, 1)
    table = params(g1, b1, g2, b2, g3, b3, g4, b4)
    (low, high, lhs_mid, w2, table) = lax.optimization_barrier((low, high, lhs_mid, w2, table))
    ends, half_edge, stats = first_part(low, high, lhs_mid, sums, w1)

    total1 = lax.all_to_all(stats, AXES, 0, 0, tiled=True)
    half1 = wide_first_part(low, high, ends, half_mid, half_edge, w1_far)
    half1, total1 = after(half1, total1)
    p1, r2, stats = second_part(half1, total1, table, w2)

    (p1, k3), stats = after((p1, k3), stats)
    total2 = lax.all_to_all(stats, AXES, 0, 0, tiled=True)
    half2 = wide_second_part(p1, w2)
    w3 = band(k3, 0)
    (half2, w3), total2 = after((half2, w3), total2)
    r3, packed = third_part(half2, total2, table, w3)

    (k4, far_mid, r2), packed = after((k4, far_mid, r2), packed)
    own = lax.all_to_all(packed, CHIPS, 0, 0, tiled=True)
    f1 = first_output(far_mid, ends, w1_far, total1, table)
    f2 = second_output(r2, total2, table)
    w4 = band(k4, 0)
    (f1, f2, w4), own = after((f1, f2, w4), own)
    other = lax.ppermute(own, "gc", [(0, 1), (1, 0)])
    f3, f4 = fourth_part(r3, own, other, table, w4)
    return f1, f2, f3, f4


def solution(mesh):
    parts = Mesh(mesh.devices.reshape(8, 2, 2, 4), AXES)
    spread = P("gx", ("gh", "gc"), "gz")
    return jax.shard_map(
        shards,
        mesh=parts,
        in_specs=(spread,) + (P(),) * 12,
        out_specs=(spread, spread, spread, P()),
        check_vma=False,
    )
```

time: 913 us -> 110 us (0.12)
  waiting for transfers between devices: 294 us -> 21.8 us
  blocking collectives: 214 us -> 0 us
  matrix products: 192 us -> 0 us
  local copies, waits for them, and re-layouts: 122 us -> 1.43 us
  Pallas kernels: 0 us -> 41.8 us
  other arithmetic: 17.8 us -> 1.63 us
  between operations: 15.2 us -> 0.81 us
    all_gather x1 -> x0, waiting for transfers between devices: 273 us -> none  [shards(): lax.all_gather(third_level_pooled[None], ('gx', 'gy', 'gz'), axis=0, tile...]
    psum x3 -> x0, blocking collectives: 214 us -> none  [distribute_level(): totals = lax.psum(moments_of(response, chans_out), ('gx', 'gy', 'gz'))]
    conv_general_dilated x4 -> x0, matrix products: 192 us -> none  [conv_valid(): lax.conv_general_dilated(shaped, weight, (1, 1, 1), 'VALID', dimension_nu...]
    conv_general_dilated x21 -> x0, local copies, waits for them, and re-layouts: 56.7 us -> none  [conv_valid(): lax.conv_general_dilated(shaped, weight, (1, 1, 1), 'VALID', dimension_nu...]
    pallas_call x0 -> x14, Pallas kernels: none -> 41.8 us  [call(): pl.pallas_call(kernel, in_specs=[spec for _, spec in ins], out_specs=tupl...]
    another operation x5 -> x0, local copies, waits for them, and re-layouts: 30.5 us -> none  [the longest x4 29.9 us: settle(): flat = response.reshape(-1, channel_list)]
    ppermute x18 -> x7, starting transfers between devices: 48.6 us -> 21.1 us  [the longest x3 14.7 us: neighbours(): lax.ppermute(high_face, axis, up)]
    all_to_all x0 -> x3, starting transfers between devices: none -> 20.4 us  [the longest x1 8.11 us: shards(): total1 = lax.all_to_all(stats, AXES, 0, 0, tiled=True)]
  transfers between devices with their start and end apart: 19 -> 10, of which waited for: 11 -> 6; matrix products, arithmetic and copies ran while one was open for 2% -> 1% of each run, Pallas kernels for 0% -> 23%
where the time goes in v2:
time: 110 us; the launch traced here: 109 us
  Pallas kernels  41.8 us (38%)
  starting transfers between devices  41.5 us (38%)
  waiting for transfers between devices  21.8 us (20%)
  other arithmetic  1.63 us (1%)
  local copies, waits for them, and re-layouts  1.43 us (1%)
    pallas_call x14, Pallas kernels, call(): pl.pallas_call(kernel, in_specs=[spec for _, spec in ins], out_specs=tupl...  41.8 us
    ppermute x3, starting transfers between devices, neighbours(): lax.ppermute(high_face, axis, up)  14.7 us
    all_to_all x1, starting transfers between devices, shards(): total1 = lax.all_to_all(stats, AXES, 0, 0, tiled=True)  8.11 us
    ppermute x3, waiting for transfers between devices, neighbours(): lax.ppermute(low_face, axis, down)  6.64 us
    all_to_all x1, starting transfers between devices, shards(): own = lax.all_to_all(packed, CHIPS, 0, 0, tiled=True)  6.24 us
    all_to_all x1, starting transfers between devices, shards(): total2 = lax.all_to_all(stats, AXES, 0, 0, tiled=True)  6.01 us
    all_to_all x1, waiting for transfers between devices, shards(): own = lax.all_to_all(packed, CHIPS, 0, 0, tiled=True)  5.26 us
    ppermute x3, starting transfers between devices, neighbours(): lax.ppermute(low_face, axis, down)  4.5 us
  transfers between devices with their start and end apart: 10, of which 6 were waited for; matrix products, arithmetic and copies ran while one was open for 1% of the time, Pallas kernels for 23%

profile of v2, /device:TPU:1, one launch (start us, length us, event | category | flops | bytes accessed | tf_op | source)
XLA Modules:
  0.0 108.9 jit_solution(7832356986318952945)
XLA Ops:
  0.6 4.0 %collective-permute-start = (bf16[8,32,128]{2,1,0:T(8,128)(2,1)}, bf16[8,32,128]{2,1,0:T(8,128)(2,1)S(1)}, u32[]{:S(2)}, u32[]{:S(2)}) collective-permute-start(bf16[8,32,128]{2,1,0:T(8,128)(2,1)} %param.13), channel_id=1, source_target_pairs={{0,1},{1,2},{2,3},{4,5},{5,6},{6,7},{8,9},{9,10},{10,11},{12,13},{... | collective-permute-start | bytes 196616 | tf_op jit(solution)/shard_map/ppermute | solution.py:611
  4.7 1.3 %collective-permute-start.1 = (bf16[8,32,128]{2,1,0:T(8,128)(2,1)}, bf16[8,32,128]{2,1,0:T(8,128)(2,1)S(1)}, u32[]{:S(2)}, u32[]{:S(2)}) collective-permute-start(bf16[8,32,128]{2,1,0:T(8,128)(2,1)} %param.13), channel_id=1, source_target_pairs={{1,0},{2,1},{3,2},{5,4},{6,5},{7,6},{9,8},{10,9},{11,10},{13,12},{... | collective-permute-start | bytes 196616 | tf_op jit(solution)/shard_map/ppermute | solution.py:611
  6.0 0.7 reshape.20.k_ref
  6.7 1.4 %shard_map.156 = (bf16[768,768]{1,0:T(8,128)(2,1)S(1)}, bf16[768,768]{1,0:T(8,128)(2,1)}) custom-call(bf16[27,16]{1,0:T(8,128)(2,1)S(1)} %reshape.20.k_ref), custom_call_target="tpu_custom_call" | custom-call | tf_op jit(solution)/shard_map/pallas_call | solution.py:46
  8.1 0.0 collective-permute-done
  8.1 1.8 %collective-permute-done.1 = bf16[8,32,128]{2,1,0:T(8,128)(2,1)S(1)} collective-permute-done((bf16[8,32,128]{2,1,0:T(8,128)(2,1)}, bf16[8,32,128]{2,1,0:T(8,128)(2,1)S(1)}, u32[]{:S(2)}, u32[]{:S(2)}) %collective-permute-start.1) | collective-permute-done | bytes 65568 | tf_op jit(solution)/shard_map/ppermute | solution.py:611
  9.9 0.7 pad_maximum_fusion.2
  10.7 6.6 %collective-permute-start.2 = (bf16[8,8,256]{2,1,0:T(8,128)(2,1)S(1)}, bf16[8,8,256]{2,1,0:T(8,128)(2,1)S(1)}, u32[]{:S(2)}, u32[]{:S(2)}) collective-permute-start(bf16[8,8,256]{2,1,0:T(8,128)(2,1)S(1)} %get-tuple-element.90), channel_id=1, source_target_pairs={{0,4},{4,8},{8,12},{1,5},{5,9},{9,13},{2,6},{6,10},{10,14},{3,7},{... | collective-permute-start | bytes 98312 | tf_op jit(solution)/shard_map/ppermute | solution.py:611
  17.3 1.9 %collective-permute-start.3 = (bf16[8,8,256]{2,1,0:T(8,128)(2,1)S(1)}, bf16[8,8,256]{2,1,0:T(8,128)(2,1)S(1)}, u32[]{:S(2)}, u32[]{:S(2)}) collective-permute-start(bf16[8,8,256]{2,1,0:T(8,128)(2,1)S(1)} %get-tuple-element.91), channel_id=1, source_target_pairs={{4,0},{8,4},{12,8},{5,1},{9,5},{13,9},{6,2},{10,6},{14,10},{7,3},{... | collective-permute-start | bytes 98312 | tf_op jit(solution)/shard_map/ppermute | solution.py:611
  19.2 0.0 collective-permute-done.2
  19.2 4.8 %collective-permute-done.3 = bf16[8,8,256]{2,1,0:T(8,128)(2,1)S(1)} collective-permute-done((bf16[8,8,256]{2,1,0:T(8,128)(2,1)S(1)}, bf16[8,8,256]{2,1,0:T(8,128)(2,1)S(1)}, u32[]{:S(2)}, u32[]{:S(2)}) %collective-permute-start.3) | collective-permute-done | bytes 32800 | tf_op jit(solution)/shard_map/ppermute | solution.py:611
  24.0 0.9 pad_maximum_fusion.mid_ref
  24.9 1.3 %collective-permute-start.5 = (bf16[8,48,256]{2,1,0:T(8,128)(2,1)S(1)}, bf16[8,48,256]{2,1,0:T(8,128)(2,1)S(1)}, u32[]{:S(2)}, u32[]{:S(2)}) collective-permute-start(bf16[8,48,256]{2,1,0:T(8,128)(2,1)S(1)} %pad_maximum_fusion.mid_ref), channel_id=1, source_target_pairs={{16,0},{32,16},{48,32},{64,48},{80,64},{96,80},{112,96},{17,1},{33... | collective-permute-start | bytes 589832 | tf_op jit(solution)/shard_map/ppermute | solution.py:611
  26.2 4.0 %collective-permute-start.4 = (bf16[8,48,256]{2,1,0:T(8,128)(2,1)S(1)}, bf16[8,48,256]{2,1,0:T(8,128)(2,1)S(1)}, u32[]{:S(2)}, u32[]{:S(2)}) collective-permute-start(bf16[8,48,256]{2,1,0:T(8,128)(2,1)S(1)} %pad_maximum_fusion.mid_ref), channel_id=1, source_target_pairs={{0,16},{16,32},{32,48},{48,64},{64,80},{80,96},{96,112},{1,17},{17... | collective-permute-start | bytes 589832 | tf_op jit(solution)/shard_map/ppermute | solution.py:611
  30.2 1.3 %shard_map.158.w2_ref = bf16[2304,256]{1,0:T(8,128)(2,1)S(1)} custom-call(bf16[432,32]{1,0:T(8,128)(2,1)} %bitcast.7), custom_call_target="tpu_custom_call" | custom-call | tf_op jit(solution)/shard_map/pallas_call | solution.py:46
  31.5 3.2 %shard_map.157 = (bf16[3,8,48,256]{3,2,1,0:T(8,128)(2,1)S(1)}, bf16[3,8,48,256]{3,2,1,0:T(8,128)(2,1)}, f32[18,144,128]{2,1,0:T(8,128)}, f32[8,768]{1,0:T(8,128)S(1)}) custom-call(bf16[8,48,256]{2,1,0:T(8,128)(2,1)S(1)} %pad_maximum_fusion.mid_ref, bf16[768,768]{1,0:T(8,128)(2,1)S(1)} %get-tuple-element.51.w1_ref), custom_call_target="tpu_custom_call" | custom-call | tf_op jit(solution)/shard_map/pallas_call | solution.py:46
  34.8 1.0 shard_map.159.params_ref
  35.8 0.0 collective-permute-done.5.hi_ref
  35.8 0.0 copy-start
  35.8 0.0 collective-permute-done.4.lo_ref
  35.8 0.0 copy-start.1
  35.8 0.7 copy-done
  36.5 0.0 copy-done.1
  36.5 2.4 %shard_map.160 = (bf16[3,4,48,256]{3,2,1,0:T(8,128)(2,1)}, f32[18,48,128]{2,1,0:T(8,128)}, f32[128,1,128]{2,1,0:T(1,128)}) custom-call(bf16[8,48,256]{2,1,0:T(8,128)(2,1)} %copy-done.1, bf16[8,48,256]{2,1,0:T(8,128)(2,1)} %copy-done, bf16[3,8,48,256]{3,2,1,0:T(8,128)(2,1)S(1)} %get-tuple-element.58.mid_ref, f32[8,768]{1,0:T(8,128)S(1)} %get-tuple-element.59.sums_ref, ...), custom_call_target="tpu_custom_call" | custom-call | tf_op jit(solution)/shard_map/pallas_call | solution.py:46
  39.0 8.1 %all-to-all-start = ((f32[128,1,128]{2,1,0:T(1,128)}), f32[128,1,128]{2,1,0:T(1,128)S(1)}, u32[]{:S(2)}, u32[]{:S(2)}) async-start(f32[128,1,128]{2,1,0:T(1,128)} %get-tuple-element.64), calls=%async_computation | async-start | bytes 131072 | tf_op jit(solution)/shard_map/all_to_all | solution.py:634
  47.1 5.8 %shard_map.161.half_ref = f32[18,240,128]{2,1,0:T(8,128)S(1)} custom-call(bf16[8,48,256]{2,1,0:T(8,128)(2,1)} %copy-done.1, bf16[8,48,256]{2,1,0:T(8,128)(2,1)} %copy-done, bf16[3,4,48,256]{3,2,1,0:T(8,128)(2,1)} %get-tuple-element.60.ends_ref, f32[18,144,128]{2,1,0:T(8,128)} %get-tuple-element.61.half_mid_ref, ...), custom_call_target="tpu_custom_call" | custom-call | tf_op jit(solution)/shard_map/pallas_call | solution.py:46
  52.9 3.8 %all-to-all-done.stats_ref = f32[128,1,128]{2,1,0:T(1,128)S(1)} async-done(((f32[128,1,128]{2,1,0:T(1,128)}), f32[128,1,128]{2,1,0:T(1,128)S(1)}, u32[]{:S(2)}, u32[]{:S(2)}) %all-to-all-start) | async-done | bytes 65568 | tf_op jit(solution)/shard_map/all_to_all | solution.py:634
  56.6 2.8 %shard_map.162 = (bf16[10,24,1280]{2,1,0:T(8,128)(2,1)}, f32[576,256]{1,0:T(8,128)}, f32[128,1,128]{2,1,0:T(1,128)}) custom-call(f32[18,240,128]{2,1,0:T(8,128)S(1)} %shard_map.161.half_ref, f32[128,1,128]{2,1,0:T(1,128)S(1)} %all-to-all-done.stats_ref, f32[8,128]{1,0:T(8,128)S(1)} %shard_map.159.params_ref, bf16[2304,256]{1,0:T(8,128)(2,1)S(1)} %shard_map.158.w2_ref), custom_call_target="tpu_custom_call" | custom-call | tf_op jit(solution)/shard_map/pallas_call | solution.py:46
  59.4 6.0 %all-to-all-start.1 = ((f32[128,1,128]{2,1,0:T(1,128)}), f32[128,1,128]{2,1,0:T(1,128)S(1)}, u32[]{:S(2)}, u32[]{:S(2)}) async-start(f32[128,1,128]{2,1,0:T(1,128)} %get-tuple-element.74), calls=%async_computation.1 | async-start | bytes 131072 | tf_op jit(solution)/shard_map/all_to_all | solution.py:640
  65.4 3.7 %shard_map.163.half_ref = f32[18,48,128]{2,1,0:T(8,128)S(1)} custom-call(bf16[10,24,1280]{2,1,0:T(8,128)(2,1)} %get-tuple-element.72.p1_ref, bf16[2304,256]{1,0:T(8,128)(2,1)S(1)} %shard_map.158.w2_ref), custom_call_target="tpu_custom_call" | custom-call | tf_op jit(solution)/shard_map/pallas_call | solution.py:46
  69.1 1.4 %shard_map.164.w3_ref = bf16[2304,256]{1,0:T(8,128)(2,1)S(1)} custom-call(bf16[864,64]{1,0:T(8,128)(2,1)} %bitcast.6), custom_call_target="tpu_custom_call" | custom-call | tf_op jit(solution)/shard_map/pallas_call | solution.py:46
  70.5 4.5 %all-to-all-done.1.stats_ref = f32[128,1,128]{2,1,0:T(1,128)S(1)} async-done(((f32[128,1,128]{2,1,0:T(1,128)}), f32[128,1,128]{2,1,0:T(1,128)S(1)}, u32[]{:S(2)}, u32[]{:S(2)}) %all-to-all-start.1) | async-done | bytes 65568 | tf_op jit(solution)/shard_map/all_to_all | solution.py:640
  75.0 2.1 %shard_map.165 = (f32[128,256]{1,0:T(8,128)S(1)}, bf16[64,4,1152]{2,1,0:T(4,128)(2,1)}) custom-call(f32[18,48,128]{2,1,0:T(8,128)S(1)} %shard_map.163.half_ref, f32[128,1,128]{2,1,0:T(1,128)S(1)} %all-to-all-done.1.stats_ref, f32[8,128]{1,0:T(8,128)S(1)} %shard_map.159.params_ref, bf16[2304,256]{1,0:T(8,128)(2,1)S(1)} %shard_map.164.w3_ref), custom_call_target="tpu_custom_call" | custom-call | tf_op jit(solution)/shard_map/pallas_call | solution.py:46
  77.1 6.2 %all-to-all-start.2 = ((bf16[64,4,1152]{2,1,0:T(4,128)(2,1)}), bf16[64,4,1152]{2,1,0:T(4,128)(2,1)S(1)}, u32[]{:S(2)}, u32[]{:S(2)}) async-start(bf16[64,4,1152]{2,1,0:T(4,128)(2,1)} %get-tuple-element.82), calls=%async_computation.2 | async-start | bytes 1179648 | tf_op jit(solution)/shard_map/all_to_all | solution.py:647
  83.4 3.6 %shard_map.166 = bf16[8,32,2048]{2,1,0:T(8,128)(2,1)} custom-call(bf16[3,8,48,256]{3,2,1,0:T(8,128)(2,1)} %get-tuple-element.79.mid_ref, bf16[3,4,48,256]{3,2,1,0:T(8,128)(2,1)} %get-tuple-element.60.ends_ref, bf16[768,768]{1,0:T(8,128)(2,1)} %get-tuple-element.63.w1_far.w1_ref, f32[128,1,128]{2,1,0:T(1,128)S(1)} %all-to-all-done.stats_ref, ...), custom_call_target="tpu_custom_call" | custom-call | tf_op jit(solution)/shard_map/pallas_call | solution.py:46
  87.0 2.1 %shard_map.167 = bf16[4,16,2048]{2,1,0:T(8,128)(2,1)} custom-call(f32[576,256]{1,0:T(8,128)} %get-tuple-element.80.r2_ref, f32[128,1,128]{2,1,0:T(1,128)S(1)} %all-to-all-done.1.stats_ref, f32[8,128]{1,0:T(8,128)S(1)} %shard_map.159.params_ref), custom_call_target="tpu_custom_call" | custom-call | tf_op jit(solution)/shard_map/pallas_call | solution.py:46
  89.1 1.6 %shard_map.168.w4_ref = bf16[2304,256]{1,0:T(8,128)(2,1)S(1)} custom-call(bf16[1728,128]{1,0:T(8,128)(2,1)} %bitcast.5), custom_call_target="tpu_custom_call" | custom-call | tf_op jit(solution)/shard_map/pallas_call | solution.py:46
  90.8 5.3 %all-to-all-done.2.own_ref = bf16[64,4,1152]{2,1,0:T(4,128)(2,1)S(1)} async-done(((bf16[64,4,1152]{2,1,0:T(4,128)(2,1)}), bf16[64,4,1152]{2,1,0:T(4,128)(2,1)S(1)}, u32[]{:S(2)}, u32[]{:S(2)}) %all-to-all-start.2) | async-done | bytes 589856 | tf_op jit(solution)/shard_map/all_to_all | solution.py:647
  96.0 1.9 %collective-permute-start.6 = (bf16[64,4,1152]{2,1,0:T(4,128)(2,1)S(1)}, bf16[64,4,1152]{2,1,0:T(4,128)(2,1)S(1)}, u32[]{:S(2)}, u32[]{:S(2)}) collective-permute-start(bf16[64,4,1152]{2,1,0:T(4,128)(2,1)S(1)} %all-to-all-done.2.own_ref), channel_id=1, source_target_pairs={{0,4},{4,0},{1,5},{5,1},{2,6},{6,2},{3,7},{7,3},{8,12},{12,8},{9,1... | collective-permute-start | bytes 1769480 | tf_op jit(solution)/shard_map/ppermute | solution.py:652
  97.9 1.6 %collective-permute-done.6.other_ref = bf16[64,4,1152]{2,1,0:T(4,128)(2,1)S(1)} collective-permute-done((bf16[64,4,1152]{2,1,0:T(4,128)(2,1)S(1)}, bf16[64,4,1152]{2,1,0:T(4,128)(2,1)S(1)}, u32[]{:S(2)}, u32[]{:S(2)}) %collective-permute-start.6) | collective-permute-done | bytes 589856 | tf_op jit(solution)/shard_map/ppermute | solution.py:652
  99.6 9.4 %shard_map.169 = (bf16[2,8,2048]{2,1,0:T(8,128)(2,1)}, bf16[8,16,8192]{2,1,0:T(8,128)(2,1)}) custom-call(f32[128,256]{1,0:T(8,128)S(1)} %get-tuple-element.85.r3_ref, bf16[64,4,1152]{2,1,0:T(4,128)(2,1)S(1)} %all-to-all-done.2.own_ref, bf16[64,4,1152]{2,1,0:T(4,128)(2,1)S(1)} %collective-permute-done.6.other_ref, f32[8,128]{1,0:T(8,128)S(1)} %shard_map.159.params_ref, ...), custom_call_target="tpu_custom_call" | custom-call | tf_op jit(solution)/shard_map/pallas_call | solution.py:46
  (2 shorter events, 0.0 us)
Async XLA Ops:
  0.6 7.4 %collective-permute-start = (bf16[8,32,128]{2,1,0:T(8,128)(2,1)}, bf16[8,32,128]{2,1,0:T(8,128)(2,1)S(1)}, u32[]{:S(2)}, u32[]{:S(2)}) collective-permute-start(bf16[8,32,128]{2,1,0:T(8,128)(2,1)} %param.13), channel_id=1, source_target_pairs={{0,1},{1,2},{2,3},{4,5},{5,6},{6,7},{8,9},{9,10},{10,11},{12,13},{... | collective-permute-start | bytes 196616 | tf_op jit(solution)/shard_map/ppermute | solution.py:611
  4.7 5.2 %collective-permute-start.1 = (bf16[8,32,128]{2,1,0:T(8,128)(2,1)}, bf16[8,32,128]{2,1,0:T(8,128)(2,1)S(1)}, u32[]{:S(2)}, u32[]{:S(2)}) collective-permute-start(bf16[8,32,128]{2,1,0:T(8,128)(2,1)} %param.13), channel_id=1, source_target_pairs={{1,0},{2,1},{3,2},{5,4},{6,5},{7,6},{9,8},{10,9},{11,10},{13,12},{... | collective-permute-start | bytes 196616 | tf_op jit(solution)/shard_map/ppermute | solution.py:611
  10.7 8.6 %collective-permute-start.2 = (bf16[8,8,256]{2,1,0:T(8,128)(2,1)S(1)}, bf16[8,8,256]{2,1,0:T(8,128)(2,1)S(1)}, u32[]{:S(2)}, u32[]{:S(2)}) collective-permute-start(bf16[8,8,256]{2,1,0:T(8,128)(2,1)S(1)} %get-tuple-element.90), channel_id=1, source_target_pairs={{0,4},{4,8},{8,12},{1,5},{5,9},{9,13},{2,6},{6,10},{10,14},{3,7},{... | collective-permute-start | bytes 98312 | tf_op jit(solution)/shard_map/ppermute | solution.py:611
  17.3 6.7 %collective-permute-start.3 = (bf16[8,8,256]{2,1,0:T(8,128)(2,1)S(1)}, bf16[8,8,256]{2,1,0:T(8,128)(2,1)S(1)}, u32[]{:S(2)}, u32[]{:S(2)}) collective-permute-start(bf16[8,8,256]{2,1,0:T(8,128)(2,1)S(1)} %get-tuple-element.91), channel_id=1, source_target_pairs={{4,0},{8,4},{12,8},{5,1},{9,5},{13,9},{6,2},{10,6},{14,10},{7,3},{... | collective-permute-start | bytes 98312 | tf_op jit(solution)/shard_map/ppermute | solution.py:611
  24.9 10.9 %collective-permute-start.5 = (bf16[8,48,256]{2,1,0:T(8,128)(2,1)S(1)}, bf16[8,48,256]{2,1,0:T(8,128)(2,1)S(1)}, u32[]{:S(2)}, u32[]{:S(2)}) collective-permute-start(bf16[8,48,256]{2,1,0:T(8,128)(2,1)S(1)} %pad_maximum_fusion.mid_ref), channel_id=1, source_target_pairs={{16,0},{32,16},{48,32},{64,48},{80,64},{96,80},{112,96},{17,1},{33... | collective-permute-start | bytes 589832 | tf_op jit(solution)/shard_map/ppermute | solution.py:611
  26.2 9.6 %collective-permute-start.4 = (bf16[8,48,256]{2,1,0:T(8,128)(2,1)S(1)}, bf16[8,48,256]{2,1,0:T(8,128)(2,1)S(1)}, u32[]{:S(2)}, u32[]{:S(2)}) collective-permute-start(bf16[8,48,256]{2,1,0:T(8,128)(2,1)S(1)} %pad_maximum_fusion.mid_ref), channel_id=1, source_target_pairs={{0,16},{16,32},{32,48},{48,64},{64,80},{80,96},{96,112},{1,17},{17... | collective-permute-start | bytes 589832 | tf_op jit(solution)/shard_map/ppermute | solution.py:611
  35.8 0.7 copy-start
  35.8 0.7 copy-start.1
  39.0 17.7 %all-to-all-start = ((f32[128,1,128]{2,1,0:T(1,128)}), f32[128,1,128]{2,1,0:T(1,128)S(1)}, u32[]{:S(2)}, u32[]{:S(2)}) async-start(f32[128,1,128]{2,1,0:T(1,128)} %get-tuple-element.64), calls=%async_computation | async-start | bytes 131072 | tf_op jit(solution)/shard_map/all_to_all | solution.py:634
  59.4 15.6 %all-to-all-start.1 = ((f32[128,1,128]{2,1,0:T(1,128)}), f32[128,1,128]{2,1,0:T(1,128)S(1)}, u32[]{:S(2)}, u32[]{:S(2)}) async-start(f32[128,1,128]{2,1,0:T(1,128)} %get-tuple-element.74), calls=%async_computation.1 | async-start | bytes 131072 | tf_op jit(solution)/shard_map/all_to_all | solution.py:640
  77.1 18.9 %all-to-all-start.2 = ((bf16[64,4,1152]{2,1,0:T(4,128)(2,1)}), bf16[64,4,1152]{2,1,0:T(4,128)(2,1)S(1)}, u32[]{:S(2)}, u32[]{:S(2)}) async-start(bf16[64,4,1152]{2,1,0:T(4,128)(2,1)} %get-tuple-element.82), calls=%async_computation.2 | async-start | bytes 1179648 | tf_op jit(solution)/shard_map/all_to_all | solution.py:647
  96.0 3.5 %collective-permute-start.6 = (bf16[64,4,1152]{2,1,0:T(4,128)(2,1)S(1)}, bf16[64,4,1152]{2,1,0:T(4,128)(2,1)S(1)}, u32[]{:S(2)}, u32[]{:S(2)}) collective-permute-start(bf16[64,4,1152]{2,1,0:T(4,128)(2,1)S(1)} %all-to-all-done.2.own_ref), channel_id=1, source_target_pairs={{0,4},{4,0},{1,5},{5,1},{2,6},{6,2},{3,7},{7,3},{8,12},{12,8},{9,1... | collective-permute-start | bytes 1769480 | tf_op jit(solution)/shard_map/ppermute | solution.py:652

commit v3 on v2

--- a/solution.py
+++ b/solution.py
@@ -42,11 +42,11 @@
     return pltpu.with_memory_space_constraint(array, pltpu.HBM)
 
 
-def call(kernel, outs, ins, scratch=()):
+def call(kernel, outs, ins, scratch=(), out_specs=None):
     return pl.pallas_call(
         kernel,
         in_specs=[spec for _, spec in ins],
-        out_specs=tuple(VMEM for _ in outs),
+        out_specs=tuple(out_specs or [VMEM] * len(outs)),
         out_shape=tuple(outs),
         scratch_shapes=[s if not isinstance(s, tuple) else pltpu.VMEM(*s) for s in scratch],
         compiler_params=PARAMS,
@@ -58,7 +58,9 @@
     return gx, gh * 2 + gc, gz
 
 
-def first_band_kernel(k_ref, w_ref, far_ref):
+def first_band_kernel(k_ref, volume_far, w_ref, far_ref, volume_ref, sem):
+    own = pltpu.make_async_copy(volume_far, volume_ref, sem)
+    own.start()
     spread = (iota((16, 768), 1) % 16 == iota((16, 768), 0)).astype(BF16)
     taps = jnp.dot(k_ref[...], spread, preferred_element_type=F32)
     lag = iota((64, 768), 0) - iota((64, 768), 1) // 16
@@ -71,35 +73,17 @@
             w_ref[dx * 256 + dy * 64 : dx * 256 + dy * 64 + 64, :] = block.astype(BF16)
         w_ref[dx * 256 + 192 : dx * 256 + 256, :] = jnp.zeros((64, 768), BF16)
     far_ref[...] = w_ref[...]
-
-
-def first_band(k):
-    return call(first_band_kernel, [near((768, 768), BF16), far((768, 768), BF16)], [(k, VMEM)])
-
-
-def params_kernel(*refs):
-    ins, out_ref, local, sem = refs[:8], refs[8], refs[9:17], refs[17]
-    copies = [pltpu.make_async_copy(a, b, sem.at[i]) for i, (a, b) in enumerate(zip(ins, local))]
-    for c in copies:
-        c.start()
-    for c in copies:
-        c.wait()
+    own.wait()
+
+
+def fill_params(vectors, out_ref):
     lane = iota((1, 128), 1)
-    for i, ref in enumerate(local):
+    for i, ref in enumerate(vectors):
         count = ref.shape[0]
         row = jnp.zeros((1, 128), F32)
         for c in range(count):
             row = jnp.where(lane % count == c, ref[c], row)
         out_ref[i : i + 1, :] = row
-
-
-def params(*vectors):
-    return call(
-        params_kernel,
-        [near((8, 128), F32)],
-        [(held(v), ANY) for v in vectors],
-        [pltpu.SMEM(v.shape, F32) for v in vectors] + [pltpu.SemaphoreType.DMA((8,))],
-    )[0]
 
 
 def band_kernel(cin, cout, first, k_ref, w_ref, t_ref):
@@ -122,6 +106,40 @@
     lax.fori_loop(0, 9, plane, 0)
 
 
+def first_band(k, volume):
+    return call(
+        first_band_kernel,
+        [near((768, 768), BF16), far((768, 768), BF16), near(volume.shape, BF16)],
+        [(k.reshape(27, 16), VMEM), (held(volume), ANY)],
+        [pltpu.SemaphoreType.DMA(())],
+    )
+
+
+def early_kernel(*refs):
+    k2_far, vectors_far = refs[0], refs[1:9]
+    w2_ref, params_ref, k2_ref, t_ref = refs[9:13]
+    vectors, sems = refs[13:21], refs[21]
+    copies = [pltpu.make_async_copy(k2_far, k2_ref, sems.at[8])]
+    copies += [pltpu.make_async_copy(v, p, sems.at[i]) for i, (v, p) in enumerate(zip(vectors_far, vectors))]
+    for c in copies:
+        c.start()
+    for c in copies:
+        c.wait()
+    band_kernel(16, 32, 1, k2_ref, w2_ref, t_ref)
+    fill_params(vectors, params_ref)
+
+
+def early_part(k2, vectors):
+    return call(
+        early_kernel,
+        [near((2304, 256), BF16), near((8, 128), F32)],
+        [(held(k2.reshape(432, 32)), ANY)] + [(held(v), ANY) for v in vectors],
+        [((432, 32), BF16), ((432, 256), F32)]
+        + [pltpu.SMEM(v.shape, F32) for v in vectors]
+        + [pltpu.SemaphoreType.DMA((9,))],
+    )
+
+
 def band(k, first):
     cin, cout = k.shape[3:]
     return call(
@@ -186,8 +204,8 @@
     return r.reshape(n, rows, 768)
 
 
-def sums_1(r, q):
-    own = r[:, 8:40, :].reshape(-1, 768)
+def sums_1(own, q):
+    own = own.reshape(-1, 768)
     row1 = jnp.sum(own, axis=0, keepdims=True)
     row2 = jnp.sum(own * own, axis=0, keepdims=True)
     at = iota((1, 768), 1)
@@ -207,51 +225,105 @@
         half_ref[q * 6 + j] = paired_rows(rows, j, n * 24)
 
 
-def middle_kernel(mid_ref, w1_ref, lhs_ref, far_ref, half_ref, sums_ref, rows):
-    def step(i, carry):
+def widen_kernel(volume_ref, inner_ref, outer_ref, wide_ref, outer_face_ref):
+    odd = lax.axis_index("gz") % 2
+    volume, inner, outer = (ref[...].astype(F32) for ref in (volume_ref, inner_ref, outer_ref))
+    edge = jnp.where((iota((8, 32, 128), 2) < 64) == (odd == 0), inner, outer)
+    wide = jnp.concatenate([volume, edge], axis=2)
+    wide_ref[...] = wide.astype(BF16)
+    core = lax.axis_index("gc")
+    outer_face_ref[...] = jnp.where(core == 0, wide[:, 0:8], wide[:, 24:32]).astype(BF16)
+
+
+def widen(volume, inner, outer):
+    return call(
+        widen_kernel,
+        [near((8, 32, 256), BF16), near((8, 8, 256), BF16)],
+        [(volume, VMEM), (inner, VMEM), (outer, VMEM)],
+    )
+
+
+def inner_face_kernel(wide_ref, face_ref):
+    wide = wide_ref[...].astype(F32)
+    face_ref[...] = jnp.where(lax.axis_index("gc") == 0, wide[:, 24:32], wide[:, 0:8]).astype(BF16)
+
+
+def inner_face(wide):
+    return call(inner_face_kernel, [near((8, 8, 256), BF16)], [(wide, VMEM)])[0]
+
+
+def assemble_kernel(wide_ref, inner_ref, outer_ref, mid_ref, packed_ref):
+    core = lax.axis_index("gc")
+    inner, outer = inner_ref[...].astype(F32), outer_ref[...].astype(F32)
+    low = jnp.where(core == 0, outer, inner)
+    high = jnp.where(core == 0, inner, outer)
+    mid = jnp.concatenate([low, wide_ref[...].astype(F32), high], axis=1)
+    mid_ref[...] = mid.astype(BF16)
+    packed_ref[0:8] = mid[:, :, 0:128].astype(BF16)
+    slot = (iota((48, 128), 1) + 8) % 128 // 16
+    ends = mid[0, :, 128:256]
+    for i in range(1, 8):
+        ends = jnp.where(slot == i, pltpu.roll(mid[i, :, 128:256], 16 * i, 1), ends)
+    packed_ref[8] = ends.astype(BF16)
+
+
+def assemble(wide, inner, outer):
+    return call(
+        assemble_kernel,
+        [near((8, 48, 256), BF16), near((9, 48, 128), BF16)],
+        [(wide, VMEM), (inner, VMEM), (outer, VMEM)],
+    )
+
+
+def plane(own, ends, i):
+    ends = ends.astype(F32)
+    if i:
+        ends = pltpu.roll(ends, 128 - 16 * i, 1)
+    return jnp.concatenate([own.astype(F32), ends], axis=1)
+
+
+def middle_kernel(mid_ref, w1_ref, lhs_ref, far_ref, sums_ref):
+    for i in range(8):
         fill(lhs_ref, i, mid_ref[i].astype(F32))
-        return carry
-
-    lax.fori_loop(0, 8, step, 0, unroll=4)
+    far_ref[...] = lhs_ref[...]
     s1 = jnp.zeros((1, 768), F32)
     s2 = jnp.zeros((1, 768), F32)
     for q in range(3):
-        r = response_1([lhs_ref[q, dx : 6 + dx] for dx in range(3)], w1_ref)
+        r = response_1([lhs_ref[q, dx : 6 + dx][:, 8:40] for dx in range(3)], w1_ref)
         row1, row2 = sums_1(r, q)
         s1, s2 = s1 + row1, s2 + row2
-        halve_rows(r, rows, half_ref, q)
     sums_ref[0:1, :] = s1
     sums_ref[1:2, :] = s2
-    far_ref[...] = lhs_ref[...]
 
 
 def middle_part(mid, w1):
     return call(
         middle_kernel,
-        [near((3, 8, 48, 256), BF16), far((3, 8, 48, 256), BF16), far((18, 144, 128), F32), near((8, 768), F32)],
+        [near((3, 8, 48, 256), BF16), far((3, 8, 48, 256), BF16), near((8, 768), F32)],
         [(mid, VMEM), (w1, VMEM)],
-        [((6, 288, 128), F32)],
-    )
-
-
-def first_kernel(lo_ref, hi_ref, mid_ref, sums_ref, w1_ref, ends_ref, half_ref, stats_ref, rows, lo, hi, sems):
-    copies = [
-        pltpu.make_async_copy(lo_ref.at[7], lo, sems.at[0]),
-        pltpu.make_async_copy(hi_ref.at[0], hi, sems.at[1]),
-    ]
-    for c in copies:
-        c.start()
-    ends_ref[:, 1:2] = mid_ref[:, 0:1]
-    ends_ref[:, 2:3] = mid_ref[:, 7:8]
-    for c in copies:
-        c.wait()
-    fill(ends_ref, 0, lo[...].astype(F32))
-    fill(ends_ref, 3, hi[...].astype(F32))
+    )
+
+
+def first_kernel(inner_ref, outer_ref, mid_ref, sums_ref, w1_ref, ends_ref, sides_ref, stats_ref):
+    even = lax.axis_index("gx") % 2 == 0
+
+    @pl.when(even)
+    def _():
+        sides_ref[0] = outer_ref[...]
+        sides_ref[1] = inner_ref[...]
+
+    @pl.when(jnp.logical_not(even))
+    def _():
+        sides_ref[0] = inner_ref[...]
+        sides_ref[1] = outer_ref[...]
+
+    fill(ends_ref, 0, plane(sides_ref[0, 7], sides_ref[0, 8], 7))
+    fill(ends_ref, 1, plane(sides_ref[1, 0], sides_ref[1, 8], 0))
     planes = []
     for q in range(3):
         a = [ends_ref[q, 0:1], mid_ref[q, 0:1], mid_ref[q, 1:2]]
-        b = [mid_ref[q, 6:7], mid_ref[q, 7:8], ends_ref[q, 3:4]]
-        planes.append([jnp.concatenate([a[dx], b[dx]], axis=0) for dx in range(3)])
+        b = [mid_ref[q, 6:7], mid_ref[q, 7:8], ends_ref[q, 1:2]]
+        planes.append([jnp.concatenate([a[dx], b[dx]], axis=0)[:, 8:40] for dx in range(3)])
     r = response_1([jnp.concatenate([planes[q][dx] for q in range(3)], axis=0) for dx in range(3)], w1_ref)
     s1 = sums_ref[0:1, :]
     s2 = sums_ref[1:2, :]
@@ -259,60 +331,44 @@
         row1, row2 = sums_1(r[2 * q : 2 * q + 2], q)
         s1, s2 = s1 + row1, s2 + row2
     stats_ref[...] = slots(pack_stats(s1, s2, 16))
+
+
+def first_part(inner, outer, lhs_mid, sums, w1):
+    return call(
+        first_kernel,
+        [far((3, 2, 48, 256), BF16), far((2, 9, 48, 128), BF16), far((DEVICES, 1, 128), F32)],
+        [(inner, VMEM), (outer, VMEM), (lhs_mid, VMEM), (sums, VMEM), (w1, VMEM)],
+    )
+
+
+def wide_first_kernel(sides_ref, mid_far, ends_far, w1_far, half_ref, lhs, rows, w1_ref, sems):
+    copies = [pltpu.make_async_copy(w1_far, w1_ref, sems.at[0])]
     for q in range(3):
-        halve_rows(r[2 * q : 2 * q + 2], rows, half_ref, q)
-
-
-def first_part(lo, hi, lhs_mid, sums, w1):
-    return call(
-        first_kernel,
-        [far((3, 4, 48, 256), BF16), far((18, 48, 128), F32), far((DEVICES, 1, 128), F32)],
-        [(held(lo), ANY), (held(hi), ANY), (lhs_mid, VMEM), (sums, VMEM), (w1, VMEM)],
-        [((6, 96, 128), F32), ((48, 256), BF16), ((48, 256), BF16), pltpu.SemaphoreType.DMA((2,))],
-    )
-
-
-def wide_first_kernel(
-    lo_ref, hi_ref, ends_ref, half_mid_ref, half_edge_ref, w1_far, half_ref, lhs, rows, wide, w1_ref, sem
-):
-    weights = pltpu.make_async_copy(w1_far, w1_ref, sem)
-    weights.start()
-
-    def step(i, carry):
-        fill(lhs, i, lo_ref[1 + i].astype(F32))
-        fill(lhs, 10 + i, hi_ref[1 + i].astype(F32))
-        return carry
-
-    lax.fori_loop(0, 6, step, 0, unroll=2)
-    lhs[:, 6:10] = ends_ref[...]
-    weights.wait()
+        copies.append(pltpu.make_async_copy(mid_far.at[q], lhs.at[q, 7:15], sems.at[3 * q + 1]))
+        copies.append(pltpu.make_async_copy(ends_far.at[q, 0], lhs.at[q, 6], sems.at[3 * q + 2]))
+        copies.append(pltpu.make_async_copy(ends_far.at[q, 1], lhs.at[q, 15], sems.at[3 * q + 3]))
+    for c in copies:
+        c.start()
+    for i in range(6):
+        fill(lhs, i, plane(sides_ref[0, 1 + i], sides_ref[0, 8], 1 + i))
+        fill(lhs, 16 + i, plane(sides_ref[1, 1 + i], sides_ref[1, 8], 1 + i))
+    for c in copies:
+        c.wait()
     for q in range(3):
-        planes = [jnp.concatenate([lhs[q, dx : 6 + dx], lhs[q, 8 + dx : 14 + dx]], axis=0) for dx in range(3)]
-        halve_rows(response_1(planes, w1_ref), rows, wide, q)
-
-    def merge(j, carry):
-        outer = wide[j].reshape(6, 2, 24, 128)
-        inner = half_mid_ref[j].reshape(6, 24, 128)
-        edges = half_edge_ref[j].reshape(2, 24, 128)
-        outer = jnp.maximum(outer[:, 0], outer[:, 1])
-        half_ref[j, 0:72] = outer[0:3].reshape(72, 128)
-        half_ref[j, 72:96] = jnp.maximum(edges[0], inner[0])
-        half_ref[j, 96:120] = jnp.maximum(inner[1], inner[2])
-        half_ref[j, 120:144] = jnp.maximum(inner[3], inner[4])
-        half_ref[j, 144:168] = jnp.maximum(inner[5], edges[1])
-        half_ref[j, 168:240] = outer[3:6].reshape(72, 128)
-        return carry
-
-    lax.fori_loop(0, 18, merge, 0)
-
-
-def wide_first_part(lo, hi, ends, half_mid, half_edge, w1):
+        r = response_1([lhs[q, dx : 20 + dx] for dx in range(3)], w1_ref)
+        r = jnp.max(r.reshape(10, 2, 48, 768), axis=1).reshape(480, 768)
+        for j in range(6):
+            rows[j] = r[:, j * 128 : (j + 1) * 128]
+        for j in range(6):
+            half_ref[q * 6 + j] = paired_rows(rows, j, 240)
+
+
+def wide_first_part(sides, lhs_mid, ends, w1):
     return call(
         wide_first_kernel,
         [near((18, 240, 128), F32)],
-        [(held(a), VMEM) for a in (lo, hi, ends, half_mid, half_edge)] + [(held(w1), ANY)],
-        [((3, 16, 48, 256), BF16), ((6, 576, 128), F32), ((18, 288, 128), F32), ((768, 768), BF16)]
-        + [pltpu.SemaphoreType.DMA(())],
+        [(held(sides), VMEM)] + [(held(a), ANY) for a in (lhs_mid, ends, w1)],
+        [((3, 22, 48, 256), BF16), ((6, 480, 128), F32), ((768, 768), BF16), pltpu.SemaphoreType.DMA((10,))],
     )[0]
 
 
@@ -323,7 +379,7 @@
         planes = [
             jnp.concatenate([ends_ref[q, 0:1], middle[0:7]], axis=0),
             middle,
-            jnp.concatenate([middle[1:8], ends_ref[q, 3:4]], axis=0),
+            jnp.concatenate([middle[1:8], ends_ref[q, 1:2]], axis=0),
         ]
         f = settle(response_1([p[:, 8:40, :] for p in planes], w1_ref), normal)
         a, b = (128 if q == 0 else 0), (640 if q == 2 else 768)
@@ -349,7 +405,7 @@
     return jnp.maximum(both[:, 0:128], both[:, 128:256])
 
 
-def second_kernel(half_ref, stats_ref, params_ref, w2_ref, p1_ref, r2_ref, out_stats_ref, p1, pd):
+def second_kernel(half_ref, stats_ref, params_ref, w2_ref, p1_far, out_stats_ref, p1, p1_ref, pd, sem):
     normal = normaliser(jnp.sum(stats_ref[...], axis=0), VOXELS_1, params_ref, 0, 1)
     pick = selector(16)
     bx, by, bz = position()
@@ -364,13 +420,14 @@
     for dy in range(3):
         pd[dy] = p1[2:8, 3 + dy : 19 + dy, :].astype(BF16)
     p1_ref[...] = p1[...].astype(BF16)
+    save = pltpu.make_async_copy(p1_ref, p1_far, sem)
+    save.start()
     planes = []
     for dx in range(3):
         for dy in range(3):
             pieces = [pd[dy, dx : dx + 4, :, 128 * t : 128 * t + 256].reshape(64, 256) for t in range(9)]
             planes.append(jnp.concatenate(pieces, axis=0))
     r = jnp.dot(jnp.concatenate(planes, axis=1), w2_ref[...], preferred_element_type=F32)
-    r2_ref[...] = r
     s1 = jnp.zeros((1, 256), F32)
     s2 = jnp.zeros((1, 256), F32)
     lane = iota((1, 256), 1)
@@ -384,18 +441,23 @@
             row1, row2 = (jnp.where(lane < 64, r_, 0.0) for r_ in (row1, row2))
         s1, s2 = s1 + row1, s2 + row2
     out_stats_ref[...] = slots(pack_stats(s1, s2, 32))
+    save.wait()
 
 
 def second_part(half, stats, table, w2):
     return call(
         second_kernel,
-        [far((10, 24, 1280), BF16), far((576, 256), F32), far((DEVICES, 1, 128), F32)],
+        [far((10, 24, 1280), BF16), far((DEVICES, 1, 128), F32)],
         [(a, VMEM) for a in (half, stats, table, w2)],
-        [((10, 24, 1280), F32), ((3, 6, 16, 1280), BF16)],
-    )
-
-
-def wide_second_kernel(p1_ref, w2_ref, half_ref, pd, rows):
+        [((10, 24, 1280), F32), ((10, 24, 1280), BF16), ((3, 6, 16, 1280), BF16), pltpu.SemaphoreType.DMA(())],
+        [ANY, VMEM],
+    )
+
+
+def wide_second_kernel(p1_ref, w2_ref, k3_far, half_ref, r2_ref, w3_ref, pd, rows, k3_ref, t_ref, sem):
+    kernel = pltpu.make_async_copy(k3_far, k3_ref, sem)
+    kernel.start()
+
     def shift(i, carry):
         v = p1_ref[i].astype(F32)
         pd[0, i] = pltpu.roll(v, 1, 0)
@@ -411,21 +473,26 @@
                 pieces = [pd[dy, dx : dx + 8, :, 128 * u : 128 * u + 256].reshape(192, 256) for u in range(t, t + 3)]
                 planes.append(jnp.concatenate(pieces, axis=0).astype(BF16))
         r = jnp.dot(jnp.concatenate(planes, axis=1), w2_ref[...], preferred_element_type=F32)
+        own = r.reshape(3, 8, 24, 256)[:, 2:6, 4:20]
+        r2_ref[64 * t : 64 * t + 192, :] = own.reshape(192, 256)
         r = jnp.max(r.reshape(3, 4, 2, 24, 256), axis=2).reshape(3, 96, 256)
         for i in range(3):
             for j in range(2):
                 rows[2 * i + j] = r[i, :, j * 128 : (j + 1) * 128]
         for j in range(6):
             half_ref[2 * t + j] = paired_rows(rows, j, 48)
-
-
-def wide_second_part(p1, w2):
+    kernel.wait()
+    band_kernel(32, 64, 0, k3_ref, w3_ref, t_ref)
+
+
+def wide_second_part(p1, w2, k3):
     return call(
         wide_second_kernel,
-        [near((18, 48, 128), F32)],
-        [(held(p1), VMEM), (w2, VMEM)],
-        [((3, 10, 24, 1280), F32), ((6, 96, 128), F32)],
-    )[0]
+        [near((18, 48, 128), F32), far((576, 256), F32), near((2304, 256), BF16)],
+        [(held(p1), VMEM), (w2, VMEM), (held(k3.reshape(864, 64)), ANY)],
+        [((3, 10, 24, 1280), F32), ((6, 96, 128), F32), ((864, 64), BF16), ((864, 256), F32)]
+        + [pltpu.SemaphoreType.DMA(())],
+    )
 
 
 def second_output_kernel(r2_ref, stats_ref, params_ref, f2_ref):
@@ -507,7 +574,7 @@
     )
 
 
-def fourth_kernel(r3_ref, own_ref, other_ref, params_ref, w4_ref, f3_ref, out_ref, p3, pd, r4):
+def fourth_kernel(r3_ref, own_ref, other_ref, params_ref, w4_ref, f3_ref, out_far, p3, pd, r4, out_ref, sems):
     edge = jnp.zeros((4, 128), F32)
     tail = jnp.zeros((4, 128), F32)
     for ref in (own_ref, other_ref):
@@ -566,49 +633,50 @@
     def _():
         place(other_ref, own_ref)
 
-    def tiles(i, carry):
-        s1, s2 = carry
+    s1 = jnp.zeros((1, 256), F32)
+    s2 = jnp.zeros((1, 256), F32)
+    for i in range(0, 32, 8):
         planes = []
         for dx in range(3):
             for dy in range(3):
                 pieces = [
-                    pd[dy, dx : dx + 8, :, pl.ds(pl.multiple_of(128 * (i * 8 + g), 128), 256)].reshape(128, 256)
-                    for g in range(8)
+                    pd[dy, dx : dx + 8, :, 128 * t : 128 * t + 256].reshape(128, 256) for t in range(i, i + 8)
                 ]
                 planes.append(jnp.concatenate(pieces, axis=0))
         r = jnp.dot(jnp.concatenate(planes, axis=1), w4_ref[...], preferred_element_type=F32)
-        r4[pl.ds(pl.multiple_of(i * 1024, 1024), 1024), :] = r
-        return s1 + jnp.sum(r, axis=0, keepdims=True), s2 + jnp.sum(r * r, axis=0, keepdims=True)
-
-    zeros = jnp.zeros((1, 256), F32)
-    s1, s2 = lax.fori_loop(0, 4, tiles, (zeros, zeros))
+        r4[i * 128 : i * 128 + 1024, :] = r
+        s1, s2 = s1 + jnp.sum(r, axis=0, keepdims=True), s2 + jnp.sum(r * r, axis=0, keepdims=True)
     cells = VOXELS_1 / 512
     mean = fold(s1, 128) / cells
     variance = fold(s2, 128) / cells - mean * mean
     factor = params_ref[6:7, :] * lax.rsqrt(variance + EPSILON)
     last = tuple(jnp.concatenate([v] * 2, axis=1) for v in (mean, factor, params_ref[7:8, :]))
 
-    def finish(t, carry):
-        f = settle(r4[pl.ds(pl.multiple_of(t * 128, 128), 128), :], last).astype(BF16)
-        out_ref[:, :, pl.ds(pl.multiple_of(256 * t, 256), 256)] = f.reshape(8, 16, 256)
-        return carry
-
-    lax.fori_loop(0, 32, finish, 0)
+    copies = []
+    for i in range(4):
+        for t in range(8 * i, 8 * i + 8):
+            f = settle(r4[t * 128 : t * 128 + 128, :], last).astype(BF16)
+            out_ref[:, :, 256 * t : 256 * t + 256] = f.reshape(8, 16, 256)
+        lanes = pl.ds(2048 * i, 2048)
+        copies.append(pltpu.make_async_copy(out_ref.at[:, :, lanes], out_far.at[:, :, lanes], sems.at[i]))
+        copies[i].start()
+    for c in copies:
+        c.wait()
 
 
 def fourth_part(r3, own, other, table, w4):
     return call(
         fourth_kernel,
-        [full((2, 8, 2048), BF16), full((8, 16, 8192), BF16)],
+        [full((2, 8, 2048), BF16), far((8, 16, 8192), BF16)],
         [(a, VMEM) for a in (r3, own, other, table, w4)],
-        [((16, 4224), F32), ((3, 10, 16, 4224), BF16), ((4096, 256), F32)],
-    )
-
-
-def neighbours(low_face, high_face, axis, count):
-    up = [(i, i + 1) for i in range(count - 1)]
-    down = [(i + 1, i) for i in range(count - 1)]
-    return lax.ppermute(high_face, axis, up), lax.ppermute(low_face, axis, down)
+        [((16, 4224), F32), ((3, 10, 16, 4224), BF16), ((4096, 256), F32), ((8, 16, 8192), BF16)]
+        + [pltpu.SemaphoreType.DMA((4,))],
+        [VMEM, ANY],
+    )
+
+
+def across(block, axis, swaps):
+    return lax.ppermute(block, axis, swaps + [(b, a) for a, b in swaps])
 
 
 def after(values, event):
@@ -616,30 +684,30 @@
 
 
 def shards(volume, k1, g1, b1, k2, g2, b2, k3, g3, b3, k4, g4, b4):
-    low, high = neighbours(volume, volume, "gz", 4)
-    w1, w1_far = first_band(k1.reshape(27, 16))
-    (low, high, w1) = lax.optimization_barrier((low, high, w1))
-    edge = jnp.where(lax.broadcasted_iota(jnp.int32, volume.shape, 2) < 64, high, low)
-    wide = jnp.concatenate([volume, edge], axis=2)
-    low, high = neighbours(wide[:, 0:8, :], wide[:, 24:32, :], ("gh", "gc"), 4)
-    mid = jnp.concatenate([low, wide, high], axis=1)
-    (mid, k2, g1) = lax.optimization_barrier((mid, k2, g1))
-    low, high = neighbours(mid, mid, "gx", 8)
-    lhs_mid, far_mid, half_mid, sums = middle_part(mid, w1)
-    w2 = band(k2, 1)
-    table = params(g1, b1, g2, b2, g3, b3, g4, b4)
-    (low, high, lhs_mid, w2, table) = lax.optimization_barrier((low, high, lhs_mid, w2, table))
-    ends, half_edge, stats = first_part(low, high, lhs_mid, sums, w1)
+    outer = across(volume, "gz", [(1, 2)])
+    inner = across(volume, "gz", [(0, 1), (2, 3)])
+    w1, w1_far, block = first_band(k1, volume)
+    (inner, outer, w1) = lax.optimization_barrier((inner, outer, w1))
+    wide, outer = widen(block, inner, outer)
+    outer = across(outer, ("gh", "gc"), [(1, 2)])
+    inner = across(inner_face(wide), "gc", [(0, 1)])
+    mid, packed = assemble(wide, inner, outer)
+    (packed, k2) = lax.optimization_barrier((packed, k2))
+    inner = across(packed, "gx", [(0, 1), (2, 3), (4, 5), (6, 7)])
+    outer = across(packed, "gx", [(1, 2), (3, 4), (5, 6)])
+    w2, table = early_part(k2, (g1, b1, g2, b2, g3, b3, g4, b4))
+    lhs_mid, far_mid, sums = middle_part(mid, w1)
+    (inner, outer, lhs_mid, w2) = lax.optimization_barrier((inner, outer, lhs_mid, w2))
+    ends, sides, stats = first_part(inner, outer, lhs_mid, sums, w1)
 
     total1 = lax.all_to_all(stats, AXES, 0, 0, tiled=True)
-    half1 = wide_first_part(low, high, ends, half_mid, half_edge, w1_far)
+    half1 = wide_first_part(sides, far_mid, ends, w1_far)
     half1, total1 = after(half1, total1)
-    p1, r2, stats = second_part(half1, total1, table, w2)
-
-    (p1, k3), stats = after((p1, k3), stats)
+    p1, stats = second_part(half1, total1, table, w2)
+
+    p1, stats = after(p1, stats)
     total2 = lax.all_to_all(stats, AXES, 0, 0, tiled=True)
-    half2 = wide_second_part(p1, w2)
-    w3 = band(k3, 0)
+    half2, r2, w3 = wide_second_part(p1, w2, k3)
     (half2, w3), total2 = after((half2, w3), total2)
     r3, packed = third_part(half2, total2, table, w3)
 

time: 110 us -> 100 us (0.909)
  waiting for transfers between devices: 21.8 us -> 16 us
  other arithmetic: 1.63 us -> 0 us
  Pallas kernels: 41.8 us -> 40.6 us
    ppermute x6, waiting for transfers between devices: 6.65 us -> 2.17 us  [across(): return lax.ppermute(block, axis, swaps + [(b, a) for a, b in swaps])]
    ppermute x6, starting transfers between devices: 19.2 us -> 16.1 us  [across(): return lax.ppermute(block, axis, swaps + [(b, a) for a, b in swaps])]
    all_to_all x1, starting transfers between devices: 8.11 us -> 9.54 us  [shards(): total1 = lax.all_to_all(stats, AXES, 0, 0, tiled=True)]
    all_to_all x1, starting transfers between devices: 6.01 us -> 7.38 us  [shards(): total2 = lax.all_to_all(stats, AXES, 0, 0, tiled=True)]
    all_to_all x1, waiting for transfers between devices: 3.76 us -> 2.41 us  [shards(): total1 = lax.all_to_all(stats, AXES, 0, 0, tiled=True)]
    pallas_call x14 -> x15, Pallas kernels: 41.8 us -> 40.6 us  [call(): pl.pallas_call(kernel, in_specs=[spec for _, spec in ins], out_specs=tupl...]
  transfers between devices with their start and end apart: 10 -> 10, of which waited for: 6 -> 5; matrix products, arithmetic and copies ran while one was open for 1% -> 1% of each run, Pallas kernels for 23% -> 25%
where the time goes in v3:
time: 100 us; the launch traced here: 99.3 us
  starting transfers between devices  41.1 us (41%)
  Pallas kernels  40.6 us (41%)
  waiting for transfers between devices  16 us (16%)
    pallas_call x15, Pallas kernels, call(): pl.pallas_call(kernel, in_specs=[spec for _, spec in ins], out_specs=tupl...  40.6 us
    ppermute x6, starting transfers between devices, across(): return lax.ppermute(block, axis, swaps + [(b, a) for a, b in swaps])  16.1 us
    all_to_all x1, starting transfers between devices, shards(): total1 = lax.all_to_all(stats, AXES, 0, 0, tiled=True)  9.54 us
    all_to_all x1, starting transfers between devices, shards(): total2 = lax.all_to_all(stats, AXES, 0, 0, tiled=True)  7.38 us
    all_to_all x1, starting transfers between devices, shards(): own = lax.all_to_all(packed, CHIPS, 0, 0, tiled=True)  6.18 us
    all_to_all x1, waiting for transfers between devices, shards(): own = lax.all_to_all(packed, CHIPS, 0, 0, tiled=True)  5.46 us
    all_to_all x1, waiting for transfers between devices, shards(): total2 = lax.all_to_all(stats, AXES, 0, 0, tiled=True)  4.38 us
    all_to_all x1, waiting for transfers between devices, shards(): total1 = lax.all_to_all(stats, AXES, 0, 0, tiled=True)  2.41 us
  transfers between devices with their start and end apart: 10, of which 5 were waited for; matrix products, arithmetic and copies ran while one was open for 1% of the time, Pallas kernels for 25%

profile of v3, /device:TPU:1, one launch (start us, length us, event | category | flops | bytes accessed | tf_op | source)
XLA Modules:
  0.0 99.3 jit_solution(1727342529717673442)
XLA Ops:
  0.6 0.7 collective-permute-start.1
  1.3 4.7 %collective-permute-start = (bf16[8,32,128]{2,1,0:T(8,128)(2,1)}, bf16[8,32,128]{2,1,0:T(8,128)(2,1)S(1)}, u32[]{:S(2)}, u32[]{:S(2)}) collective-permute-start(bf16[8,32,128]{2,1,0:T(8,128)(2,1)} %volume_far.1), channel_id=1, source_target_pairs={{0,1},{2,3},{1,0},{3,2},{4,5},{6,7},{5,4},{7,6},{8,9},{10,11},{9,8... | collective-permute-start | bytes 196616 | tf_op jit(solution)/shard_map/ppermute | solution.py:679
  6.1 0.7 reshape.20.k_ref
  6.8 1.9 %shard_map.156 = (bf16[768,768]{1,0:T(8,128)(2,1)S(1)}, bf16[768,768]{1,0:T(8,128)(2,1)}, bf16[8,32,128]{2,1,0:T(8,128)(2,1)S(1)}) custom-call(bf16[27,16]{1,0:T(8,128)(2,1)S(1)} %reshape.20.k_ref, bf16[8,32,128]{2,1,0:T(8,128)(2,1)} %volume_far.1), custom_call_target="tpu_custom_call" | custom-call | tf_op jit(solution)/shard_map/pallas_call | solution.py:46
  8.7 0.0 collective-permute-done.1.outer_ref
  8.7 0.0 collective-permute-done.inner_ref
  8.8 1.3 %collective-permute-start.2 = (bf16[8,8,256]{2,1,0:T(8,128)(2,1)S(1)}, bf16[8,8,256]{2,1,0:T(8,128)(2,1)S(1)}, u32[]{:S(2)}, u32[]{:S(2)}) collective-permute-start(bf16[8,8,256]{2,1,0:T(8,128)(2,1)S(1)} %shard_map.158), channel_id=1, source_target_pairs={{0,4},{4,0},{1,5},{5,1},{2,6},{6,2},{3,7},{7,3},{8,12},{12,8},{9,1... | collective-permute-start | bytes 98312 | tf_op jit(solution)/shard_map/ppermute | solution.py:679
  10.1 4.6 %collective-permute-start.3 = (bf16[8,8,256]{2,1,0:T(8,128)(2,1)S(1)}, bf16[8,8,256]{2,1,0:T(8,128)(2,1)S(1)}, u32[]{:S(2)}, u32[]{:S(2)}) collective-permute-start(bf16[8,8,256]{2,1,0:T(8,128)(2,1)S(1)} %get-tuple-element.55), channel_id=1, source_target_pairs={{4,8},{8,4},{5,9},{9,5},{6,10},{10,6},{7,11},{11,7},{20,24},{24,20... | collective-permute-start | bytes 98312 | tf_op jit(solution)/shard_map/ppermute | solution.py:679
  14.6 0.0 collective-permute-done.2.inner_ref
  14.7 2.2 %collective-permute-done.3.outer_ref = bf16[8,8,256]{2,1,0:T(8,128)(2,1)S(1)} collective-permute-done((bf16[8,8,256]{2,1,0:T(8,128)(2,1)S(1)}, bf16[8,8,256]{2,1,0:T(8,128)(2,1)S(1)}, u32[]{:S(2)}, u32[]{:S(2)}) %collective-permute-start.3) | collective-permute-done | bytes 32800 | tf_op jit(solution)/shard_map/ppermute | solution.py:679
  16.8 0.1 shard_map.159
  16.9 0.7 collective-permute-start.5
  17.6 4.1 %collective-permute-start.4 = (bf16[9,48,128]{2,1,0:T(8,128)(2,1)S(1)}, bf16[9,48,128]{2,1,0:T(8,128)(2,1)S(1)}, u32[]{:S(2)}, u32[]{:S(2)}) collective-permute-start(bf16[9,48,128]{2,1,0:T(8,128)(2,1)S(1)} %get-tuple-element.60), channel_id=1, source_target_pairs={{0,16},{32,48},{64,80},{96,112},{16,0},{48,32},{80,64},{112,96},{1... | collective-permute-start | bytes 331784 | tf_op jit(solution)/shard_map/ppermute | solution.py:679
  21.7 2.0 %shard_map.160 = (bf16[3,8,48,256]{3,2,1,0:T(8,128)(2,1)S(1)}, bf16[3,8,48,256]{3,2,1,0:T(8,128)(2,1)}, f32[8,768]{1,0:T(8,128)S(1)}) custom-call(bf16[8,48,256]{2,1,0:T(8,128)(2,1)S(1)} %get-tuple-element.56.mid_ref, bf16[768,768]{1,0:T(8,128)(2,1)S(1)} %get-tuple-element.57.w1_ref), custom_call_target="tpu_custom_call" | custom-call | tf_op jit(solution)/shard_map/pallas_call | solution.py:46
  23.7 1.7 %shard_map.161 = (bf16[2304,256]{1,0:T(8,128)(2,1)S(1)}, f32[8,128]{1,0:T(8,128)S(1)}) custom-call(bf16[432,32]{1,0:T(8,128)(2,1)} %bitcast.7, f32[16]{0:T(128)} %refs_1_.1, f32[16]{0:T(128)} %refs_2_.1, f32[32]{0:T(128)} %refs_3_.1, f32[32]{0:T(128)} %refs_4_.1, f32[64]{0:T(128)} %refs_5_.1, f32[64]{0:T(128)} %refs_6_.1, f32[128]{0:T(128)} %refs_7_.1, ...), custom_call_target="tpu_custom_call" | custom-call | tf_op jit(solution)/shard_map/pallas_call | solution.py:46
  25.4 0.0 collective-permute-done.5.outer_ref
  25.4 0.0 collective-permute-done.4.inner_ref
  25.4 1.6 %shard_map.162 = (bf16[3,2,48,256]{3,2,1,0:T(8,128)(2,1)}, bf16[2,9,48,128]{3,2,1,0:T(8,128)(2,1)}, f32[128,1,128]{2,1,0:T(1,128)}) custom-call(bf16[9,48,128]{2,1,0:T(8,128)(2,1)S(1)} %collective-permute-done.4.inner_ref, bf16[9,48,128]{2,1,0:T(8,128)(2,1)S(1)} %collective-permute-done.5.outer_ref, bf16[3,8,48,256]{3,2,1,0:T(8,128)(2,1)S(1)} %get-tuple-element.66.mid_ref, ...), custom_call_target="tpu_custom_call" | custom-call | tf_op jit(solution)/shard_map/pallas_call | solution.py:46
  27.0 9.5 %all-to-all-start = ((f32[128,1,128]{2,1,0:T(1,128)}), f32[128,1,128]{2,1,0:T(1,128)S(1)}, u32[]{:S(2)}, u32[]{:S(2)}) async-start(f32[128,1,128]{2,1,0:T(1,128)} %get-tuple-element.71), calls=%async_computation | async-start | bytes 131072 | tf_op jit(solution)/shard_map/all_to_all | solution.py:703
  36.5 7.1 %shard_map.163.half_ref = f32[18,240,128]{2,1,0:T(8,128)S(1)} custom-call(bf16[2,9,48,128]{3,2,1,0:T(8,128)(2,1)} %get-tuple-element.68.sides_ref, bf16[3,8,48,256]{3,2,1,0:T(8,128)(2,1)} %get-tuple-element.85.mid_far.mid_ref, bf16[3,2,48,256]{3,2,1,0:T(8,128)(2,1)} %get-tuple-element.69.ends_far.ends_ref, bf16[768,768]{1,0:T(8,128)(2,1)} %get-tuple-element.70.w1_far.w1_ref), custom_call_target="tpu_custom_call" | custom-call | tf_op jit(solution)/shard_map/pallas_call | solution.py:46
  43.7 2.4 %all-to-all-done.stats_ref = f32[128,1,128]{2,1,0:T(1,128)S(1)} async-done(((f32[128,1,128]{2,1,0:T(1,128)}), f32[128,1,128]{2,1,0:T(1,128)S(1)}, u32[]{:S(2)}, u32[]{:S(2)}) %all-to-all-start) | async-done | bytes 65568 | tf_op jit(solution)/shard_map/all_to_all | solution.py:703
  46.1 2.5 %shard_map.164 = (bf16[10,24,1280]{2,1,0:T(8,128)(2,1)}, f32[128,1,128]{2,1,0:T(1,128)}) custom-call(f32[18,240,128]{2,1,0:T(8,128)S(1)} %shard_map.163.half_ref, f32[128,1,128]{2,1,0:T(1,128)S(1)} %all-to-all-done.stats_ref, f32[8,128]{1,0:T(8,128)S(1)} %get-tuple-element.74.params_ref, bf16[2304,256]{1,0:T(8,128)(2,1)S(1)} %get-tuple-element.75.w2_ref), custom_call_target="tpu_custom_call" | custom-call | tf_op jit(solution)/shard_map/pallas_call | solution.py:46
  48.6 7.4 %all-to-all-start.1 = ((f32[128,1,128]{2,1,0:T(1,128)}), f32[128,1,128]{2,1,0:T(1,128)S(1)}, u32[]{:S(2)}, u32[]{:S(2)}) async-start(f32[128,1,128]{2,1,0:T(1,128)} %get-tuple-element.80), calls=%async_computation.1 | async-start | bytes 131072 | tf_op jit(solution)/shard_map/all_to_all | solution.py:709
  56.0 5.2 %shard_map.165 = (f32[18,48,128]{2,1,0:T(8,128)S(1)}, f32[576,256]{1,0:T(8,128)}, bf16[2304,256]{1,0:T(8,128)(2,1)S(1)}) custom-call(bf16[10,24,1280]{2,1,0:T(8,128)(2,1)} %get-tuple-element.76.p1_ref, bf16[2304,256]{1,0:T(8,128)(2,1)S(1)} %get-tuple-element.75.w2_ref, bf16[864,64]{1,0:T(8,128)(2,1)} %bitcast.6), custom_call_target="tpu_custom_call" | custom-call | tf_op jit(solution)/shard_map/pallas_call | solution.py:46
  61.2 4.4 %all-to-all-done.1.stats_ref = f32[128,1,128]{2,1,0:T(1,128)S(1)} async-done(((f32[128,1,128]{2,1,0:T(1,128)}), f32[128,1,128]{2,1,0:T(1,128)S(1)}, u32[]{:S(2)}, u32[]{:S(2)}) %all-to-all-start.1) | async-done | bytes 65568 | tf_op jit(solution)/shard_map/all_to_all | solution.py:709
  65.6 2.1 %shard_map.166 = (f32[128,256]{1,0:T(8,128)S(1)}, bf16[64,4,1152]{2,1,0:T(4,128)(2,1)}) custom-call(f32[18,48,128]{2,1,0:T(8,128)S(1)} %get-tuple-element.81.half_ref, f32[128,1,128]{2,1,0:T(1,128)S(1)} %all-to-all-done.1.stats_ref, f32[8,128]{1,0:T(8,128)S(1)} %get-tuple-element.74.params_ref, bf16[2304,256]{1,0:T(8,128)(2,1)S(1)} %get-tuple-element.83.w3_ref), custom_call_target="tpu_custom_call" | custom-call | tf_op jit(solution)/shard_map/pallas_call | solution.py:46
  67.7 6.2 %all-to-all-start.2 = ((bf16[64,4,1152]{2,1,0:T(4,128)(2,1)}), bf16[64,4,1152]{2,1,0:T(4,128)(2,1)S(1)}, u32[]{:S(2)}, u32[]{:S(2)}) async-start(bf16[64,4,1152]{2,1,0:T(4,128)(2,1)} %get-tuple-element.88), calls=%async_computation.2 | async-start | bytes 1179648 | tf_op jit(solution)/shard_map/all_to_all | solution.py:715
  73.9 3.6 %shard_map.167 = bf16[8,32,2048]{2,1,0:T(8,128)(2,1)} custom-call(bf16[3,8,48,256]{3,2,1,0:T(8,128)(2,1)} %get-tuple-element.85.mid_far.mid_ref, bf16[3,2,48,256]{3,2,1,0:T(8,128)(2,1)} %get-tuple-element.69.ends_far.ends_ref, bf16[768,768]{1,0:T(8,128)(2,1)} %get-tuple-element.70.w1_far.w1_ref, f32[128,1,128]{2,1,0:T(1,128)S(1)} %all-to-all-done.stats_ref, ...), custom_call_target="tpu_custom_call" | custom-call | tf_op jit(solution)/shard_map/pallas_call | solution.py:46
  77.5 2.1 %shard_map.168 = bf16[4,16,2048]{2,1,0:T(8,128)(2,1)} custom-call(f32[576,256]{1,0:T(8,128)} %get-tuple-element.86.r2_ref, f32[128,1,128]{2,1,0:T(1,128)S(1)} %all-to-all-done.1.stats_ref, f32[8,128]{1,0:T(8,128)S(1)} %get-tuple-element.74.params_ref), custom_call_target="tpu_custom_call" | custom-call | tf_op jit(solution)/shard_map/pallas_call | solution.py:46
  79.6 1.6 %shard_map.169.w4_ref = bf16[2304,256]{1,0:T(8,128)(2,1)S(1)} custom-call(bf16[1728,128]{1,0:T(8,128)(2,1)} %bitcast.5), custom_call_target="tpu_custom_call" | custom-call | tf_op jit(solution)/shard_map/pallas_call | solution.py:46
  81.3 5.5 %all-to-all-done.2.own_ref = bf16[64,4,1152]{2,1,0:T(4,128)(2,1)S(1)} async-done(((bf16[64,4,1152]{2,1,0:T(4,128)(2,1)}), bf16[64,4,1152]{2,1,0:T(4,128)(2,1)S(1)}, u32[]{:S(2)}, u32[]{:S(2)}) %all-to-all-start.2) | async-done | bytes 589856 | tf_op jit(solution)/shard_map/all_to_all | solution.py:715
  86.7 1.9 %collective-permute-start.6 = (bf16[64,4,1152]{2,1,0:T(4,128)(2,1)S(1)}, bf16[64,4,1152]{2,1,0:T(4,128)(2,1)S(1)}, u32[]{:S(2)}, u32[]{:S(2)}) collective-permute-start(bf16[64,4,1152]{2,1,0:T(4,128)(2,1)S(1)} %all-to-all-done.2.own_ref), channel_id=1, source_target_pairs={{0,4},{4,0},{1,5},{5,1},{2,6},{6,2},{3,7},{7,3},{8,12},{12,8},{9,1... | collective-permute-start | bytes 1769480 | tf_op jit(solution)/shard_map/ppermute | solution.py:720
  88.6 1.6 %collective-permute-done.6.other_ref = bf16[64,4,1152]{2,1,0:T(4,128)(2,1)S(1)} collective-permute-done((bf16[64,4,1152]{2,1,0:T(4,128)(2,1)S(1)}, bf16[64,4,1152]{2,1,0:T(4,128)(2,1)S(1)}, u32[]{:S(2)}, u32[]{:S(2)}) %collective-permute-start.6) | collective-permute-done | bytes 589856 | tf_op jit(solution)/shard_map/ppermute | solution.py:720
  90.3 8.9 %shard_map.170 = (bf16[2,8,2048]{2,1,0:T(8,128)(2,1)}, bf16[8,16,8192]{2,1,0:T(8,128)(2,1)}) custom-call(f32[128,256]{1,0:T(8,128)S(1)} %get-tuple-element.91.r3_ref, bf16[64,4,1152]{2,1,0:T(4,128)(2,1)S(1)} %all-to-all-done.2.own_ref, bf16[64,4,1152]{2,1,0:T(4,128)(2,1)S(1)} %collective-permute-done.6.other_ref, f32[8,128]{1,0:T(8,128)S(1)} %get-tuple-element.74.params_ref, ...), custom_call_target="tpu_custom_call" | custom-call | tf_op jit(solution)/shard_map/pallas_call | solution.py:46
  (2 shorter events, 0.1 us)
Async XLA Ops:
  0.6 8.0 %collective-permute-start.1 = (bf16[8,32,128]{2,1,0:T(8,128)(2,1)}, bf16[8,32,128]{2,1,0:T(8,128)(2,1)S(1)}, u32[]{:S(2)}, u32[]{:S(2)}) collective-permute-start(bf16[8,32,128]{2,1,0:T(8,128)(2,1)} %volume_far.1), channel_id=1, source_target_pairs={{1,2},{2,1},{5,6},{6,5},{9,10},{10,9},{13,14},{14,13},{17,18},{18,... | collective-permute-start | bytes 196616 | tf_op jit(solution)/shard_map/ppermute | solution.py:679
  1.3 7.4 %collective-permute-start = (bf16[8,32,128]{2,1,0:T(8,128)(2,1)}, bf16[8,32,128]{2,1,0:T(8,128)(2,1)S(1)}, u32[]{:S(2)}, u32[]{:S(2)}) collective-permute-start(bf16[8,32,128]{2,1,0:T(8,128)(2,1)} %volume_far.1), channel_id=1, source_target_pairs={{0,1},{2,3},{1,0},{3,2},{4,5},{6,7},{5,4},{7,6},{8,9},{10,11},{9,8... | collective-permute-start | bytes 196616 | tf_op jit(solution)/shard_map/ppermute | solution.py:679
  8.8 5.9 %collective-permute-start.2 = (bf16[8,8,256]{2,1,0:T(8,128)(2,1)S(1)}, bf16[8,8,256]{2,1,0:T(8,128)(2,1)S(1)}, u32[]{:S(2)}, u32[]{:S(2)}) collective-permute-start(bf16[8,8,256]{2,1,0:T(8,128)(2,1)S(1)} %shard_map.158), channel_id=1, source_target_pairs={{0,4},{4,0},{1,5},{5,1},{2,6},{6,2},{3,7},{7,3},{8,12},{12,8},{9,1... | collective-permute-start | bytes 98312 | tf_op jit(solution)/shard_map/ppermute | solution.py:679
  10.1 6.7 %collective-permute-start.3 = (bf16[8,8,256]{2,1,0:T(8,128)(2,1)S(1)}, bf16[8,8,256]{2,1,0:T(8,128)(2,1)S(1)}, u32[]{:S(2)}, u32[]{:S(2)}) collective-permute-start(bf16[8,8,256]{2,1,0:T(8,128)(2,1)S(1)} %get-tuple-element.55), channel_id=1, source_target_pairs={{4,8},{8,4},{5,9},{9,5},{6,10},{10,6},{7,11},{11,7},{20,24},{24,20... | collective-permute-start | bytes 98312 | tf_op jit(solution)/shard_map/ppermute | solution.py:679
  16.9 8.5 %collective-permute-start.5 = (bf16[9,48,128]{2,1,0:T(8,128)(2,1)S(1)}, bf16[9,48,128]{2,1,0:T(8,128)(2,1)S(1)}, u32[]{:S(2)}, u32[]{:S(2)}) collective-permute-start(bf16[9,48,128]{2,1,0:T(8,128)(2,1)S(1)} %get-tuple-element.60), channel_id=1, source_target_pairs={{16,32},{48,64},{80,96},{32,16},{64,48},{96,80},{17,33},{49,65},{8... | collective-permute-start | bytes 331784 | tf_op jit(solution)/shard_map/ppermute | solution.py:679
  17.6 7.8 %collective-permute-start.4 = (bf16[9,48,128]{2,1,0:T(8,128)(2,1)S(1)}, bf16[9,48,128]{2,1,0:T(8,128)(2,1)S(1)}, u32[]{:S(2)}, u32[]{:S(2)}) collective-permute-start(bf16[9,48,128]{2,1,0:T(8,128)(2,1)S(1)} %get-tuple-element.60), channel_id=1, source_target_pairs={{0,16},{32,48},{64,80},{96,112},{16,0},{48,32},{80,64},{112,96},{1... | collective-permute-start | bytes 331784 | tf_op jit(solution)/shard_map/ppermute | solution.py:679
  27.0 19.1 %all-to-all-start = ((f32[128,1,128]{2,1,0:T(1,128)}), f32[128,1,128]{2,1,0:T(1,128)S(1)}, u32[]{:S(2)}, u32[]{:S(2)}) async-start(f32[128,1,128]{2,1,0:T(1,128)} %get-tuple-element.71), calls=%async_computation | async-start | bytes 131072 | tf_op jit(solution)/shard_map/all_to_all | solution.py:703
  48.6 17.0 %all-to-all-start.1 = ((f32[128,1,128]{2,1,0:T(1,128)}), f32[128,1,128]{2,1,0:T(1,128)S(1)}, u32[]{:S(2)}, u32[]{:S(2)}) async-start(f32[128,1,128]{2,1,0:T(1,128)} %get-tuple-element.80), calls=%async_computation.1 | async-start | bytes 131072 | tf_op jit(solution)/shard_map/all_to_all | solution.py:709
  67.7 19.0 %all-to-all-start.2 = ((bf16[64,4,1152]{2,1,0:T(4,128)(2,1)}), bf16[64,4,1152]{2,1,0:T(4,128)(2,1)S(1)}, u32[]{:S(2)}, u32[]{:S(2)}) async-start(bf16[64,4,1152]{2,1,0:T(4,128)(2,1)} %get-tuple-element.88), calls=%async_computation.2 | async-start | bytes 1179648 | tf_op jit(solution)/shard_map/all_to_all | solution.py:715
  86.7 3.5 %collective-permute-start.6 = (bf16[64,4,1152]{2,1,0:T(4,128)(2,1)S(1)}, bf16[64,4,1152]{2,1,0:T(4,128)(2,1)S(1)}, u32[]{:S(2)}, u32[]{:S(2)}) collective-permute-start(bf16[64,4,1152]{2,1,0:T(4,128)(2,1)S(1)} %all-to-all-done.2.own_ref), channel_id=1, source_target_pairs={{0,4},{4,0},{1,5},{5,1},{2,6},{6,2},{3,7},{7,3},{8,12},{12,8},{9,1... | collective-permute-start | bytes 1769480 | tf_op jit(solution)/shard_map/ppermute | solution.py:720

commit v4 on v3

--- a/solution.py
+++ b/solution.py
@@ -42,7 +42,7 @@
     return pltpu.with_memory_space_constraint(array, pltpu.HBM)
 
 
-def call(kernel, outs, ins, scratch=(), out_specs=None):
+def call(kernel, outs, ins, scratch=(), out_specs=None, cost=None):
     return pl.pallas_call(
         kernel,
         in_specs=[spec for _, spec in ins],
@@ -50,6 +50,7 @@
         out_shape=tuple(outs),
         scratch_shapes=[s if not isinstance(s, tuple) else pltpu.VMEM(*s) for s in scratch],
         compiler_params=PARAMS,
+        cost_estimate=cost,
     )(*[array for array, _ in ins])
 
 
@@ -249,28 +250,33 @@
 
 
 def inner_face(wide):
-    return call(inner_face_kernel, [near((8, 8, 256), BF16)], [(wide, VMEM)])[0]
-
-
-def assemble_kernel(wide_ref, inner_ref, outer_ref, mid_ref, packed_ref):
+    cost = pl.CostEstimate(flops=0, bytes_accessed=8_000_000, transcendentals=0)
+    return call(inner_face_kernel, [near((8, 8, 256), BF16)], [(wide, VMEM)], cost=cost)[0]
+
+
+def assemble_kernel(wide_ref, inner_ref, outer_ref, mid_ref, inner_out, outer_out):
     core = lax.axis_index("gc")
     inner, outer = inner_ref[...].astype(F32), outer_ref[...].astype(F32)
     low = jnp.where(core == 0, outer, inner)
     high = jnp.where(core == 0, inner, outer)
     mid = jnp.concatenate([low, wide_ref[...].astype(F32), high], axis=1)
     mid_ref[...] = mid.astype(BF16)
-    packed_ref[0:8] = mid[:, :, 0:128].astype(BF16)
     slot = (iota((48, 128), 1) + 8) % 128 // 16
     ends = mid[0, :, 128:256]
     for i in range(1, 8):
         ends = jnp.where(slot == i, pltpu.roll(mid[i, :, 128:256], 16 * i, 1), ends)
-    packed_ref[8] = ends.astype(BF16)
+    even = lax.axis_index("gx") % 2 == 0
+    lower, upper = mid[0:7, :, 0:128], mid[1:8, :, 0:128]
+    inner_out[0:7] = jnp.where(even, upper, lower).astype(BF16)
+    outer_out[0:7] = jnp.where(even, lower, upper).astype(BF16)
+    inner_out[7] = ends.astype(BF16)
+    outer_out[7] = ends.astype(BF16)
 
 
 def assemble(wide, inner, outer):
     return call(
         assemble_kernel,
-        [near((8, 48, 256), BF16), near((9, 48, 128), BF16)],
+        [near((8, 48, 256), BF16), near((8, 48, 128), BF16), near((8, 48, 128), BF16)],
         [(wide, VMEM), (inner, VMEM), (outer, VMEM)],
     )
 
@@ -317,8 +323,8 @@
         sides_ref[0] = inner_ref[...]
         sides_ref[1] = outer_ref[...]
 
-    fill(ends_ref, 0, plane(sides_ref[0, 7], sides_ref[0, 8], 7))
-    fill(ends_ref, 1, plane(sides_ref[1, 0], sides_ref[1, 8], 0))
+    fill(ends_ref, 0, plane(sides_ref[0, 6], sides_ref[0, 7], 7))
+    fill(ends_ref, 1, plane(sides_ref[1, 0], sides_ref[1, 7], 0))
     planes = []
     for q in range(3):
         a = [ends_ref[q, 0:1], mid_ref[q, 0:1], mid_ref[q, 1:2]]
@@ -336,7 +342,7 @@
 def first_part(inner, outer, lhs_mid, sums, w1):
     return call(
         first_kernel,
-        [far((3, 2, 48, 256), BF16), far((2, 9, 48, 128), BF16), far((DEVICES, 1, 128), F32)],
+        [far((3, 2, 48, 256), BF16), far((2, 8, 48, 128), BF16), far((DEVICES, 1, 128), F32)],
         [(inner, VMEM), (outer, VMEM), (lhs_mid, VMEM), (sums, VMEM), (w1, VMEM)],
     )
 
@@ -350,8 +356,8 @@
     for c in copies:
         c.start()
     for i in range(6):
-        fill(lhs, i, plane(sides_ref[0, 1 + i], sides_ref[0, 8], 1 + i))
-        fill(lhs, 16 + i, plane(sides_ref[1, 1 + i], sides_ref[1, 8], 1 + i))
+        fill(lhs, i, plane(sides_ref[0, i], sides_ref[0, 7], 1 + i))
+        fill(lhs, 16 + i, plane(sides_ref[1, 1 + i], sides_ref[1, 7], 1 + i))
     for c in copies:
         c.wait()
     for q in range(3):
@@ -595,57 +601,59 @@
         pd[dy, 0] = zero
         pd[dy, 9] = zero
 
-    def place(even_ref, odd_ref):
-        def step(gx, carry):
-            for gy in range(4):
-                ref = even_ref if gy % 2 == 0 else odd_ref
-                last = jnp.zeros((4, 128), F32)
-                for gz in range(4):
-                    v = ref[(gx * 2 + gy // 2) * 4 + gz].astype(F32)
+    first_core = lax.axis_index("gc") == 0
+
+    def place(gx):
+        for gh in range(2):
+            last = [jnp.zeros((4, 128), F32)] * 2
+            for gz in range(4):
+                block = (gx * 2 + gh) * 4 + gz
+                mine, theirs = own_ref[block].astype(F32), other_ref[block].astype(F32)
+                start = gz * 1024
+                for gc, v in enumerate((jnp.where(first_core, mine, theirs), jnp.where(first_core, theirs, mine))):
+                    y0 = 8 * gh + 4 * gc
                     v0, v8 = v[:, 0:128], v[:, 1024:1152]
                     offset = jnp.where(lane < 64, v0, v8)[3:4, :]
-                    start = gz * 1024
-                    p3[4 * gy : 4 * gy + 4, start : start + 128] = jnp.where(lane < 64, last, v0 + offset)
-                    p3[4 * gy : 4 * gy + 4, start + 128 : start + 1024] = v[:, 128:1024] + jnp.concatenate([offset] * 7, axis=1)
-                    last = v8 + offset
-                p3[4 * gy : 4 * gy + 4, 4096:4224] = last
-            for j in range(33):
-                lanes = slice(j * 128, (j + 1) * 128)
-                v = settle(p3[:, lanes], one)
-                if j == 0:
-                    v = jnp.where(low, 0.0, v)
-                if j == 32:
-                    v = jnp.where(low, v, 0.0)
-                pd[0, gx + 1, :, lanes] = jnp.where(y > 0, pltpu.roll(v, 1, 0), 0.0).astype(BF16)
-                pd[1, gx + 1, :, lanes] = v.astype(BF16)
-                pd[2, gx + 1, :, lanes] = jnp.where(y < 15, pltpu.roll(v, 15, 0), 0.0).astype(BF16)
-            return carry
-
-        lax.fori_loop(0, 8, step, 0)
-
-    core = lax.axis_index("gc")
-
-    @pl.when(core == 0)
-    def _():
-        place(own_ref, other_ref)
-
-    @pl.when(core != 0)
-    def _():
-        place(other_ref, own_ref)
-
-    s1 = jnp.zeros((1, 256), F32)
-    s2 = jnp.zeros((1, 256), F32)
-    for i in range(0, 32, 8):
+                    p3[gx % 2, y0 : y0 + 4, start : start + 128] = jnp.where(lane < 64, last[gc], v0 + offset)
+                    p3[gx % 2, y0 : y0 + 4, start + 128 : start + 1024] = v[:, 128:1024] + jnp.concatenate([offset] * 7, axis=1)
+                    last[gc] = v8 + offset
+            for gc in range(2):
+                p3[gx % 2, 8 * gh + 4 * gc : 8 * gh + 4 * gc + 4, 4096:4224] = last[gc]
+        for j in range(33):
+            lanes = slice(j * 128, (j + 1) * 128)
+            v = settle(p3[gx % 2, :, lanes], one)
+            if j == 0:
+                v = jnp.where(low, 0.0, v)
+            if j == 32:
+                v = jnp.where(low, v, 0.0)
+            pd[0, gx + 1, :, lanes] = jnp.where(y > 0, pltpu.roll(v, 1, 0), 0.0).astype(BF16)
+            pd[1, gx + 1, :, lanes] = v.astype(BF16)
+            pd[2, gx + 1, :, lanes] = jnp.where(y < 15, pltpu.roll(v, 15, 0), 0.0).astype(BF16)
+
+    def multiply(x0, count, t0, tiles, sums):
         planes = []
         for dx in range(3):
             for dy in range(3):
                 pieces = [
-                    pd[dy, dx : dx + 8, :, 128 * t : 128 * t + 256].reshape(128, 256) for t in range(i, i + 8)
+                    pd[dy, x0 + dx : x0 + dx + count, :, 128 * t : 128 * t + 256].reshape(count * 16, 256)
+                    for t in range(t0, t0 + tiles)
                 ]
                 planes.append(jnp.concatenate(pieces, axis=0))
         r = jnp.dot(jnp.concatenate(planes, axis=1), w4_ref[...], preferred_element_type=F32)
-        r4[i * 128 : i * 128 + 1024, :] = r
-        s1, s2 = s1 + jnp.sum(r, axis=0, keepdims=True), s2 + jnp.sum(r * r, axis=0, keepdims=True)
+        for i in range(tiles):
+            at = (t0 + i) * 128 + x0 * 16
+            r4[at : at + count * 16, :] = r[i * count * 16 : (i + 1) * count * 16]
+        return sums[0] + jnp.sum(r, axis=0, keepdims=True), sums[1] + jnp.sum(r * r, axis=0, keepdims=True)
+
+    sums = (jnp.zeros((1, 256), F32), jnp.zeros((1, 256), F32))
+    for gx in range(8):
+        place(gx)
+        if gx % 2 == 0 and gx:
+            for t in (0, 16):
+                sums = multiply(gx - 2, 2, t, 16, sums)
+    for t in (0, 16):
+        sums = multiply(6, 2, t, 16, sums)
+    s1, s2 = sums
     cells = VOXELS_1 / 512
     mean = fold(s1, 128) / cells
     variance = fold(s2, 128) / cells - mean * mean
@@ -669,7 +677,7 @@
         fourth_kernel,
         [full((2, 8, 2048), BF16), far((8, 16, 8192), BF16)],
         [(a, VMEM) for a in (r3, own, other, table, w4)],
-        [((16, 4224), F32), ((3, 10, 16, 4224), BF16), ((4096, 256), F32), ((8, 16, 8192), BF16)]
+        [((2, 16, 4224), F32), ((3, 10, 16, 4224), BF16), ((4096, 256), F32), ((8, 16, 8192), BF16)]
         + [pltpu.SemaphoreType.DMA((4,))],
         [VMEM, ANY],
     )
@@ -689,12 +697,13 @@
     w1, w1_far, block = first_band(k1, volume)
     (inner, outer, w1) = lax.optimization_barrier((inner, outer, w1))
     wide, outer = widen(block, inner, outer)
+    (wide, outer, k2) = lax.optimization_barrier((wide, outer, k2))
     outer = across(outer, ("gh", "gc"), [(1, 2)])
     inner = across(inner_face(wide), "gc", [(0, 1)])
-    mid, packed = assemble(wide, inner, outer)
-    (packed, k2) = lax.optimization_barrier((packed, k2))
-    inner = across(packed, "gx", [(0, 1), (2, 3), (4, 5), (6, 7)])
-    outer = across(packed, "gx", [(1, 2), (3, 4), (5, 6)])
+    mid, inner, outer = assemble(wide, inner, outer)
+    (mid, k2) = lax.optimization_barrier((mid, k2))
+    inner = across(inner, "gx", [(0, 1), (2, 3), (4, 5), (6, 7)])
+    outer = across(outer, "gx", [(1, 2), (3, 4), (5, 6)])
     w2, table = early_part(k2, (g1, b1, g2, b2, g3, b3, g4, b4))
     lhs_mid, far_mid, sums = middle_part(mid, w1)
     (inner, outer, lhs_mid, w2) = lax.optimization_barrier((inner, outer, lhs_mid, w2))

time: 100 us -> 98.9 us (0.989)
    ppermute x6, starting transfers between devices: 16.1 us -> 12.9 us  [across(): return lax.ppermute(block, axis, swaps + [(b, a) for a, b in swaps])]
    all_to_all x1, starting transfers between devices: 9.54 us -> 12.2 us  [shards(): total1 = lax.all_to_all(stats, AXES, 0, 0, tiled=True)]
  transfers between devices with their start and end apart: 10 -> 10, of which waited for: 5 -> 5; matrix products, arithmetic and copies ran while one was open for 1% -> 1% of each run, Pallas kernels for 25% -> 26%
where the time goes in v4:
time: 98.9 us; the launch traced here: 98.3 us
  starting transfers between devices  40.6 us (41%)
  Pallas kernels  39.7 us (40%)
  waiting for transfers between devices  16.3 us (16%)
    pallas_call x15, Pallas kernels, call(): pl.pallas_call(kernel, in_specs=[spec for _, spec in ins], out_specs=tupl...  39.7 us
    ppermute x6, starting transfers between devices, across(): return lax.ppermute(block, axis, swaps + [(b, a) for a, b in swaps])  12.9 us
    all_to_all x1, starting transfers between devices, shards(): total1 = lax.all_to_all(stats, AXES, 0, 0, tiled=True)  12.2 us
    all_to_all x1, starting transfers between devices, shards(): total2 = lax.all_to_all(stats, AXES, 0, 0, tiled=True)  7.36 us
    all_to_all x1, starting transfers between devices, shards(): own = lax.all_to_all(packed, CHIPS, 0, 0, tiled=True)  6.2 us
    all_to_all x1, waiting for transfers between devices, shards(): own = lax.all_to_all(packed, CHIPS, 0, 0, tiled=True)  5.45 us
    all_to_all x1, waiting for transfers between devices, shards(): total2 = lax.all_to_all(stats, AXES, 0, 0, tiled=True)  4.34 us
    ppermute x6, waiting for transfers between devices, across(): return lax.ppermute(block, axis, swaps + [(b, a) for a, b in swaps])  2.47 us
  transfers between devices with their start and end apart: 10, of which 5 were waited for; matrix products, arithmetic and copies ran while one was open for 1% of the time, Pallas kernels for 26%

profile of v4, /device:TPU:1, one launch (start us, length us, event | category | flops | bytes accessed | tf_op | source)
XLA Modules:
  0.0 98.3 jit_solution(777991282082571722)
XLA Ops:
  0.6 0.7 collective-permute-start.1
  1.3 4.7 %collective-permute-start = (bf16[8,32,128]{2,1,0:T(8,128)(2,1)}, bf16[8,32,128]{2,1,0:T(8,128)(2,1)S(1)}, u32[]{:S(2)}, u32[]{:S(2)}) collective-permute-start(bf16[8,32,128]{2,1,0:T(8,128)(2,1)} %volume_far.1), channel_id=1, source_target_pairs={{0,1},{2,3},{1,0},{3,2},{4,5},{6,7},{5,4},{7,6},{8,9},{10,11},{9,8... | collective-permute-start | bytes 196616 | tf_op jit(solution)/shard_map/ppermute | solution.py:687
  6.1 0.7 reshape.20.k_ref
  6.8 1.9 %shard_map.156 = (bf16[768,768]{1,0:T(8,128)(2,1)S(1)}, bf16[768,768]{1,0:T(8,128)(2,1)}, bf16[8,32,128]{2,1,0:T(8,128)(2,1)S(1)}) custom-call(bf16[27,16]{1,0:T(8,128)(2,1)S(1)} %reshape.20.k_ref, bf16[8,32,128]{2,1,0:T(8,128)(2,1)} %volume_far.1), custom_call_target="tpu_custom_call" | custom-call | tf_op jit(solution)/shard_map/pallas_call | solution.py:46
  8.7 0.0 collective-permute-done.1.outer_ref
  8.7 0.0 collective-permute-done.inner_ref
  8.8 1.3 %collective-permute-start.2 = (bf16[8,8,256]{2,1,0:T(8,128)(2,1)S(1)}, bf16[8,8,256]{2,1,0:T(8,128)(2,1)S(1)}, u32[]{:S(2)}, u32[]{:S(2)}) collective-permute-start(bf16[8,8,256]{2,1,0:T(8,128)(2,1)S(1)} %shard_map.158), channel_id=1, source_target_pairs={{0,4},{4,0},{1,5},{5,1},{2,6},{6,2},{3,7},{7,3},{8,12},{12,8},{9,1... | collective-permute-start | bytes 98312 | tf_op jit(solution)/shard_map/ppermute | solution.py:687
  10.1 4.6 %collective-permute-start.3 = (bf16[8,8,256]{2,1,0:T(8,128)(2,1)S(1)}, bf16[8,8,256]{2,1,0:T(8,128)(2,1)S(1)}, u32[]{:S(2)}, u32[]{:S(2)}) collective-permute-start(bf16[8,8,256]{2,1,0:T(8,128)(2,1)S(1)} %get-tuple-element.61), channel_id=1, source_target_pairs={{4,8},{8,4},{5,9},{9,5},{6,10},{10,6},{7,11},{11,7},{20,24},{24,20... | collective-permute-start | bytes 98312 | tf_op jit(solution)/shard_map/ppermute | solution.py:687
  14.6 0.0 collective-permute-done.2.inner_ref
  14.7 2.5 %collective-permute-done.3.outer_ref = bf16[8,8,256]{2,1,0:T(8,128)(2,1)S(1)} collective-permute-done((bf16[8,8,256]{2,1,0:T(8,128)(2,1)S(1)}, bf16[8,8,256]{2,1,0:T(8,128)(2,1)S(1)}, u32[]{:S(2)}, u32[]{:S(2)}) %collective-permute-start.3) | collective-permute-done | bytes 32800 | tf_op jit(solution)/shard_map/ppermute | solution.py:687
  17.1 0.1 shard_map.159
  17.2 1.0 %collective-permute-start.4 = (bf16[8,48,128]{2,1,0:T(8,128)(2,1)S(1)}, bf16[8,48,128]{2,1,0:T(8,128)(2,1)S(1)}, u32[]{:S(2)}, u32[]{:S(2)}) collective-permute-start(bf16[8,48,128]{2,1,0:T(8,128)(2,1)S(1)} %get-tuple-element.67), channel_id=1, source_target_pairs={{0,16},{32,48},{64,80},{96,112},{16,0},{48,32},{80,64},{112,96},{1... | collective-permute-start | bytes 294920 | tf_op jit(solution)/shard_map/ppermute | solution.py:687
  18.2 0.7 collective-permute-start.5
  18.9 2.0 %shard_map.160 = (bf16[3,8,48,256]{3,2,1,0:T(8,128)(2,1)S(1)}, bf16[3,8,48,256]{3,2,1,0:T(8,128)(2,1)}, f32[8,768]{1,0:T(8,128)S(1)}) custom-call(bf16[8,48,256]{2,1,0:T(8,128)(2,1)S(1)} %get-tuple-element.64.mid_ref, bf16[768,768]{1,0:T(8,128)(2,1)S(1)} %get-tuple-element.65.w1_ref), custom_call_target="tpu_custom_call" | custom-call | tf_op jit(solution)/shard_map/pallas_call | solution.py:46
  20.9 1.7 %shard_map.161 = (bf16[2304,256]{1,0:T(8,128)(2,1)S(1)}, f32[8,128]{1,0:T(8,128)S(1)}) custom-call(bf16[432,32]{1,0:T(8,128)(2,1)} %bitcast.7, f32[16]{0:T(128)} %refs_1_.1, f32[16]{0:T(128)} %refs_2_.1, f32[32]{0:T(128)} %refs_3_.1, f32[32]{0:T(128)} %refs_4_.1, f32[64]{0:T(128)} %refs_5_.1, f32[64]{0:T(128)} %refs_6_.1, f32[128]{0:T(128)} %refs_7_.1, ...), custom_call_target="tpu_custom_call" | custom-call | tf_op jit(solution)/shard_map/pallas_call | solution.py:46
  22.5 0.0 collective-permute-done.4.inner_ref
  22.5 0.0 collective-permute-done.5.outer_ref
  22.5 1.6 %shard_map.162 = (bf16[3,2,48,256]{3,2,1,0:T(8,128)(2,1)}, bf16[2,8,48,128]{3,2,1,0:T(8,128)(2,1)}, f32[128,1,128]{2,1,0:T(1,128)}) custom-call(bf16[8,48,128]{2,1,0:T(8,128)(2,1)S(1)} %collective-permute-done.4.inner_ref, bf16[8,48,128]{2,1,0:T(8,128)(2,1)S(1)} %collective-permute-done.5.outer_ref, bf16[3,8,48,256]{3,2,1,0:T(8,128)(2,1)S(1)} %get-tuple-element.74.mid_ref, ...), custom_call_target="tpu_custom_call" | custom-call | tf_op jit(solution)/shard_map/pallas_call | solution.py:46
  24.1 12.2 %all-to-all-start = ((f32[128,1,128]{2,1,0:T(1,128)}), f32[128,1,128]{2,1,0:T(1,128)S(1)}, u32[]{:S(2)}, u32[]{:S(2)}) async-start(f32[128,1,128]{2,1,0:T(1,128)} %get-tuple-element.79), calls=%async_computation | async-start | bytes 131072 | tf_op jit(solution)/shard_map/all_to_all | solution.py:712
  36.3 7.1 %shard_map.163.half_ref = f32[18,240,128]{2,1,0:T(8,128)S(1)} custom-call(bf16[2,8,48,128]{3,2,1,0:T(8,128)(2,1)} %get-tuple-element.76.sides_ref, bf16[3,8,48,256]{3,2,1,0:T(8,128)(2,1)} %get-tuple-element.93.mid_far.mid_ref, bf16[3,2,48,256]{3,2,1,0:T(8,128)(2,1)} %get-tuple-element.77.ends_far.ends_ref, bf16[768,768]{1,0:T(8,128)(2,1)} %get-tuple-element.78.w1_far.w1_ref), custom_call_target="tpu_custom_call" | custom-call | tf_op jit(solution)/shard_map/pallas_call | solution.py:46
  43.4 2.4 %all-to-all-done.stats_ref = f32[128,1,128]{2,1,0:T(1,128)S(1)} async-done(((f32[128,1,128]{2,1,0:T(1,128)}), f32[128,1,128]{2,1,0:T(1,128)S(1)}, u32[]{:S(2)}, u32[]{:S(2)}) %all-to-all-start) | async-done | bytes 65568 | tf_op jit(solution)/shard_map/all_to_all | solution.py:712
  45.9 2.6 %shard_map.164 = (bf16[10,24,1280]{2,1,0:T(8,128)(2,1)}, f32[128,1,128]{2,1,0:T(1,128)}) custom-call(f32[18,240,128]{2,1,0:T(8,128)S(1)} %shard_map.163.half_ref, f32[128,1,128]{2,1,0:T(1,128)S(1)} %all-to-all-done.stats_ref, f32[8,128]{1,0:T(8,128)S(1)} %get-tuple-element.82.params_ref, bf16[2304,256]{1,0:T(8,128)(2,1)S(1)} %get-tuple-element.83.w2_ref), custom_call_target="tpu_custom_call" | custom-call | tf_op jit(solution)/shard_map/pallas_call | solution.py:46
  48.4 7.4 %all-to-all-start.1 = ((f32[128,1,128]{2,1,0:T(1,128)}), f32[128,1,128]{2,1,0:T(1,128)S(1)}, u32[]{:S(2)}, u32[]{:S(2)}) async-start(f32[128,1,128]{2,1,0:T(1,128)} %get-tuple-element.88), calls=%async_computation.1 | async-start | bytes 131072 | tf_op jit(solution)/shard_map/all_to_all | solution.py:718
  55.8 5.2 %shard_map.165 = (f32[18,48,128]{2,1,0:T(8,128)S(1)}, f32[576,256]{1,0:T(8,128)}, bf16[2304,256]{1,0:T(8,128)(2,1)S(1)}) custom-call(bf16[10,24,1280]{2,1,0:T(8,128)(2,1)} %get-tuple-element.84.p1_ref, bf16[2304,256]{1,0:T(8,128)(2,1)S(1)} %get-tuple-element.83.w2_ref, bf16[864,64]{1,0:T(8,128)(2,1)} %bitcast.6), custom_call_target="tpu_custom_call" | custom-call | tf_op jit(solution)/shard_map/pallas_call | solution.py:46
  61.0 4.3 %all-to-all-done.1.stats_ref = f32[128,1,128]{2,1,0:T(1,128)S(1)} async-done(((f32[128,1,128]{2,1,0:T(1,128)}), f32[128,1,128]{2,1,0:T(1,128)S(1)}, u32[]{:S(2)}, u32[]{:S(2)}) %all-to-all-start.1) | async-done | bytes 65568 | tf_op jit(solution)/shard_map/all_to_all | solution.py:718
  65.4 2.2 %shard_map.166 = (f32[128,256]{1,0:T(8,128)S(1)}, bf16[64,4,1152]{2,1,0:T(4,128)(2,1)}) custom-call(f32[18,48,128]{2,1,0:T(8,128)S(1)} %get-tuple-element.89.half_ref, f32[128,1,128]{2,1,0:T(1,128)S(1)} %all-to-all-done.1.stats_ref, f32[8,128]{1,0:T(8,128)S(1)} %get-tuple-element.82.params_ref, bf16[2304,256]{1,0:T(8,128)(2,1)S(1)} %get-tuple-element.91.w3_ref), custom_call_target="tpu_custom_call" | custom-call | tf_op jit(solution)/shard_map/pallas_call | solution.py:46
  67.5 6.2 %all-to-all-start.2 = ((bf16[64,4,1152]{2,1,0:T(4,128)(2,1)}), bf16[64,4,1152]{2,1,0:T(4,128)(2,1)S(1)}, u32[]{:S(2)}, u32[]{:S(2)}) async-start(bf16[64,4,1152]{2,1,0:T(4,128)(2,1)} %get-tuple-element.96), calls=%async_computation.2 | async-start | bytes 1179648 | tf_op jit(solution)/shard_map/all_to_all | solution.py:724
  73.7 3.6 %shard_map.167 = bf16[8,32,2048]{2,1,0:T(8,128)(2,1)} custom-call(bf16[3,8,48,256]{3,2,1,0:T(8,128)(2,1)} %get-tuple-element.93.mid_far.mid_ref, bf16[3,2,48,256]{3,2,1,0:T(8,128)(2,1)} %get-tuple-element.77.ends_far.ends_ref, bf16[768,768]{1,0:T(8,128)(2,1)} %get-tuple-element.78.w1_far.w1_ref, f32[128,1,128]{2,1,0:T(1,128)S(1)} %all-to-all-done.stats_ref, ...), custom_call_target="tpu_custom_call" | custom-call | tf_op jit(solution)/shard_map/pallas_call | solution.py:46
  77.4 2.1 %shard_map.168 = bf16[4,16,2048]{2,1,0:T(8,128)(2,1)} custom-call(f32[576,256]{1,0:T(8,128)} %get-tuple-element.94.r2_ref, f32[128,1,128]{2,1,0:T(1,128)S(1)} %all-to-all-done.1.stats_ref, f32[8,128]{1,0:T(8,128)S(1)} %get-tuple-element.82.params_ref), custom_call_target="tpu_custom_call" | custom-call | tf_op jit(solution)/shard_map/pallas_call | solution.py:46
  79.5 1.6 %shard_map.169.w4_ref = bf16[2304,256]{1,0:T(8,128)(2,1)S(1)} custom-call(bf16[1728,128]{1,0:T(8,128)(2,1)} %bitcast.5), custom_call_target="tpu_custom_call" | custom-call | tf_op jit(solution)/shard_map/pallas_call | solution.py:46
  81.1 5.5 %all-to-all-done.2.own_ref = bf16[64,4,1152]{2,1,0:T(4,128)(2,1)S(1)} async-done(((bf16[64,4,1152]{2,1,0:T(4,128)(2,1)}), bf16[64,4,1152]{2,1,0:T(4,128)(2,1)S(1)}, u32[]{:S(2)}, u32[]{:S(2)}) %all-to-all-start.2) | async-done | bytes 589856 | tf_op jit(solution)/shard_map/all_to_all | solution.py:724
  86.6 1.9 %collective-permute-start.6 = (bf16[64,4,1152]{2,1,0:T(4,128)(2,1)S(1)}, bf16[64,4,1152]{2,1,0:T(4,128)(2,1)S(1)}, u32[]{:S(2)}, u32[]{:S(2)}) collective-permute-start(bf16[64,4,1152]{2,1,0:T(4,128)(2,1)S(1)} %all-to-all-done.2.own_ref), channel_id=1, source_target_pairs={{0,4},{4,0},{1,5},{5,1},{2,6},{6,2},{3,7},{7,3},{8,12},{12,8},{9,1... | collective-permute-start | bytes 1769480 | tf_op jit(solution)/shard_map/ppermute | solution.py:729
  88.5 1.6 %collective-permute-done.6.other_ref = bf16[64,4,1152]{2,1,0:T(4,128)(2,1)S(1)} collective-permute-done((bf16[64,4,1152]{2,1,0:T(4,128)(2,1)S(1)}, bf16[64,4,1152]{2,1,0:T(4,128)(2,1)S(1)}, u32[]{:S(2)}, u32[]{:S(2)}) %collective-permute-start.6) | collective-permute-done | bytes 589856 | tf_op jit(solution)/shard_map/ppermute | solution.py:729
  90.1 8.0 %shard_map.170 = (bf16[2,8,2048]{2,1,0:T(8,128)(2,1)}, bf16[8,16,8192]{2,1,0:T(8,128)(2,1)}) custom-call(f32[128,256]{1,0:T(8,128)S(1)} %get-tuple-element.99.r3_ref, bf16[64,4,1152]{2,1,0:T(4,128)(2,1)S(1)} %all-to-all-done.2.own_ref, bf16[64,4,1152]{2,1,0:T(4,128)(2,1)S(1)} %collective-permute-done.6.other_ref, f32[8,128]{1,0:T(8,128)S(1)} %get-tuple-element.82.params_ref, ...), custom_call_target="tpu_custom_call" | custom-call | tf_op jit(solution)/shard_map/pallas_call | solution.py:46
  (2 shorter events, 0.1 us)
Async XLA Ops:
  0.6 8.0 %collective-permute-start.1 = (bf16[8,32,128]{2,1,0:T(8,128)(2,1)}, bf16[8,32,128]{2,1,0:T(8,128)(2,1)S(1)}, u32[]{:S(2)}, u32[]{:S(2)}) collective-permute-start(bf16[8,32,128]{2,1,0:T(8,128)(2,1)} %volume_far.1), channel_id=1, source_target_pairs={{1,2},{2,1},{5,6},{6,5},{9,10},{10,9},{13,14},{14,13},{17,18},{18,... | collective-permute-start | bytes 196616 | tf_op jit(solution)/shard_map/ppermute | solution.py:687
  1.3 7.4 %collective-permute-start = (bf16[8,32,128]{2,1,0:T(8,128)(2,1)}, bf16[8,32,128]{2,1,0:T(8,128)(2,1)S(1)}, u32[]{:S(2)}, u32[]{:S(2)}) collective-permute-start(bf16[8,32,128]{2,1,0:T(8,128)(2,1)} %volume_far.1), channel_id=1, source_target_pairs={{0,1},{2,3},{1,0},{3,2},{4,5},{6,7},{5,4},{7,6},{8,9},{10,11},{9,8... | collective-permute-start | bytes 196616 | tf_op jit(solution)/shard_map/ppermute | solution.py:687
  8.8 5.9 %collective-permute-start.2 = (bf16[8,8,256]{2,1,0:T(8,128)(2,1)S(1)}, bf16[8,8,256]{2,1,0:T(8,128)(2,1)S(1)}, u32[]{:S(2)}, u32[]{:S(2)}) collective-permute-start(bf16[8,8,256]{2,1,0:T(8,128)(2,1)S(1)} %shard_map.158), channel_id=1, source_target_pairs={{0,4},{4,0},{1,5},{5,1},{2,6},{6,2},{3,7},{7,3},{8,12},{12,8},{9,1... | collective-permute-start | bytes 98312 | tf_op jit(solution)/shard_map/ppermute | solution.py:687
  10.1 7.0 %collective-permute-start.3 = (bf16[8,8,256]{2,1,0:T(8,128)(2,1)S(1)}, bf16[8,8,256]{2,1,0:T(8,128)(2,1)S(1)}, u32[]{:S(2)}, u32[]{:S(2)}) collective-permute-start(bf16[8,8,256]{2,1,0:T(8,128)(2,1)S(1)} %get-tuple-element.61), channel_id=1, source_target_pairs={{4,8},{8,4},{5,9},{9,5},{6,10},{10,6},{7,11},{11,7},{20,24},{24,20... | collective-permute-start | bytes 98312 | tf_op jit(solution)/shard_map/ppermute | solution.py:687
  17.2 5.3 %collective-permute-start.4 = (bf16[8,48,128]{2,1,0:T(8,128)(2,1)S(1)}, bf16[8,48,128]{2,1,0:T(8,128)(2,1)S(1)}, u32[]{:S(2)}, u32[]{:S(2)}) collective-permute-start(bf16[8,48,128]{2,1,0:T(8,128)(2,1)S(1)} %get-tuple-element.67), channel_id=1, source_target_pairs={{0,16},{32,48},{64,80},{96,112},{16,0},{48,32},{80,64},{112,96},{1... | collective-permute-start | bytes 294920 | tf_op jit(solution)/shard_map/ppermute | solution.py:687
  18.2 4.3 %collective-permute-start.5 = (bf16[8,48,128]{2,1,0:T(8,128)(2,1)S(1)}, bf16[8,48,128]{2,1,0:T(8,128)(2,1)S(1)}, u32[]{:S(2)}, u32[]{:S(2)}) collective-permute-start(bf16[8,48,128]{2,1,0:T(8,128)(2,1)S(1)} %get-tuple-element.68), channel_id=1, source_target_pairs={{16,32},{48,64},{80,96},{32,16},{64,48},{96,80},{17,33},{49,65},{8... | collective-permute-start | bytes 294920 | tf_op jit(solution)/shard_map/ppermute | solution.py:687
  24.1 21.8 %all-to-all-start = ((f32[128,1,128]{2,1,0:T(1,128)}), f32[128,1,128]{2,1,0:T(1,128)S(1)}, u32[]{:S(2)}, u32[]{:S(2)}) async-start(f32[128,1,128]{2,1,0:T(1,128)} %get-tuple-element.79), calls=%async_computation | async-start | bytes 131072 | tf_op jit(solution)/shard_map/all_to_all | solution.py:712
  48.4 16.9 %all-to-all-start.1 = ((f32[128,1,128]{2,1,0:T(1,128)}), f32[128,1,128]{2,1,0:T(1,128)S(1)}, u32[]{:S(2)}, u32[]{:S(2)}) async-start(f32[128,1,128]{2,1,0:T(1,128)} %get-tuple-element.88), calls=%async_computation.1 | async-start | bytes 131072 | tf_op jit(solution)/shard_map/all_to_all | solution.py:718
  67.5 19.0 %all-to-all-start.2 = ((bf16[64,4,1152]{2,1,0:T(4,128)(2,1)}), bf16[64,4,1152]{2,1,0:T(4,128)(2,1)S(1)}, u32[]{:S(2)}, u32[]{:S(2)}) async-start(bf16[64,4,1152]{2,1,0:T(4,128)(2,1)} %get-tuple-element.96), calls=%async_computation.2 | async-start | bytes 1179648 | tf_op jit(solution)/shard_map/all_to_all | solution.py:724
  86.6 3.5 %collective-permute-start.6 = (bf16[64,4,1152]{2,1,0:T(4,128)(2,1)S(1)}, bf16[64,4,1152]{2,1,0:T(4,128)(2,1)S(1)}, u32[]{:S(2)}, u32[]{:S(2)}) collective-permute-start(bf16[64,4,1152]{2,1,0:T(4,128)(2,1)S(1)} %all-to-all-done.2.own_ref), channel_id=1, source_target_pairs={{0,4},{4,0},{1,5},{5,1},{2,6},{6,2},{3,7},{7,3},{8,12},{12,8},{9,1... | collective-permute-start | bytes 1769480 | tf_op jit(solution)/shard_map/ppermute | solution.py:729

commit v5 on v4

--- a/solution.py
+++ b/solution.py
@@ -364,7 +364,7 @@
         r = response_1([lhs[q, dx : 20 + dx] for dx in range(3)], w1_ref)
         r = jnp.max(r.reshape(10, 2, 48, 768), axis=1).reshape(480, 768)
         for j in range(6):
-            rows[j] = r[:, j * 128 : (j + 1) * 128]
+            rows[j, 0:480] = r[:, j * 128 : (j + 1) * 128]
         for j in range(6):
             half_ref[q * 6 + j] = paired_rows(rows, j, 240)
 
@@ -374,7 +374,7 @@
         wide_first_kernel,
         [near((18, 240, 128), F32)],
         [(held(sides), VMEM)] + [(held(a), ANY) for a in (lhs_mid, ends, w1)],
-        [((3, 22, 48, 256), BF16), ((6, 480, 128), F32), ((768, 768), BF16), pltpu.SemaphoreType.DMA((10,))],
+        [((3, 22, 48, 256), BF16), ((6, 488, 128), F32), ((768, 768), BF16), pltpu.SemaphoreType.DMA((10,))],
     )[0]
 
 
@@ -484,7 +484,7 @@
         r = jnp.max(r.reshape(3, 4, 2, 24, 256), axis=2).reshape(3, 96, 256)
         for i in range(3):
             for j in range(2):
-                rows[2 * i + j] = r[i, :, j * 128 : (j + 1) * 128]
+                rows[2 * i + j, 0:96] = r[i, :, j * 128 : (j + 1) * 128]
         for j in range(6):
             half_ref[2 * t + j] = paired_rows(rows, j, 48)
     kernel.wait()
@@ -496,7 +496,7 @@
         wide_second_kernel,
         [near((18, 48, 128), F32), far((576, 256), F32), near((2304, 256), BF16)],
         [(held(p1), VMEM), (w2, VMEM), (held(k3.reshape(864, 64)), ANY)],
-        [((3, 10, 24, 1280), F32), ((6, 96, 128), F32), ((864, 64), BF16), ((864, 256), F32)]
+        [((3, 10, 24, 1280), F32), ((6, 104, 128), F32), ((864, 64), BF16), ((864, 256), F32)]
         + [pltpu.SemaphoreType.DMA(())],
     )
 

time: 98.9 us -> 98.9 us (level)
  no operation moved by 1% of the time
where the time goes in v5:
time: 98.9 us; the launch traced here: 98.3 us
  starting transfers between devices  40.6 us (41%)
  Pallas kernels  39.7 us (40%)
  waiting for transfers between devices  16.3 us (16%)
    pallas_call x15, Pallas kernels, call(): pl.pallas_call(kernel, in_specs=[spec for _, spec in ins], out_specs=tupl...  39.7 us
    ppermute x6, starting transfers between devices, across(): return lax.ppermute(block, axis, swaps + [(b, a) for a, b in swaps])  12.9 us
    all_to_all x1, starting transfers between devices, shards(): total1 = lax.all_to_all(stats, AXES, 0, 0, tiled=True)  12.2 us
    all_to_all x1, starting transfers between devices, shards(): total2 = lax.all_to_all(stats, AXES, 0, 0, tiled=True)  7.37 us
    all_to_all x1, starting transfers between devices, shards(): own = lax.all_to_all(packed, CHIPS, 0, 0, tiled=True)  6.2 us
    all_to_all x1, waiting for transfers between devices, shards(): own = lax.all_to_all(packed, CHIPS, 0, 0, tiled=True)  5.45 us
    all_to_all x1, waiting for transfers between devices, shards(): total2 = lax.all_to_all(stats, AXES, 0, 0, tiled=True)  4.35 us
    ppermute x6, waiting for transfers between devices, across(): return lax.ppermute(block, axis, swaps + [(b, a) for a, b in swaps])  2.47 us
  transfers between devices with their start and end apart: 10, of which 5 were waited for; matrix products, arithmetic and copies ran while one was open for 1% of the time, Pallas kernels for 26%

profile of v5, /device:TPU:1, one launch (start us, length us, event | category | flops | bytes accessed | tf_op | source)
XLA Modules:
  0.0 98.3 jit_solution(10571004747005640999)
XLA Ops:
  0.6 0.7 collective-permute-start.1
  1.3 4.7 %collective-permute-start = (bf16[8,32,128]{2,1,0:T(8,128)(2,1)}, bf16[8,32,128]{2,1,0:T(8,128)(2,1)S(1)}, u32[]{:S(2)}, u32[]{:S(2)}) collective-permute-start(bf16[8,32,128]{2,1,0:T(8,128)(2,1)} %volume_far.1), channel_id=1, source_target_pairs={{0,1},{2,3},{1,0},{3,2},{4,5},{6,7},{5,4},{7,6},{8,9},{10,11},{9,8... | collective-permute-start | bytes 196616 | tf_op jit(solution)/shard_map/ppermute | solution.py:687
  6.1 0.7 reshape.20.k_ref
  6.8 1.9 %shard_map.156 = (bf16[768,768]{1,0:T(8,128)(2,1)S(1)}, bf16[768,768]{1,0:T(8,128)(2,1)}, bf16[8,32,128]{2,1,0:T(8,128)(2,1)S(1)}) custom-call(bf16[27,16]{1,0:T(8,128)(2,1)S(1)} %reshape.20.k_ref, bf16[8,32,128]{2,1,0:T(8,128)(2,1)} %volume_far.1), custom_call_target="tpu_custom_call" | custom-call | tf_op jit(solution)/shard_map/pallas_call | solution.py:46
  8.7 0.0 collective-permute-done.1.outer_ref
  8.7 0.0 collective-permute-done.inner_ref
  8.8 1.3 %collective-permute-start.2 = (bf16[8,8,256]{2,1,0:T(8,128)(2,1)S(1)}, bf16[8,8,256]{2,1,0:T(8,128)(2,1)S(1)}, u32[]{:S(2)}, u32[]{:S(2)}) collective-permute-start(bf16[8,8,256]{2,1,0:T(8,128)(2,1)S(1)} %shard_map.158), channel_id=1, source_target_pairs={{0,4},{4,0},{1,5},{5,1},{2,6},{6,2},{3,7},{7,3},{8,12},{12,8},{9,1... | collective-permute-start | bytes 98312 | tf_op jit(solution)/shard_map/ppermute | solution.py:687
  10.1 4.6 %collective-permute-start.3 = (bf16[8,8,256]{2,1,0:T(8,128)(2,1)S(1)}, bf16[8,8,256]{2,1,0:T(8,128)(2,1)S(1)}, u32[]{:S(2)}, u32[]{:S(2)}) collective-permute-start(bf16[8,8,256]{2,1,0:T(8,128)(2,1)S(1)} %get-tuple-element.61), channel_id=1, source_target_pairs={{4,8},{8,4},{5,9},{9,5},{6,10},{10,6},{7,11},{11,7},{20,24},{24,20... | collective-permute-start | bytes 98312 | tf_op jit(solution)/shard_map/ppermute | solution.py:687
  14.6 0.0 collective-permute-done.2.inner_ref
  14.7 2.5 %collective-permute-done.3.outer_ref = bf16[8,8,256]{2,1,0:T(8,128)(2,1)S(1)} collective-permute-done((bf16[8,8,256]{2,1,0:T(8,128)(2,1)S(1)}, bf16[8,8,256]{2,1,0:T(8,128)(2,1)S(1)}, u32[]{:S(2)}, u32[]{:S(2)}) %collective-permute-start.3) | collective-permute-done | bytes 32800 | tf_op jit(solution)/shard_map/ppermute | solution.py:687
  17.1 0.1 shard_map.159
  17.2 1.0 %collective-permute-start.4 = (bf16[8,48,128]{2,1,0:T(8,128)(2,1)S(1)}, bf16[8,48,128]{2,1,0:T(8,128)(2,1)S(1)}, u32[]{:S(2)}, u32[]{:S(2)}) collective-permute-start(bf16[8,48,128]{2,1,0:T(8,128)(2,1)S(1)} %get-tuple-element.67), channel_id=1, source_target_pairs={{0,16},{32,48},{64,80},{96,112},{16,0},{48,32},{80,64},{112,96},{1... | collective-permute-start | bytes 294920 | tf_op jit(solution)/shard_map/ppermute | solution.py:687
  18.2 0.7 collective-permute-start.5
  18.9 2.0 %shard_map.160 = (bf16[3,8,48,256]{3,2,1,0:T(8,128)(2,1)S(1)}, bf16[3,8,48,256]{3,2,1,0:T(8,128)(2,1)}, f32[8,768]{1,0:T(8,128)S(1)}) custom-call(bf16[8,48,256]{2,1,0:T(8,128)(2,1)S(1)} %get-tuple-element.64.mid_ref, bf16[768,768]{1,0:T(8,128)(2,1)S(1)} %get-tuple-element.65.w1_ref), custom_call_target="tpu_custom_call" | custom-call | tf_op jit(solution)/shard_map/pallas_call | solution.py:46
  20.9 1.7 %shard_map.161 = (bf16[2304,256]{1,0:T(8,128)(2,1)S(1)}, f32[8,128]{1,0:T(8,128)S(1)}) custom-call(bf16[432,32]{1,0:T(8,128)(2,1)} %bitcast.7, f32[16]{0:T(128)} %refs_1_.1, f32[16]{0:T(128)} %refs_2_.1, f32[32]{0:T(128)} %refs_3_.1, f32[32]{0:T(128)} %refs_4_.1, f32[64]{0:T(128)} %refs_5_.1, f32[64]{0:T(128)} %refs_6_.1, f32[128]{0:T(128)} %refs_7_.1, ...), custom_call_target="tpu_custom_call" | custom-call | tf_op jit(solution)/shard_map/pallas_call | solution.py:46
  22.5 0.0 collective-permute-done.4.inner_ref
  22.5 0.0 collective-permute-done.5.outer_ref
  22.5 1.6 %shard_map.162 = (bf16[3,2,48,256]{3,2,1,0:T(8,128)(2,1)}, bf16[2,8,48,128]{3,2,1,0:T(8,128)(2,1)}, f32[128,1,128]{2,1,0:T(1,128)}) custom-call(bf16[8,48,128]{2,1,0:T(8,128)(2,1)S(1)} %collective-permute-done.4.inner_ref, bf16[8,48,128]{2,1,0:T(8,128)(2,1)S(1)} %collective-permute-done.5.outer_ref, bf16[3,8,48,256]{3,2,1,0:T(8,128)(2,1)S(1)} %get-tuple-element.74.mid_ref, ...), custom_call_target="tpu_custom_call" | custom-call | tf_op jit(solution)/shard_map/pallas_call | solution.py:46
  24.1 12.2 %all-to-all-start = ((f32[128,1,128]{2,1,0:T(1,128)}), f32[128,1,128]{2,1,0:T(1,128)S(1)}, u32[]{:S(2)}, u32[]{:S(2)}) async-start(f32[128,1,128]{2,1,0:T(1,128)} %get-tuple-element.79), calls=%async_computation | async-start | bytes 131072 | tf_op jit(solution)/shard_map/all_to_all | solution.py:712
  36.3 7.2 %shard_map.163.half_ref = f32[18,240,128]{2,1,0:T(8,128)S(1)} custom-call(bf16[2,8,48,128]{3,2,1,0:T(8,128)(2,1)} %get-tuple-element.76.sides_ref, bf16[3,8,48,256]{3,2,1,0:T(8,128)(2,1)} %get-tuple-element.93.mid_far.mid_ref, bf16[3,2,48,256]{3,2,1,0:T(8,128)(2,1)} %get-tuple-element.77.ends_far.ends_ref, bf16[768,768]{1,0:T(8,128)(2,1)} %get-tuple-element.78.w1_far.w1_ref), custom_call_target="tpu_custom_call" | custom-call | tf_op jit(solution)/shard_map/pallas_call | solution.py:46
  43.5 2.4 %all-to-all-done.stats_ref = f32[128,1,128]{2,1,0:T(1,128)S(1)} async-done(((f32[128,1,128]{2,1,0:T(1,128)}), f32[128,1,128]{2,1,0:T(1,128)S(1)}, u32[]{:S(2)}, u32[]{:S(2)}) %all-to-all-start) | async-done | bytes 65568 | tf_op jit(solution)/shard_map/all_to_all | solution.py:712
  45.9 2.6 %shard_map.164 = (bf16[10,24,1280]{2,1,0:T(8,128)(2,1)}, f32[128,1,128]{2,1,0:T(1,128)}) custom-call(f32[18,240,128]{2,1,0:T(8,128)S(1)} %shard_map.163.half_ref, f32[128,1,128]{2,1,0:T(1,128)S(1)} %all-to-all-done.stats_ref, f32[8,128]{1,0:T(8,128)S(1)} %get-tuple-element.82.params_ref, bf16[2304,256]{1,0:T(8,128)(2,1)S(1)} %get-tuple-element.83.w2_ref), custom_call_target="tpu_custom_call" | custom-call | tf_op jit(solution)/shard_map/pallas_call | solution.py:46
  48.4 7.4 %all-to-all-start.1 = ((f32[128,1,128]{2,1,0:T(1,128)}), f32[128,1,128]{2,1,0:T(1,128)S(1)}, u32[]{:S(2)}, u32[]{:S(2)}) async-start(f32[128,1,128]{2,1,0:T(1,128)} %get-tuple-element.88), calls=%async_computation.1 | async-start | bytes 131072 | tf_op jit(solution)/shard_map/all_to_all | solution.py:718
  55.8 5.2 %shard_map.165 = (f32[18,48,128]{2,1,0:T(8,128)S(1)}, f32[576,256]{1,0:T(8,128)}, bf16[2304,256]{1,0:T(8,128)(2,1)S(1)}) custom-call(bf16[10,24,1280]{2,1,0:T(8,128)(2,1)} %get-tuple-element.84.p1_ref, bf16[2304,256]{1,0:T(8,128)(2,1)S(1)} %get-tuple-element.83.w2_ref, bf16[864,64]{1,0:T(8,128)(2,1)} %bitcast.6), custom_call_target="tpu_custom_call" | custom-call | tf_op jit(solution)/shard_map/pallas_call | solution.py:46
  61.0 4.4 %all-to-all-done.1.stats_ref = f32[128,1,128]{2,1,0:T(1,128)S(1)} async-done(((f32[128,1,128]{2,1,0:T(1,128)}), f32[128,1,128]{2,1,0:T(1,128)S(1)}, u32[]{:S(2)}, u32[]{:S(2)}) %all-to-all-start.1) | async-done | bytes 65568 | tf_op jit(solution)/shard_map/all_to_all | solution.py:718
  65.4 2.2 %shard_map.166 = (f32[128,256]{1,0:T(8,128)S(1)}, bf16[64,4,1152]{2,1,0:T(4,128)(2,1)}) custom-call(f32[18,48,128]{2,1,0:T(8,128)S(1)} %get-tuple-element.89.half_ref, f32[128,1,128]{2,1,0:T(1,128)S(1)} %all-to-all-done.1.stats_ref, f32[8,128]{1,0:T(8,128)S(1)} %get-tuple-element.82.params_ref, bf16[2304,256]{1,0:T(8,128)(2,1)S(1)} %get-tuple-element.91.w3_ref), custom_call_target="tpu_custom_call" | custom-call | tf_op jit(solution)/shard_map/pallas_call | solution.py:46
  67.5 6.2 %all-to-all-start.2 = ((bf16[64,4,1152]{2,1,0:T(4,128)(2,1)}), bf16[64,4,1152]{2,1,0:T(4,128)(2,1)S(1)}, u32[]{:S(2)}, u32[]{:S(2)}) async-start(bf16[64,4,1152]{2,1,0:T(4,128)(2,1)} %get-tuple-element.96), calls=%async_computation.2 | async-start | bytes 1179648 | tf_op jit(solution)/shard_map/all_to_all | solution.py:724
  73.7 3.6 %shard_map.167 = bf16[8,32,2048]{2,1,0:T(8,128)(2,1)} custom-call(bf16[3,8,48,256]{3,2,1,0:T(8,128)(2,1)} %get-tuple-element.93.mid_far.mid_ref, bf16[3,2,48,256]{3,2,1,0:T(8,128)(2,1)} %get-tuple-element.77.ends_far.ends_ref, bf16[768,768]{1,0:T(8,128)(2,1)} %get-tuple-element.78.w1_far.w1_ref, f32[128,1,128]{2,1,0:T(1,128)S(1)} %all-to-all-done.stats_ref, ...), custom_call_target="tpu_custom_call" | custom-call | tf_op jit(solution)/shard_map/pallas_call | solution.py:46
  77.4 2.1 %shard_map.168 = bf16[4,16,2048]{2,1,0:T(8,128)(2,1)} custom-call(f32[576,256]{1,0:T(8,128)} %get-tuple-element.94.r2_ref, f32[128,1,128]{2,1,0:T(1,128)S(1)} %all-to-all-done.1.stats_ref, f32[8,128]{1,0:T(8,128)S(1)} %get-tuple-element.82.params_ref), custom_call_target="tpu_custom_call" | custom-call | tf_op jit(solution)/shard_map/pallas_call | solution.py:46
  79.5 1.6 %shard_map.169.w4_ref = bf16[2304,256]{1,0:T(8,128)(2,1)S(1)} custom-call(bf16[1728,128]{1,0:T(8,128)(2,1)} %bitcast.5), custom_call_target="tpu_custom_call" | custom-call | tf_op jit(solution)/shard_map/pallas_call | solution.py:46
  81.1 5.4 %all-to-all-done.2.own_ref = bf16[64,4,1152]{2,1,0:T(4,128)(2,1)S(1)} async-done(((bf16[64,4,1152]{2,1,0:T(4,128)(2,1)}), bf16[64,4,1152]{2,1,0:T(4,128)(2,1)S(1)}, u32[]{:S(2)}, u32[]{:S(2)}) %all-to-all-start.2) | async-done | bytes 589856 | tf_op jit(solution)/shard_map/all_to_all | solution.py:724
  86.6 1.9 %collective-permute-start.6 = (bf16[64,4,1152]{2,1,0:T(4,128)(2,1)S(1)}, bf16[64,4,1152]{2,1,0:T(4,128)(2,1)S(1)}, u32[]{:S(2)}, u32[]{:S(2)}) collective-permute-start(bf16[64,4,1152]{2,1,0:T(4,128)(2,1)S(1)} %all-to-all-done.2.own_ref), channel_id=1, source_target_pairs={{0,4},{4,0},{1,5},{5,1},{2,6},{6,2},{3,7},{7,3},{8,12},{12,8},{9,1... | collective-permute-start | bytes 1769480 | tf_op jit(solution)/shard_map/ppermute | solution.py:729
  88.5 1.6 %collective-permute-done.6.other_ref = bf16[64,4,1152]{2,1,0:T(4,128)(2,1)S(1)} collective-permute-done((bf16[64,4,1152]{2,1,0:T(4,128)(2,1)S(1)}, bf16[64,4,1152]{2,1,0:T(4,128)(2,1)S(1)}, u32[]{:S(2)}, u32[]{:S(2)}) %collective-permute-start.6) | collective-permute-done | bytes 589856 | tf_op jit(solution)/shard_map/ppermute | solution.py:729
  90.1 8.0 %shard_map.170 = (bf16[2,8,2048]{2,1,0:T(8,128)(2,1)}, bf16[8,16,8192]{2,1,0:T(8,128)(2,1)}) custom-call(f32[128,256]{1,0:T(8,128)S(1)} %get-tuple-element.99.r3_ref, bf16[64,4,1152]{2,1,0:T(4,128)(2,1)S(1)} %all-to-all-done.2.own_ref, bf16[64,4,1152]{2,1,0:T(4,128)(2,1)S(1)} %collective-permute-done.6.other_ref, f32[8,128]{1,0:T(8,128)S(1)} %get-tuple-element.82.params_ref, ...), custom_call_target="tpu_custom_call" | custom-call | tf_op jit(solution)/shard_map/pallas_call | solution.py:46
  (2 shorter events, 0.1 us)
Async XLA Ops:
  0.6 8.0 %collective-permute-start.1 = (bf16[8,32,128]{2,1,0:T(8,128)(2,1)}, bf16[8,32,128]{2,1,0:T(8,128)(2,1)S(1)}, u32[]{:S(2)}, u32[]{:S(2)}) collective-permute-start(bf16[8,32,128]{2,1,0:T(8,128)(2,1)} %volume_far.1), channel_id=1, source_target_pairs={{1,2},{2,1},{5,6},{6,5},{9,10},{10,9},{13,14},{14,13},{17,18},{18,... | collective-permute-start | bytes 196616 | tf_op jit(solution)/shard_map/ppermute | solution.py:687
  1.3 7.4 %collective-permute-start = (bf16[8,32,128]{2,1,0:T(8,128)(2,1)}, bf16[8,32,128]{2,1,0:T(8,128)(2,1)S(1)}, u32[]{:S(2)}, u32[]{:S(2)}) collective-permute-start(bf16[8,32,128]{2,1,0:T(8,128)(2,1)} %volume_far.1), channel_id=1, source_target_pairs={{0,1},{2,3},{1,0},{3,2},{4,5},{6,7},{5,4},{7,6},{8,9},{10,11},{9,8... | collective-permute-start | bytes 196616 | tf_op jit(solution)/shard_map/ppermute | solution.py:687
  8.8 5.9 %collective-permute-start.2 = (bf16[8,8,256]{2,1,0:T(8,128)(2,1)S(1)}, bf16[8,8,256]{2,1,0:T(8,128)(2,1)S(1)}, u32[]{:S(2)}, u32[]{:S(2)}) collective-permute-start(bf16[8,8,256]{2,1,0:T(8,128)(2,1)S(1)} %shard_map.158), channel_id=1, source_target_pairs={{0,4},{4,0},{1,5},{5,1},{2,6},{6,2},{3,7},{7,3},{8,12},{12,8},{9,1... | collective-permute-start | bytes 98312 | tf_op jit(solution)/shard_map/ppermute | solution.py:687
  10.1 7.0 %collective-permute-start.3 = (bf16[8,8,256]{2,1,0:T(8,128)(2,1)S(1)}, bf16[8,8,256]{2,1,0:T(8,128)(2,1)S(1)}, u32[]{:S(2)}, u32[]{:S(2)}) collective-permute-start(bf16[8,8,256]{2,1,0:T(8,128)(2,1)S(1)} %get-tuple-element.61), channel_id=1, source_target_pairs={{4,8},{8,4},{5,9},{9,5},{6,10},{10,6},{7,11},{11,7},{20,24},{24,20... | collective-permute-start | bytes 98312 | tf_op jit(solution)/shard_map/ppermute | solution.py:687
  17.2 5.3 %collective-permute-start.4 = (bf16[8,48,128]{2,1,0:T(8,128)(2,1)S(1)}, bf16[8,48,128]{2,1,0:T(8,128)(2,1)S(1)}, u32[]{:S(2)}, u32[]{:S(2)}) collective-permute-start(bf16[8,48,128]{2,1,0:T(8,128)(2,1)S(1)} %get-tuple-element.67), channel_id=1, source_target_pairs={{0,16},{32,48},{64,80},{96,112},{16,0},{48,32},{80,64},{112,96},{1... | collective-permute-start | bytes 294920 | tf_op jit(solution)/shard_map/ppermute | solution.py:687
  18.2 4.3 %collective-permute-start.5 = (bf16[8,48,128]{2,1,0:T(8,128)(2,1)S(1)}, bf16[8,48,128]{2,1,0:T(8,128)(2,1)S(1)}, u32[]{:S(2)}, u32[]{:S(2)}) collective-permute-start(bf16[8,48,128]{2,1,0:T(8,128)(2,1)S(1)} %get-tuple-element.68), channel_id=1, source_target_pairs={{16,32},{48,64},{80,96},{32,16},{64,48},{96,80},{17,33},{49,65},{8... | collective-permute-start | bytes 294920 | tf_op jit(solution)/shard_map/ppermute | solution.py:687
  24.1 21.8 %all-to-all-start = ((f32[128,1,128]{2,1,0:T(1,128)}), f32[128,1,128]{2,1,0:T(1,128)S(1)}, u32[]{:S(2)}, u32[]{:S(2)}) async-start(f32[128,1,128]{2,1,0:T(1,128)} %get-tuple-element.79), calls=%async_computation | async-start | bytes 131072 | tf_op jit(solution)/shard_map/all_to_all | solution.py:712
  48.4 16.9 %all-to-all-start.1 = ((f32[128,1,128]{2,1,0:T(1,128)}), f32[128,1,128]{2,1,0:T(1,128)S(1)}, u32[]{:S(2)}, u32[]{:S(2)}) async-start(f32[128,1,128]{2,1,0:T(1,128)} %get-tuple-element.88), calls=%async_computation.1 | async-start | bytes 131072 | tf_op jit(solution)/shard_map/all_to_all | solution.py:718
  67.5 19.0 %all-to-all-start.2 = ((bf16[64,4,1152]{2,1,0:T(4,128)(2,1)}), bf16[64,4,1152]{2,1,0:T(4,128)(2,1)S(1)}, u32[]{:S(2)}, u32[]{:S(2)}) async-start(bf16[64,4,1152]{2,1,0:T(4,128)(2,1)} %get-tuple-element.96), calls=%async_computation.2 | async-start | bytes 1179648 | tf_op jit(solution)/shard_map/all_to_all | solution.py:724
  86.6 3.5 %collective-permute-start.6 = (bf16[64,4,1152]{2,1,0:T(4,128)(2,1)S(1)}, bf16[64,4,1152]{2,1,0:T(4,128)(2,1)S(1)}, u32[]{:S(2)}, u32[]{:S(2)}) collective-permute-start(bf16[64,4,1152]{2,1,0:T(4,128)(2,1)S(1)} %all-to-all-done.2.own_ref), channel_id=1, source_target_pairs={{0,4},{4,0},{1,5},{5,1},{2,6},{6,2},{3,7},{7,3},{8,12},{12,8},{9,1... | collective-permute-start | bytes 1769480 | tf_op jit(solution)/shard_map/ppermute | solution.py:729
